TPU v7x, 128 devices: a whole 4x4x4 slice. The times are simulated.
128 devices in a mesh: row: 8 (over z, core), col: 16 (over y, x).
Axes of the slice: x: 4, y: 4, z: 4, core: 2. Of those that a mesh axis runs over, the one named last changes fastest.
Arguments:
- tokens: bfloat16 [128, 8192], P('row', 'col'), may hold values from -6 to 6
- gate_weight: bfloat16 [8192, 26624], P('col', 'row'), may hold values from -0.0625 to 0.0625
- up_weight: bfloat16 [8192, 26624], P('col', 'row'), may hold values from -0.0625 to 0.0625
- down_weight: bfloat16 [26624, 8192], P('row', 'col'), may hold values from -0.0390625 to 0.0390625
- gate_tangent: bfloat16 [8192, 26624], P('col', 'row'), may hold values from -0.0625 to 0.0625
- up_tangent: bfloat16 [8192, 26624], P('col', 'row'), may hold values from -0.0625 to 0.0625
Outputs:
- gate_product: bfloat16 [8192, 26624], P('col', 'row')
- up_product: bfloat16 [8192, 26624], P('col', 'row')
All inputs are finite; a program needn't handle non-finite values.
Results may differ from a plain program's by a relative error of at most 0.0085.
Values may be sent and summed in bfloat16 or wider, within the bound.
No kernel may reach another device: no remote copies, remote signals or barrier semaphores. Data moves between devices by JAX's collectives and lax.ppermute only.
A program may use at most 128 MiB of HBM per device.

v0:
```python
import jax
import jax.numpy as jnp
from jax import lax
from jax.sharding import PartitionSpec as P


def matmul(left, right):
    return jnp.dot(left, right, preferred_element_type=jnp.float32)


def transposed(left, right):
    return lax.dot_general(
        left, right, (((0,), (0,)), ((), ())), preferred_element_type=jnp.float32
    )


def against_rows(left, right):
    return lax.dot_general(
        left, right, (((1,), (1,)), ((), ())), preferred_element_type=jnp.float32
    )


def silu_terms(gate_sum):
    sigmoid_val = jax.nn.sigmoid(gate_sum)
    return (gate_sum * sigmoid_val, sigmoid_val * (1.0 + gate_sum * (1.0 - sigmoid_val)))


def tangent_hidden(activated, slopes, up_sum, gate_dir, up_dir):
    return (slopes * gate_dir * up_sum + activated * up_dir).astype(jnp.bfloat16)


def cotangents(back_sum, up_sum, activated, slopes):
    gate_cot = (back_sum * up_sum * slopes).astype(jnp.bfloat16)
    up_cot = (back_sum * activated).astype(jnp.bfloat16)
    return (gate_cot, up_cot)


def body(tokens, gate_weight, up_weight, down_weight, gate_tangent, up_tangent):
    gathered = lax.all_gather(tokens, "row", axis=0, tiled=True)
    total_rows = gathered.shape[0]
    out_scale = float(total_rows) ** (-0.5)
    gate_sum, up_sum, gate_dir, up_dir = lax.psum(
        (
            matmul(gathered, gate_weight),
            matmul(gathered, up_weight),
            matmul(gathered, gate_tangent),
            matmul(gathered, up_tangent),
        ),
        "col",
    )
    activated, slopes = silu_terms(gate_sum)
    hidden_dir = tangent_hidden(activated, slopes, up_sum, gate_dir, up_dir)
    output_part = matmul(hidden_dir, down_weight)
    output_dir = (lax.psum(output_part, "row") * out_scale).astype(jnp.bfloat16)
    back_sum = lax.psum(against_rows(output_dir, down_weight), "col")
    gate_cot, up_cot = cotangents(back_sum, up_sum, activated, slopes)
    gate_grad = transposed(gathered, gate_cot)
    up_grad = transposed(gathered, up_cot)
    return (gate_grad.astype(jnp.bfloat16), up_grad.astype(jnp.bfloat16))


def solution(mesh):
    placed = (
        P("row", "col"),
        P("col", "row"),
        P("col", "row"),
        P("row", "col"),
        P("col", "row"),
        P("col", "row"),
    )
    return jax.shard_map(
        body,
        mesh=mesh,
        in_specs=placed,
        out_specs=(P("col", "row"), P("col", "row")),
        check_vma=False,
    )
```

profile of v0, /device:TPU:0, one launch (start us, length us, event | category | flops | bytes accessed | tf_op | source)
XLA Modules:
  0.0 345.7 jit_solution(4777390323199901349)
XLA Ops:
  7.2 0.0 copy-start
  7.2 0.0 all-reduce.9.cloned.1.call-start
  7.2 14.4 %all_gather.3 = bf16[128,512]{1,0:T(8,128)(2,1)S(1)} all-gather(bf16[16,512]{1,0:T(8,128)(2,1)} %param.6), channel_id=1, replica_groups=mesh['row'=8,'col'=16] {'row'}, dimensions={0}, use_global_device_ids=true | all-gather | bytes 147456 | tf_op jit(solution)/shard_map/all_gather | solution.py:39
  21.6 0.0 copy-start.1
  21.6 3.9 %fusion.14 = f32[128,3328]{1,0:T(8,128)} fusion(bf16[128,512]{1,0:T(8,128)(2,1)S(1)} %all_gather.3, bf16[512,3328]{1,0:T(8,128)(2,1)} %param.11), kind=kOutput, calls=%fused_computation.20 | convolution fusion | flops 436207616 | bytes 5242880 | tf_op jit(solution)/shard_map/dot_general | solution.py:8
  25.5 0.0 copy-done.1
  25.5 0.0 copy-start.2
  25.5 1.8 fusion.13
  27.3 0.8 copy-done.2
  28.1 0.0 copy-start.3
  28.1 1.9 fusion.12
  30.0 0.7 copy-done.3
  30.7 1.9 fusion.11
  32.6 0.0 all-reduce.9.cloned.1.call-update
  32.6 0.0 all-reduce.5.cloned.1.call-start
  32.6 128.7 %all-reduce.9.cloned.1.call-done = (f32[128,3328]{1,0:T(8,128)}, f32[128,3328]{1,0:T(8,128)}, f32[128,3328]{1,0:T(8,128)}, f32[128,3328]{1,0:T(8,128)}) async-done(((f32[128,3328]{1,0:T(8,128)}, f32[128,3328]{1,0:T(8,128)}, f32[128,3328]{1,0:T(8,128)}, f32[128,3328]{1,0:T(8,128)}), (f32[128,3328]{1,0:T(8,128)}, f32[128,3328]{1,0:T(8,128)}, f32[128,3328]{1,0:T(8,128)}, ...) | async-done | bytes 6815760 | tf_op jit(solution)/shard_map/psum | solution.py:42
  161.3 0.0 copy-done
  161.3 4.9 %fusion.3 = f32[128,512]{1,0:T(8,128)} fusion(bf16[3328,512]{1,0:T(8,128)(2,1)S(1)} %copy-done, f32[128,3328]{1,0:T(8,128)} %get-tuple-element.4, f32[128,3328]{1,0:T(8,128)} %get-tuple-element.5, f32[128,3328]{1,0:T(8,128)} %get-tuple-element.6, f32[128,3328]{1,0:T(8,128)} %get-tuple-element.7), kind=kOutput, calls=%fused_computation.10 | convolution fusion | flops 441745408 | bytes 10485760 | tf_op jit(solution)/shard_map/dot_general | solution.py:8
  166.2 0.0 all-reduce.5.cloned.1.call-update
  166.3 0.0 all-reduce.7.cloned.1.call-start
  166.3 59.9 %all-reduce.5.cloned.1.call-done = f32[128,512]{1,0:T(8,128)} async-done(((f32[128,512]{1,0:T(8,128)}), f32[128,512]{1,0:T(8,128)}) %all-reduce.5.cloned.1.call-update) | async-done | bytes 262160 | tf_op jit(solution)/shard_map/psum | solution.py:54
  226.2 3.4 fusion.6
  229.6 0.0 all-reduce.7.cloned.1.call-update
  229.6 88.3 %all-reduce.7.cloned.1.call-done = f32[128,3328]{1,0:T(8,128)} async-done(((f32[128,3328]{1,0:T(8,128)}), f32[128,3328]{1,0:T(8,128)}) %all-reduce.7.cloned.1.call-update) | async-done | bytes 1703952 | tf_op jit(solution)/shard_map/psum | solution.py:55
  317.9 4.8 %fusion.1 = bf16[512,3328]{0,1:T(8,128)(2,1)} fusion(bf16[128,512]{1,0:T(8,128)(2,1)S(1)} %all_gather.3, f32[128,3328]{1,0:T(8,128)} %all-reduce.7.cloned.1.call-done, f32[128,3328]{1,0:T(8,128)} %get-tuple-element.7), kind=kOutput, calls=%fused_computation.3 | convolution fusion | flops 440467456 | bytes 6946816 | tf_op jit(solution)/shard_map/dot_general | solution.py:12
  322.7 5.5 %copy.9 = bf16[512,3328]{1,0:T(8,128)(2,1)} copy(bf16[512,3328]{0,1:T(8,128)(2,1)} %fusion.1) | data formatting | bytes 6815744
  328.3 5.3 %fusion = bf16[512,3328]{0,1:T(8,128)(2,1)} fusion(bf16[128,512]{1,0:T(8,128)(2,1)S(1)} %all_gather.3, f32[128,3328]{1,0:T(8,128)} %all-reduce.7.cloned.1.call-done, f32[128,3328]{1,0:T(8,128)} %get-tuple-element.5, f32[128,3328]{1,0:T(8,128)} %get-tuple-element.7), kind=kOutput, calls=%fused_computation.2 | convolution fusion | flops 442171392 | bytes 8650752 | tf_op jit(solution)/shard_map/dot_general | solution.py:12
  333.6 5.5 %copy.8 = bf16[512,3328]{1,0:T(8,128)(2,1)} copy(bf16[512,3328]{0,1:T(8,128)(2,1)} %fusion) | data formatting | bytes 6815744
Async XLA Ops:
  7.2 154.2 %copy-start = (bf16[3328,512]{1,0:T(8,128)(2,1)S(1)}, bf16[3328,512]{1,0:T(8,128)(2,1)}, u32[]{:S(2)}) copy-start(bf16[3328,512]{1,0:T(8,128)(2,1)} %param.9) | copy-start | bytes 10223620
  7.2 154.2 %all-reduce.9.cloned.1.call-start = ((), (), s32[]{:S(2)}) async-start(), calls=%async_computation.2 | async-start | bytes 13631488 | tf_op jit(solution)/shard_map/psum | solution.py:42
  21.6 3.9 %copy-start.1 = (bf16[512,3328]{1,0:T(8,128)(2,1)S(1)}, bf16[512,3328]{1,0:T(8,128)(2,1)}, u32[]{:S(2)}) copy-start(bf16[512,3328]{1,0:T(8,128)(2,1)} %param.8) | copy-start | bytes 10223620
  25.5 2.6 copy-start.2
  28.1 2.6 copy-start.3
  32.6 193.6 %all-reduce.5.cloned.1.call-start = ((), (), s32[]{:S(2)}) async-start(), calls=%async_computation | async-start | bytes 524288 | tf_op jit(solution)/shard_map/psum | solution.py:54
  166.3 151.6 %all-reduce.7.cloned.1.call-start = ((), (), s32[]{:S(2)}) async-start(), calls=%async_computation.1 | async-start | bytes 3407872 | tf_op jit(solution)/shard_map/psum | solution.py:55
Sparse Core Ops, SparseCore 0:
  32.7 128.5 all-reduce.8
  166.4 59.7 all-reduce.4
  230.5 87.3 all-reduce.6
where the time goes:
time: 346 us
  waiting for transfers between devices  277 us (80%)
  matrix products  27.9 us (8%)
  blocking collectives  14.4 us (4%)
  between operations  13.8 us (4%)
  local copies, waits for them, and re-layouts  12.6 us (4%)
    psum x1, waiting for transfers between devices, body(): lax.psum((matmul(gathered, gate_weight), matmul(gathered, up_weight), mat...  129 us
    psum x1, waiting for transfers between devices, body(): back_sum = lax.psum(against_rows(output_dir, down_weight), 'col')  88.3 us
    psum x1, waiting for transfers between devices, body(): output_dir = (lax.psum(output_part, 'row') * out_scale).astype(jnp.bfloat16)  59.9 us
    all_gather x1, blocking collectives, body(): gathered = lax.all_gather(tokens, 'row', axis=0, tiled=True)  14.4 us
    dot_general x5, matrix products, matmul(): return jnp.dot(left, right, preferred_element_type=jnp.float32)  14.4 us
    unnamed x10, local copies, waits for them, and re-layouts  12.6 us
    dot_general x2, matrix products, transposed(): lax.dot_general(left, right, (((0,), (0,)), ((), ())), preferred_element_...  10.1 us
  transfers between devices with their start and end apart: 3, of which 3 were waited for; matrix products, arithmetic and copies ran while one was open for 0% of the time, Pallas kernels for 0%

commit v1 on v0

v1 whole, which is shorter than its diff:
```python
import jax
import jax.numpy as jnp
from jax import lax
from jax.sharding import PartitionSpec as P

BF = jnp.bfloat16
F32 = jnp.float32
RC = ("row", "col")


def device(z, k, y, x):
    return ((z % 4) * 2 + k) * 16 + (y % 4) * 4 + (x % 4)


def pairs(move):
    return [
        (device(z, k, y, x), device(*move(z, k, y, x)))
        for z in range(4)
        for k in range(2)
        for y in range(4)
        for x in range(4)
    ]


def near(i):
    return i ^ 1


def far(i):
    return i + 1 if i % 2 else i - 1


def along_first(move):
    return pairs(lambda z, k, y, x: (z, k, y, move(x)) if k == 0 else (z, k, move(y), x))


def along_second(move):
    return pairs(lambda z, k, y, x: (z, k, move(y), x) if k == 0 else (z, k, y, move(x)))


CORE = pairs(lambda z, k, y, x: (z, 1 - k, y, x))


def z_shift(d):
    return pairs(lambda z, k, y, x: (z + d, k, y, x))


def first_shift(d):
    return along_first(lambda i: i + d)


def second_shift(d):
    return along_second(lambda i: i + d)


def send(value, to):
    return lax.ppermute(value, RC, to)


def matmul(left, right):
    return jnp.dot(left, right, preferred_element_type=F32)


def against_rows(left, right):
    return lax.dot_general(left, right, (((1,), (1,)), ((), ())), preferred_element_type=F32)


def transposed(left, right):
    return lax.dot_general(left, right, (((0,), (0,)), ((), ())), preferred_element_type=F32)


def gather_tokens(tokens, z, k):
    chip = jnp.concatenate([tokens, send(tokens, CORE)])
    return jnp.concatenate([chip] + [send(chip, z_shift(d)) for d in (1, 2, 3)])


def row_order(first, second, z, k, x, y):
    first = jnp.repeat(first, 32)
    second = jnp.tile(jnp.repeat(second, 8), 4)
    high = (x + jnp.where(k == 0, first, second)) % 4
    low = (y + jnp.where(k == 0, second, first)) % 4
    token = (high * 4 + low) * 8 + jnp.tile(jnp.arange(8), 16)
    return ((z - token // 32) % 4) * 32 + ((token // 16 % 2) ^ k) * 16 + token % 16


def halve(left, right, tokens, to_half, to_quarter):
    full = jnp.stack([matmul(tokens, left), matmul(tokens, right)])
    got = send(full[:, 64:].astype(BF), to_half)
    half = full[:, :64] + got
    got = send(half[:, 32:].astype(BF), to_quarter)
    return half[:, :32] + got


def scatter_second(quarter):
    got = [send(quarter[:, 8 * e : 8 * e + 8].astype(BF), second_shift(e)) for e in (1, 2, 3)]
    return quarter[:, :8] + got[0] + got[1] + got[2]


def scatter_first(full):
    got = [send(full[:, 32 * d : 32 * d + 32].astype(BF), first_shift(d)) for d in (1, 2, 3)]
    return full[:, :32] + got[0] + got[1] + got[2]


def gather_second(own):
    return jnp.concatenate([own] + [send(own, second_shift(-e)) for e in (1, 2, 3)], axis=1)


def gather_first(own):
    return jnp.concatenate([own] + [send(own, first_shift(-d)) for d in (1, 2, 3)], axis=1)


def swap_axes(value):
    return value.reshape(4, 4, 8, -1).swapaxes(0, 1).reshape(value.shape)


def sum_rows(part, k):
    part = jnp.where(k == 0, part, swap_axes(part))
    mine = jnp.where(k == 0, part[:64], part[64:])
    other = jnp.where(k == 0, part[64:], part[:64])
    mine = mine + send(other, CORE)
    rounded = mine.astype(BF)
    got = [send(rounded, z_shift(d)) for d in (1, 2, 3)]
    return mine + got[0] + got[1] + got[2]


def join_halves(half, k):
    other = send(half, CORE)
    full = jnp.where(k == 0, jnp.concatenate([half, other]), jnp.concatenate([other, half]))
    return jnp.where(k == 0, full, swap_axes(full))


def body(tokens, gate_weight, up_weight, down_weight, gate_tangent, up_tangent):
    row, col = lax.axis_index("row"), lax.axis_index("col")
    z, k, y, x = row // 2, row % 2, col // 4, col % 4
    out_scale = 128.0 ** (-0.5)
    gathered = gather_tokens(tokens, z, k)
    step = 1 - 2 * (jnp.where(k == 0, x, y) % 2)
    straight = jnp.arange(4)
    orders = jnp.concatenate(
        [
            row_order(jnp.stack([0 * step, -step, step, 2 + 0 * step]), straight, z, k, x, y),
            row_order(jnp.stack([0 * step, step, -step, 2 + 0 * step]), straight, z, k, x, y),
            row_order(straight, straight, z, k, x, y),
        ]
    )
    picked = (orders[:, None] == jnp.arange(128)[None, :]).astype(BF)
    placed = matmul(picked, gathered).astype(BF)
    tokens_a, tokens_b, local = placed[:128], placed[128:256], placed[256:]

    sums = halve(gate_weight, up_weight, tokens_a, along_first(near), along_first(far))
    dirs = halve(gate_tangent, up_tangent, tokens_b, along_first(far), along_first(near))
    gate_sum, up_sum, gate_dir, up_dir = scatter_second(jnp.concatenate([sums, dirs]))
    sigmoid = jax.nn.sigmoid(gate_sum)
    activated = gate_sum * sigmoid
    up_slopes = up_sum * (sigmoid * (1.0 + gate_sum * (1.0 - sigmoid)))
    hidden = (up_slopes * gate_dir + activated * up_dir).astype(BF)

    hidden = gather_first(gather_second(hidden[None]))[0]
    half = sum_rows(matmul(hidden, down_weight), k)
    output_dir = join_halves((half * out_scale).astype(BF), k)
    back = scatter_second(scatter_first(against_rows(output_dir, down_weight)[None]))[0]
    cots = jnp.stack([back * up_slopes, back * activated]).astype(BF)
    gate_cot, up_cot = gather_first(gather_second(cots))
    return transposed(local, gate_cot).astype(BF), transposed(local, up_cot).astype(BF)


def solution(mesh):
    placed = (
        P("row", "col"),
        P("col", "row"),
        P("col", "row"),
        P("row", "col"),
        P("col", "row"),
        P("col", "row"),
    )
    return jax.shard_map(
        body,
        mesh=mesh,
        in_specs=placed,
        out_specs=(P("col", "row"), P("col", "row")),
        check_vma=False,
    )
```

time: 346 us -> 138 us (0.40)
  waiting for transfers between devices: 277 us -> 73.2 us
  starting transfers between devices: 0.12 us -> 47.2 us
  matrix products: 27.9 us -> 12.4 us
  blocking collectives: 14.4 us -> 0 us
  between operations: 13.8 us -> 1.14 us
  local copies, waits for them, and re-layouts: 12.6 us -> 2.07 us
    psum x3 -> x0, waiting for transfers between devices: 277 us -> none  [the longest x1 129 us: body(): lax.psum((matmul(gathered, gate_weight), matmul(gathered, up_weight), mat...]
    ppermute x0 -> x34, waiting for transfers between devices: none -> 73.2 us  [send(): return lax.ppermute(value, RC, to)]
    ppermute x0 -> x34, starting transfers between devices: none -> 47.2 us  [send(): return lax.ppermute(value, RC, to)]
    all_gather x1 -> x0, blocking collectives: 14.4 us -> none  [body(): gathered = lax.all_gather(tokens, 'row', axis=0, tiled=True)]
    unnamed x10 -> x21, local copies, waits for them, and re-layouts: 12.6 us -> 1.12 us
    dot_general x5 -> x6, matrix products: 14.4 us -> 5.51 us  [matmul(): return jnp.dot(left, right, preferred_element_type=F32)]
    dot_general x2, matrix products: 10.1 us -> 5.64 us  [transposed(): lax.dot_general(left, right, (((0,), (0,)), ((), ())), preferred_element_...]
  transfers between devices with their start and end apart: 3 -> 34, of which waited for: 3 -> 28; matrix products, arithmetic and copies ran while one was open for 0% -> 3% of each run, Pallas kernels for 0% -> 0%
where the time goes in v1:
time: 138 us; the launch traced here: 137 us
  waiting for transfers between devices  73.2 us (53%)
  starting transfers between devices  47.2 us (34%)
  matrix products  12.4 us (9%)
  local copies, waits for them, and re-layouts  2.07 us (1%)
  other arithmetic  1.54 us (1%)
    ppermute x34, waiting for transfers between devices, send(): return lax.ppermute(value, RC, to)  73.2 us
    ppermute x34, starting transfers between devices, send(): return lax.ppermute(value, RC, to)  47.2 us
    dot_general x2, matrix products, transposed(): lax.dot_general(left, right, (((0,), (0,)), ((), ())), preferred_element_...  5.64 us
    dot_general x6, matrix products, matmul(): return jnp.dot(left, right, preferred_element_type=F32)  5.51 us
  transfers between devices with their start and end apart: 34, of which 28 were waited for; matrix products, arithmetic and copies ran while one was open for 3% of the time, Pallas kernels for 0%

profile of v1, /device:TPU:0, one launch (start us, length us, event | category | flops | bytes accessed | tf_op | source)
XLA Modules:
  0.0 137.5 jit_solution(12167416428925969883)
XLA Ops:
  2.4 2.1 %collective-permute-start.1 = (bf16[32,512]{1,0:T(8,128)(2,1)S(1)}, bf16[32,512]{1,0:T(8,128)(2,1)S(1)}, u32[]{:S(2)}, u32[]{:S(2)}) collective-permute-start(bf16[32,512]{1,0:T(8,128)(2,1)S(1)} %get-tuple-element.21), channel_id=1, source_target_pairs={{0,32},{1,33},{2,34},{3,35},{4,36},{5,37},{6,38},{7,39},{8,40},{9,... | collective-permute-start | bytes 98312 | tf_op jit(solution)/shard_map/ppermute | solution.py:57
  4.5 2.2 %collective-permute-start.3 = (bf16[32,512]{1,0:T(8,128)(2,1)S(1)}, bf16[32,512]{1,0:T(8,128)(2,1)S(1)}, u32[]{:S(2)}, u32[]{:S(2)}) collective-permute-start(bf16[32,512]{1,0:T(8,128)(2,1)S(1)} %get-tuple-element.21), channel_id=1, source_target_pairs={{0,96},{1,97},{2,98},{3,99},{4,100},{5,101},{6,102},{7,103},{8,104... | collective-permute-start | bytes 98312 | tf_op jit(solution)/shard_map/ppermute | solution.py:57
  6.7 1.8 %collective-permute-start.2 = (bf16[32,512]{1,0:T(8,128)(2,1)S(1)}, bf16[32,512]{1,0:T(8,128)(2,1)S(1)}, u32[]{:S(2)}, u32[]{:S(2)}) collective-permute-start(bf16[32,512]{1,0:T(8,128)(2,1)S(1)} %get-tuple-element.21), channel_id=1, source_target_pairs={{0,64},{1,65},{2,66},{3,67},{4,68},{5,69},{6,70},{7,71},{8,72},{9,... | collective-permute-start | bytes 98312 | tf_op jit(solution)/shard_map/ppermute | solution.py:57
  8.6 3.5 %collective-permute-done.2 = bf16[32,512]{1,0:T(8,128)(2,1)S(1)} collective-permute-done((bf16[32,512]{1,0:T(8,128)(2,1)S(1)}, bf16[32,512]{1,0:T(8,128)(2,1)S(1)}, u32[]{:S(2)}, u32[]{:S(2)}) %collective-permute-start.2) | collective-permute-done | bytes 32800 | tf_op jit(solution)/shard_map/ppermute | solution.py:57
  12.5 2.7 %convolution_bitcast_fusion.1 = f32[1,128,3328]{2,1,0:T(8,128)S(1)} fusion(bf16[512,3328]{1,0:T(8,128)(2,1)} %param.11, bf16[384,512]{1,0:T(8,128)(2,1)S(1)} %convolution_convert_fusion.2), kind=kOutput, calls=%fused_computation.3 | convolution fusion | flops 436207616 | bytes 5242880 | tf_op jit(solution)/shard_map/dot_general | solution.py:61
  16.2 2.8 %collective-permute-start.6 = (bf16[2,64,3328]{2,1,0:T(8,128)(2,1)S(1)}, bf16[2,64,3328]{2,1,0:T(8,128)(2,1)S(1)}, u32[]{:S(2)}, u32[]{:S(2)}) collective-permute-start(bf16[2,64,3328]{2,1,0:T(8,128)(2,1)S(1)} %fusion.5), channel_id=1, source_target_pairs={{0,3},{1,2},{2,1},{3,0},{4,7},{5,6},{6,5},{7,4},{8,11},{9,10},{10,... | collective-permute-start | bytes 2555912 | tf_op jit(solution)/shard_map/ppermute | solution.py:57
  21.4 8.8 %collective-permute-done.6 = bf16[2,64,3328]{2,1,0:T(8,128)(2,1)S(1)} collective-permute-done((bf16[2,64,3328]{2,1,0:T(8,128)(2,1)S(1)}, bf16[2,64,3328]{2,1,0:T(8,128)(2,1)S(1)}, u32[]{:S(2)}, u32[]{:S(2)}) %collective-permute-start.6) | collective-permute-done | bytes 852000 | tf_op jit(solution)/shard_map/ppermute | solution.py:57
  30.8 2.4 %collective-permute-done.4 = bf16[2,64,3328]{2,1,0:T(8,128)(2,1)S(1)} collective-permute-done((bf16[2,64,3328]{2,1,0:T(8,128)(2,1)S(1)}, bf16[2,64,3328]{2,1,0:T(8,128)(2,1)S(1)}, u32[]{:S(2)}, u32[]{:S(2)}) %collective-permute-start.4) | collective-permute-done | bytes 852000 | tf_op jit(solution)/shard_map/ppermute | solution.py:57
  33.4 2.3 %collective-permute-start.5 = (bf16[2,32,3328]{2,1,0:T(8,128)(2,1)S(1)}, bf16[2,32,3328]{2,1,0:T(8,128)(2,1)S(1)}, u32[]{:S(2)}, u32[]{:S(2)}) collective-permute-start(bf16[2,32,3328]{2,1,0:T(8,128)(2,1)S(1)} %slice.204), channel_id=1, source_target_pairs={{0,3},{1,2},{2,1},{3,0},{4,7},{5,6},{6,5},{7,4},{8,11},{9,10},{10,... | collective-permute-start | bytes 1277960 | tf_op jit(solution)/shard_map/ppermute | solution.py:57
  35.7 2.9 %collective-permute-done.7 = bf16[2,32,3328]{2,1,0:T(8,128)(2,1)S(1)} collective-permute-done((bf16[2,32,3328]{2,1,0:T(8,128)(2,1)S(1)}, bf16[2,32,3328]{2,1,0:T(8,128)(2,1)S(1)}, u32[]{:S(2)}, u32[]{:S(2)}) %collective-permute-start.7) | collective-permute-done | bytes 426016 | tf_op jit(solution)/shard_map/ppermute | solution.py:57
  38.7 4.1 %collective-permute-done.5 = bf16[2,32,3328]{2,1,0:T(8,128)(2,1)S(1)} collective-permute-done((bf16[2,32,3328]{2,1,0:T(8,128)(2,1)S(1)}, bf16[2,32,3328]{2,1,0:T(8,128)(2,1)S(1)}, u32[]{:S(2)}, u32[]{:S(2)}) %collective-permute-start.5) | collective-permute-done | bytes 426016 | tf_op jit(solution)/shard_map/ppermute | solution.py:57
  43.1 1.9 %collective-permute-start.8 = (bf16[4,8,3328]{2,1,0:T(8,128)(2,1)S(1)}, bf16[4,8,3328]{2,1,0:T(8,128)(2,1)S(1)}, u32[]{:S(2)}, u32[]{:S(2)}) collective-permute-start(bf16[4,8,3328]{2,1,0:T(8,128)(2,1)S(1)} %get-tuple-element.13), channel_id=1, source_target_pairs={{0,4},{1,5},{2,6},{3,7},{4,8},{5,9},{6,10},{7,11},{8,12},{9,13},{1... | collective-permute-start | bytes 638984 | tf_op jit(solution)/shard_map/ppermute | solution.py:57
  46.4 2.3 %collective-permute-start.9 = (bf16[4,8,3328]{2,1,0:T(8,128)(2,1)S(1)}, bf16[4,8,3328]{2,1,0:T(8,128)(2,1)S(1)}, u32[]{:S(2)}, u32[]{:S(2)}) collective-permute-start(bf16[4,8,3328]{2,1,0:T(8,128)(2,1)S(1)} %get-tuple-element.15), channel_id=1, source_target_pairs={{0,8},{1,9},{2,10},{3,11},{4,12},{5,13},{6,14},{7,15},{8,0},{9,1},... | collective-permute-start | bytes 638984 | tf_op jit(solution)/shard_map/ppermute | solution.py:57
  50.8 2.9 %collective-permute-done.9 = bf16[4,8,3328]{2,1,0:T(8,128)(2,1)S(1)} collective-permute-done((bf16[4,8,3328]{2,1,0:T(8,128)(2,1)S(1)}, bf16[4,8,3328]{2,1,0:T(8,128)(2,1)S(1)}, u32[]{:S(2)}, u32[]{:S(2)}) %collective-permute-start.9) | collective-permute-done | bytes 213024 | tf_op jit(solution)/shard_map/ppermute | solution.py:57
  55.4 2.1 %collective-permute-start.12 = (bf16[1,8,3328]{2,1,0:T(8,128)(2,1)S(1)}, bf16[1,8,3328]{2,1,0:T(8,128)(2,1)S(1)}, u32[]{:S(2)}, u32[]{:S(2)}) collective-permute-start(bf16[1,8,3328]{2,1,0:T(8,128)(2,1)S(1)} %get-tuple-element.7), channel_id=1, source_target_pairs={{0,8},{1,9},{2,10},{3,11},{4,12},{5,13},{6,14},{7,15},{8,0},{9,1},... | collective-permute-start | bytes 159752 | tf_op jit(solution)/shard_map/ppermute | solution.py:57
  59.3 2.1 %collective-permute-done.12 = bf16[1,8,3328]{2,1,0:T(8,128)(2,1)S(1)} collective-permute-done((bf16[1,8,3328]{2,1,0:T(8,128)(2,1)S(1)}, bf16[1,8,3328]{2,1,0:T(8,128)(2,1)S(1)}, u32[]{:S(2)}, u32[]{:S(2)}) %collective-permute-start.12) | collective-permute-done | bytes 53280 | tf_op jit(solution)/shard_map/ppermute | solution.py:57
  62.8 3.3 %collective-permute-start.15 = (bf16[1,32,3328]{2,1,0:T(8,128)(2,1)S(1)}, bf16[1,32,3328]{2,1,0:T(8,128)(2,1)S(1)}, u32[]{:S(2)}, u32[]{:S(2)}) collective-permute-start(bf16[1,32,3328]{2,1,0:T(8,128)(2,1)S(1)} %pad_maximum_fusion.4), channel_id=1, source_target_pairs={{0,2},{1,3},{2,0},{3,1},{4,6},{5,7},{6,4},{7,5},{8,10},{9,11},{10,... | collective-permute-start | bytes 638984 | tf_op jit(solution)/shard_map/ppermute | solution.py:57
  66.2 6.9 %collective-permute-done.14 = bf16[1,32,3328]{2,1,0:T(8,128)(2,1)S(1)} collective-permute-done((bf16[1,32,3328]{2,1,0:T(8,128)(2,1)S(1)}, bf16[1,32,3328]{2,1,0:T(8,128)(2,1)S(1)}, u32[]{:S(2)}, u32[]{:S(2)}) %collective-permute-start.14) | collective-permute-done | bytes 213024 | tf_op jit(solution)/shard_map/ppermute | solution.py:57
  75.3 1.8 %collective-permute-start.20 = (bf16[64,512]{1,0:T(8,128)(2,1)S(1)}, bf16[64,512]{1,0:T(8,128)(2,1)S(1)}, u32[]{:S(2)}, u32[]{:S(2)}) collective-permute-start(bf16[64,512]{1,0:T(8,128)(2,1)S(1)} %get-tuple-element.4), channel_id=1, source_target_pairs={{0,96},{1,97},{2,98},{3,99},{4,100},{5,101},{6,102},{7,103},{8,104... | collective-permute-start | bytes 196616 | tf_op jit(solution)/shard_map/ppermute | solution.py:57
  78.3 1.9 %collective-permute-done.20 = bf16[64,512]{1,0:T(8,128)(2,1)S(1)} collective-permute-done((bf16[64,512]{1,0:T(8,128)(2,1)S(1)}, bf16[64,512]{1,0:T(8,128)(2,1)S(1)}, u32[]{:S(2)}, u32[]{:S(2)}) %collective-permute-start.20) | collective-permute-done | bytes 65568 | tf_op jit(solution)/shard_map/ppermute | solution.py:57
  80.2 3.0 %collective-permute-done.19 = bf16[64,512]{1,0:T(8,128)(2,1)S(1)} collective-permute-done((bf16[64,512]{1,0:T(8,128)(2,1)S(1)}, bf16[64,512]{1,0:T(8,128)(2,1)S(1)}, u32[]{:S(2)}, u32[]{:S(2)}) %collective-permute-start.19) | collective-permute-done | bytes 65568 | tf_op jit(solution)/shard_map/ppermute | solution.py:57
  87.1 2.8 %collective-permute-start.24 = (bf16[1,32,3328]{2,1,0:T(8,128)(2,1)S(1)}, bf16[1,32,3328]{2,1,0:T(8,128)(2,1)S(1)}, u32[]{:S(2)}, u32[]{:S(2)}) collective-permute-start(bf16[1,32,3328]{2,1,0:T(8,128)(2,1)S(1)} %get-tuple-element.11), channel_id=1, source_target_pairs={{0,3},{1,0},{2,1},{3,2},{4,7},{5,4},{6,5},{7,6},{8,11},{9,8},{10,9... | collective-permute-start | bytes 638984 | tf_op jit(solution)/shard_map/ppermute | solution.py:57
  90.7 3.0 %collective-permute-done.22 = bf16[1,32,3328]{2,1,0:T(8,128)(2,1)S(1)} collective-permute-done((bf16[1,32,3328]{2,1,0:T(8,128)(2,1)S(1)}, bf16[1,32,3328]{2,1,0:T(8,128)(2,1)S(1)}, u32[]{:S(2)}, u32[]{:S(2)}) %collective-permute-start.22) | collective-permute-done | bytes 213024 | tf_op jit(solution)/shard_map/ppermute | solution.py:57
  93.7 1.9 %collective-permute-done.24 = bf16[1,32,3328]{2,1,0:T(8,128)(2,1)S(1)} collective-permute-done((bf16[1,32,3328]{2,1,0:T(8,128)(2,1)S(1)}, bf16[1,32,3328]{2,1,0:T(8,128)(2,1)S(1)}, u32[]{:S(2)}, u32[]{:S(2)}) %collective-permute-start.24) | collective-permute-done | bytes 213024 | tf_op jit(solution)/shard_map/ppermute | solution.py:57
  97.3 2.3 %collective-permute-start.25 = (bf16[1,8,3328]{2,1,0:T(8,128)(2,1)S(1)}, bf16[1,8,3328]{2,1,0:T(8,128)(2,1)S(1)}, u32[]{:S(2)}, u32[]{:S(2)}) collective-permute-start(bf16[1,8,3328]{2,1,0:T(8,128)(2,1)S(1)} %get-tuple-element.16), channel_id=1, source_target_pairs={{0,4},{1,5},{2,6},{3,7},{4,8},{5,9},{6,10},{7,11},{8,12},{9,13},{1... | collective-permute-start | bytes 159752 | tf_op jit(solution)/shard_map/ppermute | solution.py:57
  103.7 3.2 %collective-permute-done.26 = bf16[1,8,3328]{2,1,0:T(8,128)(2,1)S(1)} collective-permute-done((bf16[1,8,3328]{2,1,0:T(8,128)(2,1)S(1)}, bf16[1,8,3328]{2,1,0:T(8,128)(2,1)S(1)}, u32[]{:S(2)}, u32[]{:S(2)}) %collective-permute-start.26) | collective-permute-done | bytes 53280 | tf_op jit(solution)/shard_map/ppermute | solution.py:57
  110.5 2.8 %collective-permute-done.29 = bf16[2,8,3328]{2,1,0:T(8,128)(2,1)S(1)} collective-permute-done((bf16[2,8,3328]{2,1,0:T(8,128)(2,1)S(1)}, bf16[2,8,3328]{2,1,0:T(8,128)(2,1)S(1)}, u32[]{:S(2)}, u32[]{:S(2)}) %collective-permute-start.29) | collective-permute-done | bytes 106528 | tf_op jit(solution)/shard_map/ppermute | solution.py:57
  113.7 3.1 %collective-permute-done.30 = bf16[2,8,3328]{2,1,0:T(8,128)(2,1)S(1)} collective-permute-done((bf16[2,8,3328]{2,1,0:T(8,128)(2,1)S(1)}, bf16[2,8,3328]{2,1,0:T(8,128)(2,1)S(1)}, u32[]{:S(2)}, u32[]{:S(2)}) %collective-permute-start.30) | collective-permute-done | bytes 106528 | tf_op jit(solution)/shard_map/ppermute | solution.py:57
  118.3 2.4 %collective-permute-start.32 = (bf16[2,32,3328]{2,1,0:T(8,128)(2,1)S(1)}, bf16[2,32,3328]{2,1,0:T(8,128)(2,1)S(1)}, u32[]{:S(2)}, u32[]{:S(2)}) collective-permute-start(bf16[2,32,3328]{2,1,0:T(8,128)(2,1)S(1)} %pad_maximum_fusion.3), channel_id=1, source_target_pairs={{0,2},{1,3},{2,0},{3,1},{4,6},{5,7},{6,4},{7,5},{8,10},{9,11},{10,... | collective-permute-start | bytes 1277960 | tf_op jit(solution)/shard_map/ppermute | solution.py:57
  121.1 10.6 %collective-permute-done.31 = bf16[2,32,3328]{2,1,0:T(8,128)(2,1)S(1)} collective-permute-done((bf16[2,32,3328]{2,1,0:T(8,128)(2,1)S(1)}, bf16[2,32,3328]{2,1,0:T(8,128)(2,1)S(1)}, u32[]{:S(2)}, u32[]{:S(2)}) %collective-permute-start.31) | collective-permute-done | bytes 426016 | tf_op jit(solution)/shard_map/ppermute | solution.py:57
  131.8 2.8 %convolution_convert_fusion = bf16[512,3328]{1,0:T(8,128)(2,1)} fusion(bf16[2,128,3328]{2,1,0:T(8,128)(2,1)S(1)} %constant_dynamic-update-slice_fusion.14, bf16[384,512]{1,0:T(8,128)(2,1)S(1)} %convolution_convert_fusion.2), kind=kOutput, calls=%fused_computation | convolution fusion | flops 437911552 | bytes 4390912 | tf_op jit(solution)/shard_map/dot_general | solution.py:69
  134.7 2.8 %convolution_convert_fusion.1 = bf16[512,3328]{1,0:T(8,128)(2,1)} fusion(bf16[2,128,3328]{2,1,0:T(8,128)(2,1)S(1)} %constant_dynamic-update-slice_fusion.14, bf16[384,512]{1,0:T(8,128)(2,1)S(1)} %convolution_convert_fusion.2), kind=kOutput, calls=%fused_computation.1 | convolution fusion | flops 437911552 | bytes 4390912 | tf_op jit(solution)/shard_map/dot_general | solution.py:69
  (111 shorter events, 34.9 us)
Async XLA Ops:
  0.6 1.8 %collective-permute-start = (bf16[16,512]{1,0:T(8,128)(2,1)}, bf16[16,512]{1,0:T(8,128)(2,1)S(1)}, u32[]{:S(2)}, u32[]{:S(2)}) collective-permute-start(bf16[16,512]{1,0:T(8,128)(2,1)} %param.6), channel_id=1, source_target_pairs={{0,16},{1,17},{2,18},{3,19},{4,20},{5,21},{6,22},{7,23},{8,24},{9,... | collective-permute-start | bytes 49160 | tf_op jit(solution)/shard_map/ppermute | solution.py:57
  2.4 6.2 %collective-permute-start.1 = (bf16[32,512]{1,0:T(8,128)(2,1)S(1)}, bf16[32,512]{1,0:T(8,128)(2,1)S(1)}, u32[]{:S(2)}, u32[]{:S(2)}) collective-permute-start(bf16[32,512]{1,0:T(8,128)(2,1)S(1)} %get-tuple-element.21), channel_id=1, source_target_pairs={{0,32},{1,33},{2,34},{3,35},{4,36},{5,37},{6,38},{7,39},{8,40},{9,... | collective-permute-start | bytes 98312 | tf_op jit(solution)/shard_map/ppermute | solution.py:57
  4.5 7.6 %collective-permute-start.3 = (bf16[32,512]{1,0:T(8,128)(2,1)S(1)}, bf16[32,512]{1,0:T(8,128)(2,1)S(1)}, u32[]{:S(2)}, u32[]{:S(2)}) collective-permute-start(bf16[32,512]{1,0:T(8,128)(2,1)S(1)} %get-tuple-element.21), channel_id=1, source_target_pairs={{0,96},{1,97},{2,98},{3,99},{4,100},{5,101},{6,102},{7,103},{8,104... | collective-permute-start | bytes 98312 | tf_op jit(solution)/shard_map/ppermute | solution.py:57
  6.7 5.4 %collective-permute-start.2 = (bf16[32,512]{1,0:T(8,128)(2,1)S(1)}, bf16[32,512]{1,0:T(8,128)(2,1)S(1)}, u32[]{:S(2)}, u32[]{:S(2)}) collective-permute-start(bf16[32,512]{1,0:T(8,128)(2,1)S(1)} %get-tuple-element.21), channel_id=1, source_target_pairs={{0,64},{1,65},{2,66},{3,67},{4,68},{5,69},{6,70},{7,71},{8,72},{9,... | collective-permute-start | bytes 98312 | tf_op jit(solution)/shard_map/ppermute | solution.py:57
  16.2 14.0 %collective-permute-start.6 = (bf16[2,64,3328]{2,1,0:T(8,128)(2,1)S(1)}, bf16[2,64,3328]{2,1,0:T(8,128)(2,1)S(1)}, u32[]{:S(2)}, u32[]{:S(2)}) collective-permute-start(bf16[2,64,3328]{2,1,0:T(8,128)(2,1)S(1)} %fusion.5), channel_id=1, source_target_pairs={{0,3},{1,2},{2,1},{3,0},{4,7},{5,6},{6,5},{7,4},{8,11},{9,10},{10,... | collective-permute-start | bytes 2555912 | tf_op jit(solution)/shard_map/ppermute | solution.py:57
  20.4 12.8 %collective-permute-start.4 = (bf16[2,64,3328]{2,1,0:T(8,128)(2,1)S(1)}, bf16[2,64,3328]{2,1,0:T(8,128)(2,1)S(1)}, u32[]{:S(2)}, u32[]{:S(2)}) collective-permute-start(bf16[2,64,3328]{2,1,0:T(8,128)(2,1)S(1)} %fusion.6), channel_id=1, source_target_pairs={{0,1},{1,0},{2,3},{3,2},{4,5},{5,4},{6,7},{7,6},{8,9},{9,8},{10,11... | collective-permute-start | bytes 2555912 | tf_op jit(solution)/shard_map/ppermute | solution.py:57
  30.4 8.2 %collective-permute-start.7 = (bf16[2,32,3328]{2,1,0:T(8,128)(2,1)S(1)}, bf16[2,32,3328]{2,1,0:T(8,128)(2,1)S(1)}, u32[]{:S(2)}, u32[]{:S(2)}) collective-permute-start(bf16[2,32,3328]{2,1,0:T(8,128)(2,1)S(1)} %slice.203), channel_id=1, source_target_pairs={{0,1},{1,0},{2,3},{3,2},{4,5},{5,4},{6,7},{7,6},{8,9},{9,8},{10,11... | collective-permute-start | bytes 1277960 | tf_op jit(solution)/shard_map/ppermute | solution.py:57
  33.4 9.4 %collective-permute-start.5 = (bf16[2,32,3328]{2,1,0:T(8,128)(2,1)S(1)}, bf16[2,32,3328]{2,1,0:T(8,128)(2,1)S(1)}, u32[]{:S(2)}, u32[]{:S(2)}) collective-permute-start(bf16[2,32,3328]{2,1,0:T(8,128)(2,1)S(1)} %slice.204), channel_id=1, source_target_pairs={{0,3},{1,2},{2,1},{3,0},{4,7},{5,6},{6,5},{7,4},{8,11},{9,10},{10,... | collective-permute-start | bytes 1277960 | tf_op jit(solution)/shard_map/ppermute | solution.py:57
  43.1 7.1 %collective-permute-start.8 = (bf16[4,8,3328]{2,1,0:T(8,128)(2,1)S(1)}, bf16[4,8,3328]{2,1,0:T(8,128)(2,1)S(1)}, u32[]{:S(2)}, u32[]{:S(2)}) collective-permute-start(bf16[4,8,3328]{2,1,0:T(8,128)(2,1)S(1)} %get-tuple-element.13), channel_id=1, source_target_pairs={{0,4},{1,5},{2,6},{3,7},{4,8},{5,9},{6,10},{7,11},{8,12},{9,13},{1... | collective-permute-start | bytes 638984 | tf_op jit(solution)/shard_map/ppermute | solution.py:57
  45.0 5.8 %collective-permute-start.10 = (bf16[4,8,3328]{2,1,0:T(8,128)(2,1)S(1)}, bf16[4,8,3328]{2,1,0:T(8,128)(2,1)S(1)}, u32[]{:S(2)}, u32[]{:S(2)}) collective-permute-start(bf16[4,8,3328]{2,1,0:T(8,128)(2,1)S(1)} %get-tuple-element.14), channel_id=1, source_target_pairs={{0,12},{1,13},{2,14},{3,15},{4,0},{5,1},{6,2},{7,3},{8,4},{9,5},{1... | collective-permute-start | bytes 638984 | tf_op jit(solution)/shard_map/ppermute | solution.py:57
  46.4 7.3 %collective-permute-start.9 = (bf16[4,8,3328]{2,1,0:T(8,128)(2,1)S(1)}, bf16[4,8,3328]{2,1,0:T(8,128)(2,1)S(1)}, u32[]{:S(2)}, u32[]{:S(2)}) collective-permute-start(bf16[4,8,3328]{2,1,0:T(8,128)(2,1)S(1)} %get-tuple-element.15), channel_id=1, source_target_pairs={{0,8},{1,9},{2,10},{3,11},{4,12},{5,13},{6,14},{7,15},{8,0},{9,1},... | collective-permute-start | bytes 638984 | tf_op jit(solution)/shard_map/ppermute | solution.py:57
  53.9 5.4 %collective-permute-start.13 = (bf16[1,8,3328]{2,1,0:T(8,128)(2,1)S(1)}, bf16[1,8,3328]{2,1,0:T(8,128)(2,1)S(1)}, u32[]{:S(2)}, u32[]{:S(2)}) collective-permute-start(bf16[1,8,3328]{2,1,0:T(8,128)(2,1)S(1)} %get-tuple-element.7), channel_id=1, source_target_pairs={{0,4},{1,5},{2,6},{3,7},{4,8},{5,9},{6,10},{7,11},{8,12},{9,13},{1... | collective-permute-start | bytes 159752 | tf_op jit(solution)/shard_map/ppermute | solution.py:57
  55.4 6.1 %collective-permute-start.12 = (bf16[1,8,3328]{2,1,0:T(8,128)(2,1)S(1)}, bf16[1,8,3328]{2,1,0:T(8,128)(2,1)S(1)}, u32[]{:S(2)}, u32[]{:S(2)}) collective-permute-start(bf16[1,8,3328]{2,1,0:T(8,128)(2,1)S(1)} %get-tuple-element.7), channel_id=1, source_target_pairs={{0,8},{1,9},{2,10},{3,11},{4,12},{5,13},{6,14},{7,15},{8,0},{9,1},... | collective-permute-start | bytes 159752 | tf_op jit(solution)/shard_map/ppermute | solution.py:57
  57.5 5.2 %collective-permute-start.11 = (bf16[1,8,3328]{2,1,0:T(8,128)(2,1)S(1)}, bf16[1,8,3328]{2,1,0:T(8,128)(2,1)S(1)}, u32[]{:S(2)}, u32[]{:S(2)}) collective-permute-start(bf16[1,8,3328]{2,1,0:T(8,128)(2,1)S(1)} %get-tuple-element.7), channel_id=1, source_target_pairs={{0,12},{1,13},{2,14},{3,15},{4,0},{5,1},{6,2},{7,3},{8,4},{9,5},{1... | collective-permute-start | bytes 159752 | tf_op jit(solution)/shard_map/ppermute | solution.py:57
  62.7 10.4 %collective-permute-start.16 = (bf16[1,32,3328]{2,1,0:T(8,128)(2,1)S(1)}, bf16[1,32,3328]{2,1,0:T(8,128)(2,1)S(1)}, u32[]{:S(2)}, u32[]{:S(2)}) collective-permute-start(bf16[1,32,3328]{2,1,0:T(8,128)(2,1)S(1)} %pad_maximum_fusion.4), channel_id=1, source_target_pairs={{0,1},{1,2},{2,3},{3,0},{4,5},{5,6},{6,7},{7,4},{8,9},{9,10},{10,1... | collective-permute-start | bytes 638984 | tf_op jit(solution)/shard_map/ppermute | solution.py:57
  62.8 10.3 %collective-permute-start.15 = (bf16[1,32,3328]{2,1,0:T(8,128)(2,1)S(1)}, bf16[1,32,3328]{2,1,0:T(8,128)(2,1)S(1)}, u32[]{:S(2)}, u32[]{:S(2)}) collective-permute-start(bf16[1,32,3328]{2,1,0:T(8,128)(2,1)S(1)} %pad_maximum_fusion.4), channel_id=1, source_target_pairs={{0,2},{1,3},{2,0},{3,1},{4,6},{5,7},{6,4},{7,5},{8,10},{9,11},{10,... | collective-permute-start | bytes 638984 | tf_op jit(solution)/shard_map/ppermute | solution.py:57
  66.1 6.9 %collective-permute-start.14 = (bf16[1,32,3328]{2,1,0:T(8,128)(2,1)S(1)}, bf16[1,32,3328]{2,1,0:T(8,128)(2,1)S(1)}, u32[]{:S(2)}, u32[]{:S(2)}) collective-permute-start(bf16[1,32,3328]{2,1,0:T(8,128)(2,1)S(1)} %pad_maximum_fusion.4), channel_id=1, source_target_pairs={{0,3},{1,0},{2,1},{3,2},{4,7},{5,4},{6,5},{7,6},{8,11},{9,8},{10,9... | collective-permute-start | bytes 638984 | tf_op jit(solution)/shard_map/ppermute | solution.py:57
  75.3 4.9 %collective-permute-start.20 = (bf16[64,512]{1,0:T(8,128)(2,1)S(1)}, bf16[64,512]{1,0:T(8,128)(2,1)S(1)}, u32[]{:S(2)}, u32[]{:S(2)}) collective-permute-start(bf16[64,512]{1,0:T(8,128)(2,1)S(1)} %get-tuple-element.4), channel_id=1, source_target_pairs={{0,96},{1,97},{2,98},{3,99},{4,100},{5,101},{6,102},{7,103},{8,104... | collective-permute-start | bytes 196616 | tf_op jit(solution)/shard_map/ppermute | solution.py:57
  77.1 6.1 %collective-permute-start.19 = (bf16[64,512]{1,0:T(8,128)(2,1)S(1)}, bf16[64,512]{1,0:T(8,128)(2,1)S(1)}, u32[]{:S(2)}, u32[]{:S(2)}) collective-permute-start(bf16[64,512]{1,0:T(8,128)(2,1)S(1)} %get-tuple-element.4), channel_id=1, source_target_pairs={{0,64},{1,65},{2,66},{3,67},{4,68},{5,69},{6,70},{7,71},{8,72},{9,... | collective-permute-start | bytes 196616 | tf_op jit(solution)/shard_map/ppermute | solution.py:57
  77.3 6.3 %collective-permute-start.18 = (bf16[64,512]{1,0:T(8,128)(2,1)S(1)}, bf16[64,512]{1,0:T(8,128)(2,1)S(1)}, u32[]{:S(2)}, u32[]{:S(2)}) collective-permute-start(bf16[64,512]{1,0:T(8,128)(2,1)S(1)} %get-tuple-element.4), channel_id=1, source_target_pairs={{0,32},{1,33},{2,34},{3,35},{4,36},{5,37},{6,38},{7,39},{8,40},{9,... | collective-permute-start | bytes 196616 | tf_op jit(solution)/shard_map/ppermute | solution.py:57
  86.5 7.1 %collective-permute-start.22 = (bf16[1,32,3328]{2,1,0:T(8,128)(2,1)S(1)}, bf16[1,32,3328]{2,1,0:T(8,128)(2,1)S(1)}, u32[]{:S(2)}, u32[]{:S(2)}) collective-permute-start(bf16[1,32,3328]{2,1,0:T(8,128)(2,1)S(1)} %get-tuple-element.10), channel_id=1, source_target_pairs={{0,1},{1,2},{2,3},{3,0},{4,5},{5,6},{6,7},{7,4},{8,9},{9,10},{10,1... | collective-permute-start | bytes 638984 | tf_op jit(solution)/shard_map/ppermute | solution.py:57
  87.1 8.4 %collective-permute-start.24 = (bf16[1,32,3328]{2,1,0:T(8,128)(2,1)S(1)}, bf16[1,32,3328]{2,1,0:T(8,128)(2,1)S(1)}, u32[]{:S(2)}, u32[]{:S(2)}) collective-permute-start(bf16[1,32,3328]{2,1,0:T(8,128)(2,1)S(1)} %get-tuple-element.11), channel_id=1, source_target_pairs={{0,3},{1,0},{2,1},{3,2},{4,7},{5,4},{6,5},{7,6},{8,11},{9,8},{10,9... | collective-permute-start | bytes 638984 | tf_op jit(solution)/shard_map/ppermute | solution.py:57
  89.8 7.3 %collective-permute-start.23 = (bf16[1,32,3328]{2,1,0:T(8,128)(2,1)S(1)}, bf16[1,32,3328]{2,1,0:T(8,128)(2,1)S(1)}, u32[]{:S(2)}, u32[]{:S(2)}) collective-permute-start(bf16[1,32,3328]{2,1,0:T(8,128)(2,1)S(1)} %get-tuple-element.12), channel_id=1, source_target_pairs={{0,2},{1,3},{2,0},{3,1},{4,6},{5,7},{6,4},{7,5},{8,10},{9,11},{10,... | collective-permute-start | bytes 638984 | tf_op jit(solution)/shard_map/ppermute | solution.py:57
  97.3 6.0 %collective-permute-start.25 = (bf16[1,8,3328]{2,1,0:T(8,128)(2,1)S(1)}, bf16[1,8,3328]{2,1,0:T(8,128)(2,1)S(1)}, u32[]{:S(2)}, u32[]{:S(2)}) collective-permute-start(bf16[1,8,3328]{2,1,0:T(8,128)(2,1)S(1)} %get-tuple-element.16), channel_id=1, source_target_pairs={{0,4},{1,5},{2,6},{3,7},{4,8},{5,9},{6,10},{7,11},{8,12},{9,13},{1... | collective-permute-start | bytes 159752 | tf_op jit(solution)/shard_map/ppermute | solution.py:57
  99.6 4.1 %collective-permute-start.27 = (bf16[1,8,3328]{2,1,0:T(8,128)(2,1)S(1)}, bf16[1,8,3328]{2,1,0:T(8,128)(2,1)S(1)}, u32[]{:S(2)}, u32[]{:S(2)}) collective-permute-start(bf16[1,8,3328]{2,1,0:T(8,128)(2,1)S(1)} %get-tuple-element.17), channel_id=1, source_target_pairs={{0,12},{1,13},{2,14},{3,15},{4,0},{5,1},{6,2},{7,3},{8,4},{9,5},{1... | collective-permute-start | bytes 159752 | tf_op jit(solution)/shard_map/ppermute | solution.py:57
  101.3 5.6 %collective-permute-start.26 = (bf16[1,8,3328]{2,1,0:T(8,128)(2,1)S(1)}, bf16[1,8,3328]{2,1,0:T(8,128)(2,1)S(1)}, u32[]{:S(2)}, u32[]{:S(2)}) collective-permute-start(bf16[1,8,3328]{2,1,0:T(8,128)(2,1)S(1)} %get-tuple-element.18), channel_id=1, source_target_pairs={{0,8},{1,9},{2,10},{3,11},{4,12},{5,13},{6,14},{7,15},{8,0},{9,1},... | collective-permute-start | bytes 159752 | tf_op jit(solution)/shard_map/ppermute | solution.py:57
  107.0 6.3 %collective-permute-start.29 = (bf16[2,8,3328]{2,1,0:T(8,128)(2,1)S(1)}, bf16[2,8,3328]{2,1,0:T(8,128)(2,1)S(1)}, u32[]{:S(2)}, u32[]{:S(2)}) collective-permute-start(bf16[2,8,3328]{2,1,0:T(8,128)(2,1)S(1)} %get-tuple-element.19), channel_id=1, source_target_pairs={{0,8},{1,9},{2,10},{3,11},{4,12},{5,13},{6,14},{7,15},{8,0},{9,1},... | collective-permute-start | bytes 319496 | tf_op jit(solution)/shard_map/ppermute | solution.py:57
  108.5 5.2 %collective-permute-start.28 = (bf16[2,8,3328]{2,1,0:T(8,128)(2,1)S(1)}, bf16[2,8,3328]{2,1,0:T(8,128)(2,1)S(1)}, u32[]{:S(2)}, u32[]{:S(2)}) collective-permute-start(bf16[2,8,3328]{2,1,0:T(8,128)(2,1)S(1)} %get-tuple-element.19), channel_id=1, source_target_pairs={{0,12},{1,13},{2,14},{3,15},{4,0},{5,1},{6,2},{7,3},{8,4},{9,5},{1... | collective-permute-start | bytes 319496 | tf_op jit(solution)/shard_map/ppermute | solution.py:57
  110.1 6.7 %collective-permute-start.30 = (bf16[2,8,3328]{2,1,0:T(8,128)(2,1)S(1)}, bf16[2,8,3328]{2,1,0:T(8,128)(2,1)S(1)}, u32[]{:S(2)}, u32[]{:S(2)}) collective-permute-start(bf16[2,8,3328]{2,1,0:T(8,128)(2,1)S(1)} %get-tuple-element.19), channel_id=1, source_target_pairs={{0,4},{1,5},{2,6},{3,7},{4,8},{5,9},{6,10},{7,11},{8,12},{9,13},{1... | collective-permute-start | bytes 319496 | tf_op jit(solution)/shard_map/ppermute | solution.py:57
  116.8 15.0 %collective-permute-start.33 = (bf16[2,32,3328]{2,1,0:T(8,128)(2,1)S(1)}, bf16[2,32,3328]{2,1,0:T(8,128)(2,1)S(1)}, u32[]{:S(2)}, u32[]{:S(2)}) collective-permute-start(bf16[2,32,3328]{2,1,0:T(8,128)(2,1)S(1)} %pad_maximum_fusion.3), channel_id=1, source_target_pairs={{0,1},{1,2},{2,3},{3,0},{4,5},{5,6},{6,7},{7,4},{8,9},{9,10},{10,1... | collective-permute-start | bytes 1277960 | tf_op jit(solution)/shard_map/ppermute | solution.py:57
  118.3 13.4 %collective-permute-start.32 = (bf16[2,32,3328]{2,1,0:T(8,128)(2,1)S(1)}, bf16[2,32,3328]{2,1,0:T(8,128)(2,1)S(1)}, u32[]{:S(2)}, u32[]{:S(2)}) collective-permute-start(bf16[2,32,3328]{2,1,0:T(8,128)(2,1)S(1)} %pad_maximum_fusion.3), channel_id=1, source_target_pairs={{0,2},{1,3},{2,0},{3,1},{4,6},{5,7},{6,4},{7,5},{8,10},{9,11},{10,... | collective-permute-start | bytes 1277960 | tf_op jit(solution)/shard_map/ppermute | solution.py:57
  120.7 11.0 %collective-permute-start.31 = (bf16[2,32,3328]{2,1,0:T(8,128)(2,1)S(1)}, bf16[2,32,3328]{2,1,0:T(8,128)(2,1)S(1)}, u32[]{:S(2)}, u32[]{:S(2)}) collective-permute-start(bf16[2,32,3328]{2,1,0:T(8,128)(2,1)S(1)} %pad_maximum_fusion.3), channel_id=1, source_target_pairs={{0,3},{1,0},{2,1},{3,2},{4,7},{5,4},{6,5},{7,6},{8,11},{9,8},{10,9... | collective-permute-start | bytes 1277960 | tf_op jit(solution)/shard_map/ppermute | solution.py:57
  (6 other events, 84.9 us)

commit v2 on v1

--- a/solution.py
+++ b/solution.py
@@ -20,14 +20,6 @@
         for y in range(4)
         for x in range(4)
     ]
-
-
-def near(i):
-    return i ^ 1
-
-
-def far(i):
-    return i + 1 if i % 2 else i - 1
 
 
 def along_first(move):
@@ -74,39 +66,40 @@
     return jnp.concatenate([chip] + [send(chip, z_shift(d)) for d in (1, 2, 3)])
 
 
-def row_order(first, second, z, k, x, y):
-    first = jnp.repeat(first, 32)
-    second = jnp.tile(jnp.repeat(second, 8), 4)
+def row_order(z, k, x, y):
+    first = jnp.repeat(jnp.arange(4), 32)
+    second = jnp.tile(jnp.repeat(jnp.arange(4), 8), 4)
     high = (x + jnp.where(k == 0, first, second)) % 4
     low = (y + jnp.where(k == 0, second, first)) % 4
     token = (high * 4 + low) * 8 + jnp.tile(jnp.arange(8), 16)
     return ((z - token // 32) % 4) * 32 + ((token // 16 % 2) ^ k) * 16 + token % 16
 
 
-def halve(left, right, tokens, to_half, to_quarter):
-    full = jnp.stack([matmul(tokens, left), matmul(tokens, right)])
-    got = send(full[:, 64:].astype(BF), to_half)
-    half = full[:, :64] + got
-    got = send(half[:, 32:].astype(BF), to_quarter)
-    return half[:, :32] + got
-
-
 def scatter_second(quarter):
-    got = [send(quarter[:, 8 * e : 8 * e + 8].astype(BF), second_shift(e)) for e in (1, 2, 3)]
+    got = [send(quarter[:, 8 * e : 8 * e + 8].astype(BF), second_shift(e)) for e in (2, 1, 3)]
     return quarter[:, :8] + got[0] + got[1] + got[2]
 
 
 def scatter_first(full):
-    got = [send(full[:, 32 * d : 32 * d + 32].astype(BF), first_shift(d)) for d in (1, 2, 3)]
+    got = [send(full[:, 32 * d : 32 * d + 32].astype(BF), first_shift(d)) for d in (2, 1, 3)]
     return full[:, :32] + got[0] + got[1] + got[2]
 
 
+def sum_second(part):
+    rounded = part.astype(BF)
+    for e in (2, 1, 3):
+        part = part + jnp.roll(send(rounded, second_shift(e)), -8 * e, axis=0)
+    return part
+
+
 def gather_second(own):
-    return jnp.concatenate([own] + [send(own, second_shift(-e)) for e in (1, 2, 3)], axis=1)
+    got = {e: send(own, second_shift(-e)) for e in (2, 1, 3)}
+    return jnp.concatenate([own, got[1], got[2], got[3]], axis=1)
 
 
 def gather_first(own):
-    return jnp.concatenate([own] + [send(own, first_shift(-d)) for d in (1, 2, 3)], axis=1)
+    got = {d: send(own, first_shift(-d)) for d in (2, 1, 3)}
+    return jnp.concatenate([own, got[1], got[2], got[3]], axis=1)
 
 
 def swap_axes(value):
@@ -134,33 +127,30 @@
     z, k, y, x = row // 2, row % 2, col // 4, col % 4
     out_scale = 128.0 ** (-0.5)
     gathered = gather_tokens(tokens, z, k)
-    step = 1 - 2 * (jnp.where(k == 0, x, y) % 2)
-    straight = jnp.arange(4)
-    orders = jnp.concatenate(
-        [
-            row_order(jnp.stack([0 * step, -step, step, 2 + 0 * step]), straight, z, k, x, y),
-            row_order(jnp.stack([0 * step, step, -step, 2 + 0 * step]), straight, z, k, x, y),
-            row_order(straight, straight, z, k, x, y),
-        ]
-    )
-    picked = (orders[:, None] == jnp.arange(128)[None, :]).astype(BF)
-    placed = matmul(picked, gathered).astype(BF)
-    tokens_a, tokens_b, local = placed[:128], placed[128:256], placed[256:]
+    order = row_order(z, k, x, y)
+    picked = (order[:, None] == jnp.arange(128)[None, :]).astype(BF)
+    local = matmul(picked, gathered).astype(BF)
 
-    sums = halve(gate_weight, up_weight, tokens_a, along_first(near), along_first(far))
-    dirs = halve(gate_tangent, up_tangent, tokens_b, along_first(far), along_first(near))
-    gate_sum, up_sum, gate_dir, up_dir = scatter_second(jnp.concatenate([sums, dirs]))
+    def hidden_sums(left, right):
+        full = jnp.stack([matmul(local, left), matmul(local, right)])
+        return scatter_second(scatter_first(full))
+
+    gate_sum, up_sum = hidden_sums(gate_weight, up_weight)
+    gate_dir, up_dir = hidden_sums(gate_tangent, up_tangent)
     sigmoid = jax.nn.sigmoid(gate_sum)
     activated = gate_sum * sigmoid
     up_slopes = up_sum * (sigmoid * (1.0 + gate_sum * (1.0 - sigmoid)))
     hidden = (up_slopes * gate_dir + activated * up_dir).astype(BF)
 
-    hidden = gather_first(gather_second(hidden[None]))[0]
+    hidden, activated, up_slopes = gather_second(
+        jnp.stack([hidden, activated.astype(BF), up_slopes.astype(BF)])
+    )
+    hidden = gather_first(hidden[None])[0]
     half = sum_rows(matmul(hidden, down_weight), k)
     output_dir = join_halves((half * out_scale).astype(BF), k)
-    back = scatter_second(scatter_first(against_rows(output_dir, down_weight)[None]))[0]
-    cots = jnp.stack([back * up_slopes, back * activated]).astype(BF)
-    gate_cot, up_cot = gather_first(gather_second(cots))
+    back = sum_second(scatter_first(against_rows(output_dir, down_weight)[None])[0])
+    gate_cot = gather_first((back * up_slopes).astype(BF)[None])[0]
+    up_cot = gather_first((back * activated).astype(BF)[None])[0]
     return transposed(local, gate_cot).astype(BF), transposed(local, up_cot).astype(BF)
 
 

time: 138 us -> 134 us (0.971)
  waiting for transfers between devices: 73.2 us -> 51.9 us
  starting transfers between devices: 47.2 us -> 61.6 us
  local copies, waits for them, and re-layouts: 2.07 us -> 4.29 us
    ppermute x34 -> x39, waiting for transfers between devices: 73.2 us -> 51.9 us  [send(): return lax.ppermute(value, RC, to)]
    ppermute x34 -> x39, starting transfers between devices: 47.2 us -> 61.6 us  [send(): return lax.ppermute(value, RC, to)]
  transfers between devices with their start and end apart: 34 -> 39, of which waited for: 28 -> 26; matrix products, arithmetic and copies ran while one was open for 3% -> 6% of each run, Pallas kernels for 0% -> 0%
where the time goes in v2:
time: 134 us
  starting transfers between devices  61.6 us (46%)
  waiting for transfers between devices  51.9 us (39%)
  matrix products  12.3 us (9%)
  local copies, waits for them, and re-layouts  4.29 us (3%)
  other arithmetic  2.44 us (2%)
    ppermute x39, starting transfers between devices, send(): return lax.ppermute(value, RC, to)  61.6 us
    ppermute x39, waiting for transfers between devices, send(): return lax.ppermute(value, RC, to)  51.9 us
    dot_general x2, matrix products, transposed(): lax.dot_general(left, right, (((0,), (0,)), ((), ())), preferred_element_...  5.64 us
    dot_general x6, matrix products, matmul(): return jnp.dot(left, right, preferred_element_type=F32)  5.42 us
  transfers between devices with their start and end apart: 39, of which 26 were waited for; matrix products, arithmetic and copies ran while one was open for 6% of the time, Pallas kernels for 0%

profile of v2, /device:TPU:0, one launch (start us, length us, event | category | flops | bytes accessed | tf_op | source)
XLA Modules:
  0.0 133.6 jit_solution(15588709186289948317)
XLA Ops:
  4.5 2.0 %collective-permute-start.1 = (bf16[32,512]{1,0:T(8,128)(2,1)}, bf16[32,512]{1,0:T(8,128)(2,1)S(1)}, u32[]{:S(2)}, u32[]{:S(2)}) collective-permute-start(bf16[32,512]{1,0:T(8,128)(2,1)} %get-tuple-element.30), channel_id=1, source_target_pairs={{0,32},{1,33},{2,34},{3,35},{4,36},{5,37},{6,38},{7,39},{8,40},{9,... | collective-permute-start | bytes 98312 | tf_op jit(solution)/shard_map/ppermute | solution.py:49
  7.1 3.7 %collective-permute-start.2 = (bf16[32,512]{1,0:T(8,128)(2,1)}, bf16[32,512]{1,0:T(8,128)(2,1)S(1)}, u32[]{:S(2)}, u32[]{:S(2)}) collective-permute-start(bf16[32,512]{1,0:T(8,128)(2,1)} %get-tuple-element.30), channel_id=1, source_target_pairs={{0,64},{1,65},{2,66},{3,67},{4,68},{5,69},{6,70},{7,71},{8,72},{9,... | collective-permute-start | bytes 98312 | tf_op jit(solution)/shard_map/ppermute | solution.py:49
  12.9 2.0 %collective-permute-done.3 = bf16[32,512]{1,0:T(8,128)(2,1)S(1)} collective-permute-done((bf16[32,512]{1,0:T(8,128)(2,1)}, bf16[32,512]{1,0:T(8,128)(2,1)S(1)}, u32[]{:S(2)}, u32[]{:S(2)}) %collective-permute-start.3) | collective-permute-done | bytes 32800 | tf_op jit(solution)/shard_map/ppermute | solution.py:49
  15.2 2.7 %convolution_bitcast_fusion.3 = f32[1,128,3328]{2,1,0:T(8,128)S(1)} fusion(bf16[128,512]{1,0:T(8,128)(2,1)S(1)} %convolution_convert_fusion.2, bf16[512,3328]{1,0:T(8,128)(2,1)} %param.8), kind=kOutput, calls=%fused_computation.5 | convolution fusion | flops 436207616 | bytes 5242880 | tf_op jit(solution)/shard_map/dot_general | solution.py:53
  19.2 3.1 %collective-permute-start.4 = (bf16[2,32,3328]{2,1,0:T(8,128)(2,1)S(1)}, bf16[2,32,3328]{2,1,0:T(8,128)(2,1)S(1)}, u32[]{:S(2)}, u32[]{:S(2)}) collective-permute-start(bf16[2,32,3328]{2,1,0:T(8,128)(2,1)S(1)} %get-tuple-element.13), channel_id=1, source_target_pairs={{0,2},{1,3},{2,0},{3,1},{4,6},{5,7},{6,4},{7,5},{8,10},{9,11},{10,... | collective-permute-start | bytes 1277960 | tf_op jit(solution)/shard_map/ppermute | solution.py:49
  22.9 2.6 %collective-permute-start.6 = (bf16[2,32,3328]{2,1,0:T(8,128)(2,1)S(1)}, bf16[2,32,3328]{2,1,0:T(8,128)(2,1)S(1)}, u32[]{:S(2)}, u32[]{:S(2)}) collective-permute-start(bf16[2,32,3328]{2,1,0:T(8,128)(2,1)S(1)} %get-tuple-element.14), channel_id=1, source_target_pairs={{0,3},{1,0},{2,1},{3,2},{4,7},{5,4},{6,5},{7,6},{8,11},{9,8},{10,9... | collective-permute-start | bytes 1277960 | tf_op jit(solution)/shard_map/ppermute | solution.py:49
  29.4 2.3 %collective-permute-start.12 = (bf16[2,32,3328]{2,1,0:T(8,128)(2,1)S(1)}, bf16[2,32,3328]{2,1,0:T(8,128)(2,1)S(1)}, u32[]{:S(2)}, u32[]{:S(2)}) collective-permute-start(bf16[2,32,3328]{2,1,0:T(8,128)(2,1)S(1)} %get-tuple-element.11), channel_id=1, source_target_pairs={{0,3},{1,0},{2,1},{3,2},{4,7},{5,4},{6,5},{7,6},{8,11},{9,8},{10,9... | collective-permute-start | bytes 1277960 | tf_op jit(solution)/shard_map/ppermute | solution.py:49
  33.8 3.3 %collective-permute-start.7 = (bf16[2,8,3328]{2,1,0:T(8,128)(2,1)S(1)}, bf16[2,8,3328]{2,1,0:T(8,128)(2,1)S(1)}, u32[]{:S(2)}, u32[]{:S(2)}) collective-permute-start(bf16[2,8,3328]{2,1,0:T(8,128)(2,1)S(1)} %get-tuple-element.22), channel_id=1, source_target_pairs={{0,8},{1,9},{2,10},{3,11},{4,12},{5,13},{6,14},{7,15},{8,0},{9,1},... | collective-permute-start | bytes 319496 | tf_op jit(solution)/shard_map/ppermute | solution.py:49
  37.7 2.3 %collective-permute-done.10 = bf16[2,32,3328]{2,1,0:T(8,128)(2,1)S(1)} collective-permute-done((bf16[2,32,3328]{2,1,0:T(8,128)(2,1)S(1)}, bf16[2,32,3328]{2,1,0:T(8,128)(2,1)S(1)}, u32[]{:S(2)}, u32[]{:S(2)}) %collective-permute-start.10) | collective-permute-done | bytes 426016 | tf_op jit(solution)/shard_map/ppermute | solution.py:49
  40.0 3.4 %collective-permute-start.9 = (bf16[2,8,3328]{2,1,0:T(8,128)(2,1)S(1)}, bf16[2,8,3328]{2,1,0:T(8,128)(2,1)S(1)}, u32[]{:S(2)}, u32[]{:S(2)}) collective-permute-start(bf16[2,8,3328]{2,1,0:T(8,128)(2,1)S(1)} %get-tuple-element.23), channel_id=1, source_target_pairs={{0,12},{1,13},{2,14},{3,15},{4,0},{5,1},{6,2},{7,3},{8,4},{9,5},{1... | collective-permute-start | bytes 319496 | tf_op jit(solution)/shard_map/ppermute | solution.py:49
  45.2 3.3 %collective-permute-start.13 = (bf16[2,8,3328]{2,1,0:T(8,128)(2,1)S(1)}, bf16[2,8,3328]{2,1,0:T(8,128)(2,1)S(1)}, u32[]{:S(2)}, u32[]{:S(2)}) collective-permute-start(bf16[2,8,3328]{2,1,0:T(8,128)(2,1)S(1)} %get-tuple-element.19), channel_id=1, source_target_pairs={{0,8},{1,9},{2,10},{3,11},{4,12},{5,13},{6,14},{7,15},{8,0},{9,1},... | collective-permute-start | bytes 319496 | tf_op jit(solution)/shard_map/ppermute | solution.py:49
  49.2 2.6 %collective-permute-start.15 = (bf16[2,8,3328]{2,1,0:T(8,128)(2,1)S(1)}, bf16[2,8,3328]{2,1,0:T(8,128)(2,1)S(1)}, u32[]{:S(2)}, u32[]{:S(2)}) collective-permute-start(bf16[2,8,3328]{2,1,0:T(8,128)(2,1)S(1)} %get-tuple-element.20), channel_id=1, source_target_pairs={{0,12},{1,13},{2,14},{3,15},{4,0},{5,1},{6,2},{7,3},{8,4},{9,5},{1... | collective-permute-start | bytes 319496 | tf_op jit(solution)/shard_map/ppermute | solution.py:49
  51.8 2.6 %collective-permute-done.14 = bf16[2,8,3328]{2,1,0:T(8,128)(2,1)S(1)} collective-permute-done((bf16[2,8,3328]{2,1,0:T(8,128)(2,1)S(1)}, bf16[2,8,3328]{2,1,0:T(8,128)(2,1)S(1)}, u32[]{:S(2)}, u32[]{:S(2)}) %collective-permute-start.14) | collective-permute-done | bytes 106528 | tf_op jit(solution)/shard_map/ppermute | solution.py:49
  54.6 3.3 %collective-permute-start.16 = (bf16[3,8,3328]{2,1,0:T(8,128)(2,1)S(1)}, bf16[3,8,3328]{2,1,0:T(8,128)(2,1)S(1)}, u32[]{:S(2)}, u32[]{:S(2)}) collective-permute-start(bf16[3,8,3328]{2,1,0:T(8,128)(2,1)S(1)} %pad_maximum_fusion.3), channel_id=1, source_target_pairs={{0,12},{1,13},{2,14},{3,15},{4,0},{5,1},{6,2},{7,3},{8,4},{9,5},{1... | collective-permute-start | bytes 479240 | tf_op jit(solution)/shard_map/ppermute | solution.py:49
  58.8 3.6 %collective-permute-done.16 = bf16[3,8,3328]{2,1,0:T(8,128)(2,1)S(1)} collective-permute-done((bf16[3,8,3328]{2,1,0:T(8,128)(2,1)S(1)}, bf16[3,8,3328]{2,1,0:T(8,128)(2,1)S(1)}, u32[]{:S(2)}, u32[]{:S(2)}) %collective-permute-start.16) | collective-permute-done | bytes 159776 | tf_op jit(solution)/shard_map/ppermute | solution.py:49
  62.4 2.3 %collective-permute-done.17 = bf16[3,8,3328]{2,1,0:T(8,128)(2,1)S(1)} collective-permute-done((bf16[3,8,3328]{2,1,0:T(8,128)(2,1)S(1)}, bf16[3,8,3328]{2,1,0:T(8,128)(2,1)S(1)}, u32[]{:S(2)}, u32[]{:S(2)}) %collective-permute-start.17) | collective-permute-done | bytes 159776 | tf_op jit(solution)/shard_map/ppermute | solution.py:49
  66.2 5.7 %collective-permute-start.19 = (bf16[1,32,3328]{2,1,0:T(8,128)(2,1)S(1)}, bf16[1,32,3328]{2,1,0:T(8,128)(2,1)S(1)}, u32[]{:S(2)}, u32[]{:S(2)}) collective-permute-start(bf16[1,32,3328]{2,1,0:T(8,128)(2,1)S(1)} %unstack.38), channel_id=1, source_target_pairs={{0,3},{1,0},{2,1},{3,2},{4,7},{5,4},{6,5},{7,6},{8,11},{9,8},{10,9... | collective-permute-start | bytes 638984 | tf_op jit(solution)/shard_map/ppermute | solution.py:49
  73.3 4.2 %collective-permute-done.19 = bf16[1,32,3328]{2,1,0:T(8,128)(2,1)S(1)} collective-permute-done((bf16[1,32,3328]{2,1,0:T(8,128)(2,1)S(1)}, bf16[1,32,3328]{2,1,0:T(8,128)(2,1)S(1)}, u32[]{:S(2)}, u32[]{:S(2)}) %collective-permute-start.19) | collective-permute-done | bytes 213024 | tf_op jit(solution)/shard_map/ppermute | solution.py:49
  79.3 2.2 %collective-permute-done.21 = bf16[1,32,3328]{2,1,0:T(8,128)(2,1)S(1)} collective-permute-done((bf16[1,32,3328]{2,1,0:T(8,128)(2,1)S(1)}, bf16[1,32,3328]{2,1,0:T(8,128)(2,1)S(1)}, u32[]{:S(2)}, u32[]{:S(2)}) %collective-permute-start.21) | collective-permute-done | bytes 213024 | tf_op jit(solution)/shard_map/ppermute | solution.py:49
  83.8 3.7 %collective-permute-start.24 = (bf16[64,512]{1,0:T(8,128)(2,1)S(1)}, bf16[64,512]{1,0:T(8,128)(2,1)S(1)}, u32[]{:S(2)}, u32[]{:S(2)}) collective-permute-start(bf16[64,512]{1,0:T(8,128)(2,1)S(1)} %get-tuple-element.4), channel_id=1, source_target_pairs={{0,64},{1,65},{2,66},{3,67},{4,68},{5,69},{6,70},{7,71},{8,72},{9,... | collective-permute-start | bytes 196616 | tf_op jit(solution)/shard_map/ppermute | solution.py:49
  87.6 2.1 %collective-permute-done.23 = bf16[64,512]{1,0:T(8,128)(2,1)S(1)} collective-permute-done((bf16[64,512]{1,0:T(8,128)(2,1)S(1)}, bf16[64,512]{1,0:T(8,128)(2,1)S(1)}, u32[]{:S(2)}, u32[]{:S(2)}) %collective-permute-start.23) | collective-permute-done | bytes 65568 | tf_op jit(solution)/shard_map/ppermute | solution.py:49
  96.0 3.2 %collective-permute-start.29 = (bf16[1,32,3328]{2,1,0:T(8,128)(2,1)S(1)}, bf16[1,32,3328]{2,1,0:T(8,128)(2,1)S(1)}, u32[]{:S(2)}, u32[]{:S(2)}) collective-permute-start(bf16[1,32,3328]{2,1,0:T(8,128)(2,1)S(1)} %get-tuple-element.17), channel_id=1, source_target_pairs={{0,3},{1,0},{2,1},{3,2},{4,7},{5,4},{6,5},{7,6},{8,11},{9,8},{10,9... | collective-permute-start | bytes 638984 | tf_op jit(solution)/shard_map/ppermute | solution.py:49
  99.2 2.8 %collective-permute-done.27 = bf16[1,32,3328]{2,1,0:T(8,128)(2,1)S(1)} collective-permute-done((bf16[1,32,3328]{2,1,0:T(8,128)(2,1)S(1)}, bf16[1,32,3328]{2,1,0:T(8,128)(2,1)S(1)}, u32[]{:S(2)}, u32[]{:S(2)}) %collective-permute-start.27) | collective-permute-done | bytes 213024 | tf_op jit(solution)/shard_map/ppermute | solution.py:49
  102.0 2.2 %collective-permute-done.28 = bf16[1,32,3328]{2,1,0:T(8,128)(2,1)S(1)} collective-permute-done((bf16[1,32,3328]{2,1,0:T(8,128)(2,1)S(1)}, bf16[1,32,3328]{2,1,0:T(8,128)(2,1)S(1)}, u32[]{:S(2)}, u32[]{:S(2)}) %collective-permute-start.28) | collective-permute-done | bytes 213024 | tf_op jit(solution)/shard_map/ppermute | solution.py:49
  106.4 3.8 %collective-permute-done.32 = bf16[32,3328]{1,0:T(8,128)(2,1)S(1)} collective-permute-done((bf16[32,3328]{1,0:T(8,128)(2,1)S(1)}, bf16[32,3328]{1,0:T(8,128)(2,1)S(1)}, u32[]{:S(2)}, u32[]{:S(2)}) %collective-permute-start.32) | collective-permute-done | bytes 213024 | tf_op jit(solution)/shard_map/ppermute | solution.py:49
  110.2 4.2 %collective-permute-done.31 = bf16[32,3328]{1,0:T(8,128)(2,1)S(1)} collective-permute-done((bf16[32,3328]{1,0:T(8,128)(2,1)S(1)}, bf16[32,3328]{1,0:T(8,128)(2,1)S(1)}, u32[]{:S(2)}, u32[]{:S(2)}) %collective-permute-start.31) | collective-permute-done | bytes 213024 | tf_op jit(solution)/shard_map/ppermute | solution.py:49
  117.5 2.4 %collective-permute-start.33 = (bf16[1,32,3328]{2,1,0:T(8,128)(2,1)S(1)}, bf16[1,32,3328]{2,1,0:T(8,128)(2,1)S(1)}, u32[]{:S(2)}, u32[]{:S(2)}) collective-permute-start(bf16[1,32,3328]{2,1,0:T(8,128)(2,1)S(1)} %multiply_convert_fusion.1), channel_id=1, source_target_pairs={{0,3},{1,0},{2,1},{3,2},{4,7},{5,4},{6,5},{7,6},{8,11},{9,8},{10,9... | collective-permute-start | bytes 638984 | tf_op jit(solution)/shard_map/ppermute | solution.py:49
  119.9 2.3 %collective-permute-start.34 = (bf16[1,32,3328]{2,1,0:T(8,128)(2,1)S(1)}, bf16[1,32,3328]{2,1,0:T(8,128)(2,1)S(1)}, u32[]{:S(2)}, u32[]{:S(2)}) collective-permute-start(bf16[1,32,3328]{2,1,0:T(8,128)(2,1)S(1)} %multiply_convert_fusion.1), channel_id=1, source_target_pairs={{0,2},{1,3},{2,0},{3,1},{4,6},{5,7},{6,4},{7,5},{8,10},{9,11},{10,... | collective-permute-start | bytes 638984 | tf_op jit(solution)/shard_map/ppermute | solution.py:49
  124.0 1.9 %collective-permute-done.38 = bf16[1,32,3328]{2,1,0:T(8,128)(2,1)S(1)} collective-permute-done((bf16[1,32,3328]{2,1,0:T(8,128)(2,1)S(1)}, bf16[1,32,3328]{2,1,0:T(8,128)(2,1)S(1)}, u32[]{:S(2)}, u32[]{:S(2)}) %collective-permute-start.38) | collective-permute-done | bytes 213024 | tf_op jit(solution)/shard_map/ppermute | solution.py:49
  125.9 2.8 %convolution_convert_fusion = bf16[512,3328]{1,0:T(8,128)(2,1)} fusion(bf16[128,512]{1,0:T(8,128)(2,1)S(1)} %convolution_convert_fusion.2, bf16[1,32,3328]{2,1,0:T(8,128)(2,1)S(1)} %collective-permute-done.38, bf16[1,32,3328]{2,1,0:T(8,128)(2,1)S(1)} %collective-permute-done.37, bf16[1,32,3328]{2,1,0:T(8,128)(2,1)S(1)} %collective-permute-done.36, ...), kind=kOutput, calls=%fused_computation | convolution fusion | flops 441319424 | bytes 4390912 | tf_op jit(solution)/shard_map/dot_general | solution.py:61
  128.7 2.1 %collective-permute-done.35 = bf16[1,32,3328]{2,1,0:T(8,128)(2,1)S(1)} collective-permute-done((bf16[1,32,3328]{2,1,0:T(8,128)(2,1)S(1)}, bf16[1,32,3328]{2,1,0:T(8,128)(2,1)S(1)}, u32[]{:S(2)}, u32[]{:S(2)}) %collective-permute-start.35) | collective-permute-done | bytes 213024 | tf_op jit(solution)/shard_map/ppermute | solution.py:49
  130.8 2.8 %convolution_convert_fusion.1 = bf16[512,3328]{1,0:T(8,128)(2,1)} fusion(bf16[128,512]{1,0:T(8,128)(2,1)S(1)} %convolution_convert_fusion.2, bf16[1,32,3328]{2,1,0:T(8,128)(2,1)S(1)} %collective-permute-done.35, bf16[1,32,3328]{2,1,0:T(8,128)(2,1)S(1)} %collective-permute-done.34, bf16[1,32,3328]{2,1,0:T(8,128)(2,1)S(1)} %collective-permute-done.33, ...), kind=kOutput, calls=%fused_computation.1 | convolution fusion | flops 441319424 | bytes 4390912 | tf_op jit(solution)/shard_map/dot_general | solution.py:61
  (107 shorter events, 39.2 us)
Async XLA Ops:
  4.5 7.4 %collective-permute-start.1 = (bf16[32,512]{1,0:T(8,128)(2,1)}, bf16[32,512]{1,0:T(8,128)(2,1)S(1)}, u32[]{:S(2)}, u32[]{:S(2)}) collective-permute-start(bf16[32,512]{1,0:T(8,128)(2,1)} %get-tuple-element.30), channel_id=1, source_target_pairs={{0,32},{1,33},{2,34},{3,35},{4,36},{5,37},{6,38},{7,39},{8,40},{9,... | collective-permute-start | bytes 98312 | tf_op jit(solution)/shard_map/ppermute | solution.py:49
  19.2 10.3 %collective-permute-start.4 = (bf16[2,32,3328]{2,1,0:T(8,128)(2,1)S(1)}, bf16[2,32,3328]{2,1,0:T(8,128)(2,1)S(1)}, u32[]{:S(2)}, u32[]{:S(2)}) collective-permute-start(bf16[2,32,3328]{2,1,0:T(8,128)(2,1)S(1)} %get-tuple-element.13), channel_id=1, source_target_pairs={{0,2},{1,3},{2,0},{3,1},{4,6},{5,7},{6,4},{7,5},{8,10},{9,11},{10,... | collective-permute-start | bytes 1277960 | tf_op jit(solution)/shard_map/ppermute | solution.py:49
  22.3 11.2 %collective-permute-start.5 = (bf16[2,32,3328]{2,1,0:T(8,128)(2,1)S(1)}, bf16[2,32,3328]{2,1,0:T(8,128)(2,1)S(1)}, u32[]{:S(2)}, u32[]{:S(2)}) collective-permute-start(bf16[2,32,3328]{2,1,0:T(8,128)(2,1)S(1)} %get-tuple-element.15), channel_id=1, source_target_pairs={{0,1},{1,2},{2,3},{3,0},{4,5},{5,6},{6,7},{7,4},{8,9},{9,10},{10,1... | collective-permute-start | bytes 1277960 | tf_op jit(solution)/shard_map/ppermute | solution.py:49
  22.9 10.7 %collective-permute-start.6 = (bf16[2,32,3328]{2,1,0:T(8,128)(2,1)S(1)}, bf16[2,32,3328]{2,1,0:T(8,128)(2,1)S(1)}, u32[]{:S(2)}, u32[]{:S(2)}) collective-permute-start(bf16[2,32,3328]{2,1,0:T(8,128)(2,1)S(1)} %get-tuple-element.14), channel_id=1, source_target_pairs={{0,3},{1,0},{2,1},{3,2},{4,7},{5,4},{6,5},{7,6},{8,11},{9,8},{10,9... | collective-permute-start | bytes 1277960 | tf_op jit(solution)/shard_map/ppermute | solution.py:49
  27.2 12.8 %collective-permute-start.10 = (bf16[2,32,3328]{2,1,0:T(8,128)(2,1)S(1)}, bf16[2,32,3328]{2,1,0:T(8,128)(2,1)S(1)}, u32[]{:S(2)}, u32[]{:S(2)}) collective-permute-start(bf16[2,32,3328]{2,1,0:T(8,128)(2,1)S(1)} %get-tuple-element.10), channel_id=1, source_target_pairs={{0,2},{1,3},{2,0},{3,1},{4,6},{5,7},{6,4},{7,5},{8,10},{9,11},{10,... | collective-permute-start | bytes 1277960 | tf_op jit(solution)/shard_map/ppermute | solution.py:49
  27.9 16.9 %collective-permute-start.11 = (bf16[2,32,3328]{2,1,0:T(8,128)(2,1)S(1)}, bf16[2,32,3328]{2,1,0:T(8,128)(2,1)S(1)}, u32[]{:S(2)}, u32[]{:S(2)}) collective-permute-start(bf16[2,32,3328]{2,1,0:T(8,128)(2,1)S(1)} %get-tuple-element.12), channel_id=1, source_target_pairs={{0,1},{1,2},{2,3},{3,0},{4,5},{5,6},{6,7},{7,4},{8,9},{9,10},{10,1... | collective-permute-start | bytes 1277960 | tf_op jit(solution)/shard_map/ppermute | solution.py:49
  29.4 15.6 %collective-permute-start.12 = (bf16[2,32,3328]{2,1,0:T(8,128)(2,1)S(1)}, bf16[2,32,3328]{2,1,0:T(8,128)(2,1)S(1)}, u32[]{:S(2)}, u32[]{:S(2)}) collective-permute-start(bf16[2,32,3328]{2,1,0:T(8,128)(2,1)S(1)} %get-tuple-element.11), channel_id=1, source_target_pairs={{0,3},{1,0},{2,1},{3,2},{4,7},{5,4},{6,5},{7,6},{8,11},{9,8},{10,9... | collective-permute-start | bytes 1277960 | tf_op jit(solution)/shard_map/ppermute | solution.py:49
  33.8 15.4 %collective-permute-start.7 = (bf16[2,8,3328]{2,1,0:T(8,128)(2,1)S(1)}, bf16[2,8,3328]{2,1,0:T(8,128)(2,1)S(1)}, u32[]{:S(2)}, u32[]{:S(2)}) collective-permute-start(bf16[2,8,3328]{2,1,0:T(8,128)(2,1)S(1)} %get-tuple-element.22), channel_id=1, source_target_pairs={{0,8},{1,9},{2,10},{3,11},{4,12},{5,13},{6,14},{7,15},{8,0},{9,1},... | collective-permute-start | bytes 319496 | tf_op jit(solution)/shard_map/ppermute | solution.py:49
  37.0 14.7 %collective-permute-start.8 = (bf16[2,8,3328]{2,1,0:T(8,128)(2,1)S(1)}, bf16[2,8,3328]{2,1,0:T(8,128)(2,1)S(1)}, u32[]{:S(2)}, u32[]{:S(2)}) collective-permute-start(bf16[2,8,3328]{2,1,0:T(8,128)(2,1)S(1)} %get-tuple-element.24), channel_id=1, source_target_pairs={{0,4},{1,5},{2,6},{3,7},{4,8},{5,9},{6,10},{7,11},{8,12},{9,13},{1... | collective-permute-start | bytes 319496 | tf_op jit(solution)/shard_map/ppermute | solution.py:49
  40.0 11.8 %collective-permute-start.9 = (bf16[2,8,3328]{2,1,0:T(8,128)(2,1)S(1)}, bf16[2,8,3328]{2,1,0:T(8,128)(2,1)S(1)}, u32[]{:S(2)}, u32[]{:S(2)}) collective-permute-start(bf16[2,8,3328]{2,1,0:T(8,128)(2,1)S(1)} %get-tuple-element.23), channel_id=1, source_target_pairs={{0,12},{1,13},{2,14},{3,15},{4,0},{5,1},{6,2},{7,3},{8,4},{9,5},{1... | collective-permute-start | bytes 319496 | tf_op jit(solution)/shard_map/ppermute | solution.py:49
  45.2 6.6 %collective-permute-start.13 = (bf16[2,8,3328]{2,1,0:T(8,128)(2,1)S(1)}, bf16[2,8,3328]{2,1,0:T(8,128)(2,1)S(1)}, u32[]{:S(2)}, u32[]{:S(2)}) collective-permute-start(bf16[2,8,3328]{2,1,0:T(8,128)(2,1)S(1)} %get-tuple-element.19), channel_id=1, source_target_pairs={{0,8},{1,9},{2,10},{3,11},{4,12},{5,13},{6,14},{7,15},{8,0},{9,1},... | collective-permute-start | bytes 319496 | tf_op jit(solution)/shard_map/ppermute | solution.py:49
  48.5 5.9 %collective-permute-start.14 = (bf16[2,8,3328]{2,1,0:T(8,128)(2,1)S(1)}, bf16[2,8,3328]{2,1,0:T(8,128)(2,1)S(1)}, u32[]{:S(2)}, u32[]{:S(2)}) collective-permute-start(bf16[2,8,3328]{2,1,0:T(8,128)(2,1)S(1)} %get-tuple-element.21), channel_id=1, source_target_pairs={{0,4},{1,5},{2,6},{3,7},{4,8},{5,9},{6,10},{7,11},{8,12},{9,13},{1... | collective-permute-start | bytes 319496 | tf_op jit(solution)/shard_map/ppermute | solution.py:49
  54.6 7.8 %collective-permute-start.16 = (bf16[3,8,3328]{2,1,0:T(8,128)(2,1)S(1)}, bf16[3,8,3328]{2,1,0:T(8,128)(2,1)S(1)}, u32[]{:S(2)}, u32[]{:S(2)}) collective-permute-start(bf16[3,8,3328]{2,1,0:T(8,128)(2,1)S(1)} %pad_maximum_fusion.3), channel_id=1, source_target_pairs={{0,12},{1,13},{2,14},{3,15},{4,0},{5,1},{6,2},{7,3},{8,4},{9,5},{1... | collective-permute-start | bytes 479240 | tf_op jit(solution)/shard_map/ppermute | solution.py:49
  57.9 6.9 %collective-permute-start.17 = (bf16[3,8,3328]{2,1,0:T(8,128)(2,1)S(1)}, bf16[3,8,3328]{2,1,0:T(8,128)(2,1)S(1)}, u32[]{:S(2)}, u32[]{:S(2)}) collective-permute-start(bf16[3,8,3328]{2,1,0:T(8,128)(2,1)S(1)} %pad_maximum_fusion.3), channel_id=1, source_target_pairs={{0,8},{1,9},{2,10},{3,11},{4,12},{5,13},{6,14},{7,15},{8,0},{9,1},... | collective-permute-start | bytes 479240 | tf_op jit(solution)/shard_map/ppermute | solution.py:49
  57.9 8.2 %collective-permute-start.18 = (bf16[3,8,3328]{2,1,0:T(8,128)(2,1)S(1)}, bf16[3,8,3328]{2,1,0:T(8,128)(2,1)S(1)}, u32[]{:S(2)}, u32[]{:S(2)}) collective-permute-start(bf16[3,8,3328]{2,1,0:T(8,128)(2,1)S(1)} %pad_maximum_fusion.3), channel_id=1, source_target_pairs={{0,4},{1,5},{2,6},{3,7},{4,8},{5,9},{6,10},{7,11},{8,12},{9,13},{1... | collective-permute-start | bytes 479240 | tf_op jit(solution)/shard_map/ppermute | solution.py:49
  66.2 11.4 %collective-permute-start.19 = (bf16[1,32,3328]{2,1,0:T(8,128)(2,1)S(1)}, bf16[1,32,3328]{2,1,0:T(8,128)(2,1)S(1)}, u32[]{:S(2)}, u32[]{:S(2)}) collective-permute-start(bf16[1,32,3328]{2,1,0:T(8,128)(2,1)S(1)} %unstack.38), channel_id=1, source_target_pairs={{0,3},{1,0},{2,1},{3,2},{4,7},{5,4},{6,5},{7,6},{8,11},{9,8},{10,9... | collective-permute-start | bytes 638984 | tf_op jit(solution)/shard_map/ppermute | solution.py:49
  71.9 7.5 %collective-permute-start.20 = (bf16[1,32,3328]{2,1,0:T(8,128)(2,1)S(1)}, bf16[1,32,3328]{2,1,0:T(8,128)(2,1)S(1)}, u32[]{:S(2)}, u32[]{:S(2)}) collective-permute-start(bf16[1,32,3328]{2,1,0:T(8,128)(2,1)S(1)} %unstack.38), channel_id=1, source_target_pairs={{0,2},{1,3},{2,0},{3,1},{4,6},{5,7},{6,4},{7,5},{8,10},{9,11},{10,... | collective-permute-start | bytes 638984 | tf_op jit(solution)/shard_map/ppermute | solution.py:49
  73.3 8.2 %collective-permute-start.21 = (bf16[1,32,3328]{2,1,0:T(8,128)(2,1)S(1)}, bf16[1,32,3328]{2,1,0:T(8,128)(2,1)S(1)}, u32[]{:S(2)}, u32[]{:S(2)}) collective-permute-start(bf16[1,32,3328]{2,1,0:T(8,128)(2,1)S(1)} %unstack.38), channel_id=1, source_target_pairs={{0,1},{1,2},{2,3},{3,0},{4,5},{5,6},{6,7},{7,4},{8,9},{9,10},{10,1... | collective-permute-start | bytes 638984 | tf_op jit(solution)/shard_map/ppermute | solution.py:49
  83.7 6.0 %collective-permute-start.23 = (bf16[64,512]{1,0:T(8,128)(2,1)S(1)}, bf16[64,512]{1,0:T(8,128)(2,1)S(1)}, u32[]{:S(2)}, u32[]{:S(2)}) collective-permute-start(bf16[64,512]{1,0:T(8,128)(2,1)S(1)} %get-tuple-element.4), channel_id=1, source_target_pairs={{0,32},{1,33},{2,34},{3,35},{4,36},{5,37},{6,38},{7,39},{8,40},{9,... | collective-permute-start | bytes 196616 | tf_op jit(solution)/shard_map/ppermute | solution.py:49
  83.8 7.2 %collective-permute-start.24 = (bf16[64,512]{1,0:T(8,128)(2,1)S(1)}, bf16[64,512]{1,0:T(8,128)(2,1)S(1)}, u32[]{:S(2)}, u32[]{:S(2)}) collective-permute-start(bf16[64,512]{1,0:T(8,128)(2,1)S(1)} %get-tuple-element.4), channel_id=1, source_target_pairs={{0,64},{1,65},{2,66},{3,67},{4,68},{5,69},{6,70},{7,71},{8,72},{9,... | collective-permute-start | bytes 196616 | tf_op jit(solution)/shard_map/ppermute | solution.py:49
  94.5 7.5 %collective-permute-start.27 = (bf16[1,32,3328]{2,1,0:T(8,128)(2,1)S(1)}, bf16[1,32,3328]{2,1,0:T(8,128)(2,1)S(1)}, u32[]{:S(2)}, u32[]{:S(2)}) collective-permute-start(bf16[1,32,3328]{2,1,0:T(8,128)(2,1)S(1)} %get-tuple-element.16), channel_id=1, source_target_pairs={{0,2},{1,3},{2,0},{3,1},{4,6},{5,7},{6,4},{7,5},{8,10},{9,11},{10,... | collective-permute-start | bytes 638984 | tf_op jit(solution)/shard_map/ppermute | solution.py:49
  96.0 8.2 %collective-permute-start.28 = (bf16[1,32,3328]{2,1,0:T(8,128)(2,1)S(1)}, bf16[1,32,3328]{2,1,0:T(8,128)(2,1)S(1)}, u32[]{:S(2)}, u32[]{:S(2)}) collective-permute-start(bf16[1,32,3328]{2,1,0:T(8,128)(2,1)S(1)} %get-tuple-element.18), channel_id=1, source_target_pairs={{0,1},{1,2},{2,3},{3,0},{4,5},{5,6},{6,7},{7,4},{8,9},{9,10},{10,1... | collective-permute-start | bytes 638984 | tf_op jit(solution)/shard_map/ppermute | solution.py:49
  96.0 8.2 %collective-permute-start.29 = (bf16[1,32,3328]{2,1,0:T(8,128)(2,1)S(1)}, bf16[1,32,3328]{2,1,0:T(8,128)(2,1)S(1)}, u32[]{:S(2)}, u32[]{:S(2)}) collective-permute-start(bf16[1,32,3328]{2,1,0:T(8,128)(2,1)S(1)} %get-tuple-element.17), channel_id=1, source_target_pairs={{0,3},{1,0},{2,1},{3,2},{4,7},{5,4},{6,5},{7,6},{8,11},{9,8},{10,9... | collective-permute-start | bytes 638984 | tf_op jit(solution)/shard_map/ppermute | solution.py:49
  104.3 5.9 %collective-permute-start.32 = (bf16[32,3328]{1,0:T(8,128)(2,1)S(1)}, bf16[32,3328]{1,0:T(8,128)(2,1)S(1)}, u32[]{:S(2)}, u32[]{:S(2)}) collective-permute-start(bf16[32,3328]{1,0:T(8,128)(2,1)S(1)} %convert_bitcast_fusion), channel_id=1, source_target_pairs={{0,12},{1,13},{2,14},{3,15},{4,0},{5,1},{6,2},{7,3},{8,4},{9,5},{1... | collective-permute-start | bytes 638984 | tf_op jit(solution)/shard_map/ppermute | solution.py:49
  104.8 9.7 %collective-permute-start.30 = (bf16[32,3328]{1,0:T(8,128)(2,1)S(1)}, bf16[32,3328]{1,0:T(8,128)(2,1)S(1)}, u32[]{:S(2)}, u32[]{:S(2)}) collective-permute-start(bf16[32,3328]{1,0:T(8,128)(2,1)S(1)} %convert_bitcast_fusion), channel_id=1, source_target_pairs={{0,8},{1,9},{2,10},{3,11},{4,12},{5,13},{6,14},{7,15},{8,0},{9,1},... | collective-permute-start | bytes 638984 | tf_op jit(solution)/shard_map/ppermute | solution.py:49
  104.9 9.5 %collective-permute-start.31 = (bf16[32,3328]{1,0:T(8,128)(2,1)S(1)}, bf16[32,3328]{1,0:T(8,128)(2,1)S(1)}, u32[]{:S(2)}, u32[]{:S(2)}) collective-permute-start(bf16[32,3328]{1,0:T(8,128)(2,1)S(1)} %convert_bitcast_fusion), channel_id=1, source_target_pairs={{0,4},{1,5},{2,6},{3,7},{4,8},{5,9},{6,10},{7,11},{8,12},{9,13},{1... | collective-permute-start | bytes 638984 | tf_op jit(solution)/shard_map/ppermute | solution.py:49
  114.7 7.5 %collective-permute-start.36 = (bf16[1,32,3328]{2,1,0:T(8,128)(2,1)S(1)}, bf16[1,32,3328]{2,1,0:T(8,128)(2,1)S(1)}, u32[]{:S(2)}, u32[]{:S(2)}) collective-permute-start(bf16[1,32,3328]{2,1,0:T(8,128)(2,1)S(1)} %get-tuple-element.2), channel_id=1, source_target_pairs={{0,3},{1,0},{2,1},{3,2},{4,7},{5,4},{6,5},{7,6},{8,11},{9,8},{10,9... | collective-permute-start | bytes 638984 | tf_op jit(solution)/shard_map/ppermute | solution.py:49
  116.5 7.5 %collective-permute-start.37 = (bf16[1,32,3328]{2,1,0:T(8,128)(2,1)S(1)}, bf16[1,32,3328]{2,1,0:T(8,128)(2,1)S(1)}, u32[]{:S(2)}, u32[]{:S(2)}) collective-permute-start(bf16[1,32,3328]{2,1,0:T(8,128)(2,1)S(1)} %get-tuple-element.2), channel_id=1, source_target_pairs={{0,2},{1,3},{2,0},{3,1},{4,6},{5,7},{6,4},{7,5},{8,10},{9,11},{10,... | collective-permute-start | bytes 638984 | tf_op jit(solution)/shard_map/ppermute | solution.py:49
  116.6 9.3 %collective-permute-start.38 = (bf16[1,32,3328]{2,1,0:T(8,128)(2,1)S(1)}, bf16[1,32,3328]{2,1,0:T(8,128)(2,1)S(1)}, u32[]{:S(2)}, u32[]{:S(2)}) collective-permute-start(bf16[1,32,3328]{2,1,0:T(8,128)(2,1)S(1)} %get-tuple-element.2), channel_id=1, source_target_pairs={{0,1},{1,2},{2,3},{3,0},{4,5},{5,6},{6,7},{7,4},{8,9},{9,10},{10,1... | collective-permute-start | bytes 638984 | tf_op jit(solution)/shard_map/ppermute | solution.py:49
  117.5 11.2 %collective-permute-start.33 = (bf16[1,32,3328]{2,1,0:T(8,128)(2,1)S(1)}, bf16[1,32,3328]{2,1,0:T(8,128)(2,1)S(1)}, u32[]{:S(2)}, u32[]{:S(2)}) collective-permute-start(bf16[1,32,3328]{2,1,0:T(8,128)(2,1)S(1)} %multiply_convert_fusion.1), channel_id=1, source_target_pairs={{0,3},{1,0},{2,1},{3,2},{4,7},{5,4},{6,5},{7,6},{8,11},{9,8},{10,9... | collective-permute-start | bytes 638984 | tf_op jit(solution)/shard_map/ppermute | solution.py:49
  119.9 8.8 %collective-permute-start.34 = (bf16[1,32,3328]{2,1,0:T(8,128)(2,1)S(1)}, bf16[1,32,3328]{2,1,0:T(8,128)(2,1)S(1)}, u32[]{:S(2)}, u32[]{:S(2)}) collective-permute-start(bf16[1,32,3328]{2,1,0:T(8,128)(2,1)S(1)} %multiply_convert_fusion.1), channel_id=1, source_target_pairs={{0,2},{1,3},{2,0},{3,1},{4,6},{5,7},{6,4},{7,5},{8,10},{9,11},{10,... | collective-permute-start | bytes 638984 | tf_op jit(solution)/shard_map/ppermute | solution.py:49
  122.2 8.6 %collective-permute-start.35 = (bf16[1,32,3328]{2,1,0:T(8,128)(2,1)S(1)}, bf16[1,32,3328]{2,1,0:T(8,128)(2,1)S(1)}, u32[]{:S(2)}, u32[]{:S(2)}) collective-permute-start(bf16[1,32,3328]{2,1,0:T(8,128)(2,1)S(1)} %multiply_convert_fusion.1), channel_id=1, source_target_pairs={{0,1},{1,2},{2,3},{3,0},{4,5},{5,6},{6,7},{7,4},{8,9},{9,10},{10,1... | collective-permute-start | bytes 638984 | tf_op jit(solution)/shard_map/ppermute | solution.py:49
  (11 other events, 118.5 us)

commit v3 on v2

--- a/solution.py
+++ b/solution.py
@@ -1,6 +1,8 @@
 import jax
 import jax.numpy as jnp
 from jax import lax
+from jax.experimental import pallas as pl
+from jax.experimental.pallas import tpu as pltpu
 from jax.sharding import PartitionSpec as P
 
 BF = jnp.bfloat16
@@ -22,6 +24,14 @@
     ]
 
 
+def near(i):
+    return i ^ 1
+
+
+def far(i):
+    return i + 1 if i % 2 else i - 1
+
+
 def along_first(move):
     return pairs(lambda z, k, y, x: (z, k, y, move(x)) if k == 0 else (z, k, move(y), x))
 
@@ -61,18 +71,98 @@
     return lax.dot_general(left, right, (((0,), (0,)), ((), ())), preferred_element_type=F32)
 
 
-def gather_tokens(tokens, z, k):
-    chip = jnp.concatenate([tokens, send(tokens, CORE)])
-    return jnp.concatenate([chip] + [send(chip, z_shift(d)) for d in (1, 2, 3)])
-
-
-def row_order(z, k, x, y):
-    first = jnp.repeat(jnp.arange(4), 32)
-    second = jnp.tile(jnp.repeat(jnp.arange(4), 8), 4)
-    high = (x + jnp.where(k == 0, first, second)) % 4
-    low = (y + jnp.where(k == 0, second, first)) % 4
-    token = (high * 4 + low) * 8 + jnp.tile(jnp.arange(8), 16)
-    return ((z - token // 32) % 4) * 32 + ((token // 16 % 2) ^ k) * 16 + token % 16
+def gather_tokens(tokens, ready):
+    got = {d: send(tokens, z_shift(d)) for d in (2, 1, 3)}
+    own = jnp.concatenate([tokens, got[1], got[2], got[3]])
+    own = after(own, ready)
+    return own, send(own, CORE)
+
+
+def order_matrix(offsets, z, k, x, y):
+    local = lax.broadcasted_iota(jnp.int32, (128, 128), 0)
+    column = lax.broadcasted_iota(jnp.int32, (128, 128), 1)
+    block, second = local // 32, local // 8 % 4
+    first = jnp.where(
+        block == 1, offsets[1], jnp.where(block == 2, offsets[2], jnp.where(block == 3, offsets[3], offsets[0]))
+    )
+    high = (x + jnp.where(k == 0, first, second)) & 3
+    low = (y + jnp.where(k == 0, second, first)) & 3
+    token = (high * 4 + low) * 8 + local % 8
+    place = ((token // 16 & 1) ^ k) * 64 + ((z - token // 32) & 3) * 16 + token % 16
+    return (place == column).astype(BF)
+
+
+def into_vmem(array):
+    rows, width = array.shape
+    cut = 4
+
+    def kernel(source, target, sems):
+        copies = [
+            pltpu.make_async_copy(
+                source.at[pl.ds(i * rows // cut, rows // cut)],
+                target.at[pl.ds(i * rows // cut, rows // cut)],
+                sems.at[i],
+            )
+            for i in range(cut)
+        ]
+        for copy in copies:
+            copy.start()
+        for copy in copies:
+            copy.wait()
+
+    return pl.pallas_call(
+        kernel,
+        out_shape=jax.ShapeDtypeStruct(array.shape, array.dtype),
+        in_specs=[pl.BlockSpec(memory_space=pltpu.HBM)],
+        out_specs=pl.BlockSpec(memory_space=pltpu.VMEM),
+        scratch_shapes=[pltpu.SemaphoreType.DMA((cut,))],
+        compiler_params=pltpu.CompilerParams(vmem_limit_bytes=32 << 20),
+        cost_estimate=pl.CostEstimate(
+            flops=0, bytes_accessed=array.size * 2, transcendentals=0
+        ),
+        name="into_vmem",
+    )(array)
+
+
+def product(local, cot):
+    features, width = local.shape[1], cot.shape[1]
+    step = 256
+    count = width // step
+
+    def kernel(local_ref, cot_ref, out, held, sems):
+        left = local_ref[...].T
+        copies = []
+        for i in range(count):
+            at = pl.ds(i * step, step)
+            held[:, at] = matmul(left, cot_ref[:, at]).astype(BF)
+            copies.append(pltpu.make_async_copy(held.at[:, at], out.at[:, at], sems.at[i]))
+            copies[-1].start()
+        for copy in copies:
+            copy.wait()
+
+    return pl.pallas_call(
+        kernel,
+        out_shape=jax.ShapeDtypeStruct((features, width), BF),
+        in_specs=[pl.BlockSpec(memory_space=pltpu.VMEM)] * 2,
+        out_specs=pl.BlockSpec(memory_space=pltpu.HBM),
+        scratch_shapes=[
+            pltpu.VMEM((features, width), BF),
+            pltpu.SemaphoreType.DMA((count,)),
+        ],
+        compiler_params=pltpu.CompilerParams(vmem_limit_bytes=32 << 20),
+        name="product",
+    )(local, cot)
+
+
+def after(value, other):
+    return lax.optimization_barrier((value, other))[0]
+
+
+def halve(tokens, weight, to_half, to_quarter):
+    full = matmul(tokens, weight)
+    away = full[64:].astype(BF)
+    half = full[:64] + send(away, to_half)
+    return half[:32] + send(half[32:].astype(BF), to_quarter), away
 
 
 def scatter_second(quarter):
@@ -106,14 +196,15 @@
     return value.reshape(4, 4, 8, -1).swapaxes(0, 1).reshape(value.shape)
 
 
-def sum_rows(part, k):
+def sum_rows(part, factors, k):
     part = jnp.where(k == 0, part, swap_axes(part))
     mine = jnp.where(k == 0, part[:64], part[64:])
     other = jnp.where(k == 0, part[64:], part[:64])
     mine = mine + send(other, CORE)
     rounded = mine.astype(BF)
     got = [send(rounded, z_shift(d)) for d in (1, 2, 3)]
-    return mine + got[0] + got[1] + got[2]
+    factors = gather_second(after(factors, rounded))
+    return mine + got[0] + got[1] + got[2], factors[0], factors[1]
 
 
 def join_halves(half, k):
@@ -126,32 +217,39 @@
     row, col = lax.axis_index("row"), lax.axis_index("col")
     z, k, y, x = row // 2, row % 2, col // 4, col % 4
     out_scale = 128.0 ** (-0.5)
-    gathered = gather_tokens(tokens, z, k)
-    order = row_order(z, k, x, y)
-    picked = (order[:, None] == jnp.arange(128)[None, :]).astype(BF)
-    local = matmul(picked, gathered).astype(BF)
-
-    def hidden_sums(left, right):
-        full = jnp.stack([matmul(local, left), matmul(local, right)])
-        return scatter_second(scatter_first(full))
-
-    gate_sum, up_sum = hidden_sums(gate_weight, up_weight)
-    gate_dir, up_dir = hidden_sums(gate_tangent, up_tangent)
+    gate_weight = into_vmem(gate_weight)
+    own, other = gather_tokens(tokens, gate_weight)
+    turn = 1 - 2 * (jnp.where(k == 0, x, y) & 1)
+
+    def ordered(*offsets):
+        picked = order_matrix(offsets, z, k, x, y)
+        return (matmul(picked[:, :64], own) + matmul(picked[:, 64:], other)).astype(BF)
+
+    ahead, behind = ordered(0, -turn, turn, 2), ordered(0, turn, -turn, 2)
+    local = ordered(0, 1, 2, 3)
+    near_far = along_first(near), along_first(far)
+    far_near = along_first(far), along_first(near)
+    gate_sum, sent = halve(ahead, gate_weight, *near_far)
+    up_sum, sent = halve(after(behind, sent), up_weight, *far_near)
+    gate_dir, sent = halve(after(ahead, sent), gate_tangent, *near_far)
+    up_dir, sent = halve(after(behind, sent), up_tangent, *far_near)
+    gate_sum, up_sum, gate_dir, up_dir = scatter_second(
+        jnp.stack([gate_sum, up_sum, gate_dir, up_dir])
+    )
     sigmoid = jax.nn.sigmoid(gate_sum)
     activated = gate_sum * sigmoid
     up_slopes = up_sum * (sigmoid * (1.0 + gate_sum * (1.0 - sigmoid)))
     hidden = (up_slopes * gate_dir + activated * up_dir).astype(BF)
 
-    hidden, activated, up_slopes = gather_second(
-        jnp.stack([hidden, activated.astype(BF), up_slopes.astype(BF)])
-    )
-    hidden = gather_first(hidden[None])[0]
-    half = sum_rows(matmul(hidden, down_weight), k)
+    hidden = gather_first(gather_second(hidden[None]))[0]
+    half, up_slopes, activated = sum_rows(
+        matmul(hidden, down_weight), jnp.stack([up_slopes, activated]).astype(BF), k
+    )
     output_dir = join_halves((half * out_scale).astype(BF), k)
     back = sum_second(scatter_first(against_rows(output_dir, down_weight)[None])[0])
     gate_cot = gather_first((back * up_slopes).astype(BF)[None])[0]
     up_cot = gather_first((back * activated).astype(BF)[None])[0]
-    return transposed(local, gate_cot).astype(BF), transposed(local, up_cot).astype(BF)
+    return product(local, gate_cot), product(local, up_cot)
 
 
 def solution(mesh):

time: 134 us -> 122 us (0.910)
  matrix products: 12.3 us -> 5.49 us
  starting transfers between devices: 61.6 us -> 55.9 us
  Pallas kernels: 0 us -> 4.91 us
  waiting for transfers between devices: 51.9 us -> 47.9 us
    ppermute x39 -> x41, starting transfers between devices: 61.6 us -> 55.9 us  [send(): return lax.ppermute(value, RC, to)]
    dot_general x2 -> x0, matrix products: 5.64 us -> none  [transposed(): lax.dot_general(left, right, (((0,), (0,)), ((), ())), preferred_element_...]
    pallas_call x0 -> x3, Pallas kernels: none -> 4.91 us  [the longest x2 4.33 us: product(): pl.pallas_call(kernel, out_shape=jax.ShapeDtypeStruct((features, width),...]
    ppermute x39 -> x41, waiting for transfers between devices: 51.9 us -> 47.9 us  [send(): return lax.ppermute(value, RC, to)]
    dot_general x6 -> x11, matrix products: 5.42 us -> 4.26 us  [matmul(): return jnp.dot(left, right, preferred_element_type=F32)]
    unnamed x11 -> x20, local copies, waits for them, and re-layouts: 1.74 us -> 2.85 us
  transfers between devices with their start and end apart: 39 -> 41, of which waited for: 26 -> 25; matrix products, arithmetic and copies ran while one was open for 6% -> 5% of each run, Pallas kernels for 0% -> 2%
where the time goes in v3:
time: 122 us; the launch traced here: 121 us
  starting transfers between devices  55.9 us (46%)
  waiting for transfers between devices  47.9 us (39%)
  matrix products  5.49 us (4%)
  Pallas kernels  4.91 us (4%)
  local copies, waits for them, and re-layouts  3.33 us (3%)
  other arithmetic  2.29 us (2%)
  between operations  1.49 us (1%)
    ppermute x41, starting transfers between devices, send(): return lax.ppermute(value, RC, to)  55.9 us
    ppermute x41, waiting for transfers between devices, send(): return lax.ppermute(value, RC, to)  47.9 us
    pallas_call x2, Pallas kernels, product(): pl.pallas_call(kernel, out_shape=jax.ShapeDtypeStruct((features, width),...  4.33 us
    dot_general x11, matrix products, matmul(): return jnp.dot(left, right, preferred_element_type=F32)  4.26 us
    unnamed x20, local copies, waits for them, and re-layouts  2.85 us
  transfers between devices with their start and end apart: 41, of which 25 were waited for; matrix products, arithmetic and copies ran while one was open for 5% of the time, Pallas kernels for 2%

profile of v3, /device:TPU:0, one launch (start us, length us, event | category | flops | bytes accessed | tf_op | source)
XLA Modules:
  0.0 121.4 jit_solution(1792019929408145088)
XLA Ops:
  0.6 4.0 %collective-permute-start.1 = (bf16[16,512]{1,0:T(8,128)(2,1)}, bf16[16,512]{1,0:T(8,128)(2,1)S(1)}, u32[]{:S(2)}, u32[]{:S(2)}) collective-permute-start(bf16[16,512]{1,0:T(8,128)(2,1)} %param.6), channel_id=1, source_target_pairs={{0,64},{1,65},{2,66},{3,67},{4,68},{5,69},{6,70},{7,71},{8,72},{9,... | collective-permute-start | bytes 49160 | tf_op jit(solution)/shard_map/ppermute | solution.py:59
  5.7 2.2 %collective-permute-start.2 = (bf16[16,512]{1,0:T(8,128)(2,1)}, bf16[16,512]{1,0:T(8,128)(2,1)S(1)}, u32[]{:S(2)}, u32[]{:S(2)}) collective-permute-start(bf16[16,512]{1,0:T(8,128)(2,1)} %param.6), channel_id=1, source_target_pairs={{0,96},{1,97},{2,98},{3,99},{4,100},{5,101},{6,102},{7,103},{8,104... | collective-permute-start | bytes 49160 | tf_op jit(solution)/shard_map/ppermute | solution.py:59
  8.6 2.0 %copy-done.1 = bf16[512,3328]{1,0:T(8,128)(2,1)S(1)} copy-done((bf16[512,3328]{1,0:T(8,128)(2,1)S(1)}, bf16[512,3328]{1,0:T(8,128)(2,1)}, u32[]{:S(2)}) %copy-start.1) | copy-done | bytes 3407896
  16.0 2.3 %collective-permute-start.6 = (bf16[64,3328]{1,0:T(8,128)(2,1)S(1)}, bf16[64,3328]{1,0:T(8,128)(2,1)S(1)}, u32[]{:S(2)}, u32[]{:S(2)}) collective-permute-start(bf16[64,3328]{1,0:T(8,128)(2,1)S(1)} %slice.286), channel_id=1, source_target_pairs={{0,3},{1,2},{2,1},{3,0},{4,7},{5,6},{6,5},{7,4},{8,11},{9,10},{10,... | collective-permute-start | bytes 1277960 | tf_op jit(solution)/shard_map/ppermute | solution.py:59
  22.6 2.1 %collective-permute-start.5 = (bf16[32,3328]{1,0:T(8,128)(2,1)S(1)}, bf16[32,3328]{1,0:T(8,128)(2,1)S(1)}, u32[]{:S(2)}, u32[]{:S(2)}) collective-permute-start(bf16[32,3328]{1,0:T(8,128)(2,1)S(1)} %slice.291), channel_id=1, source_target_pairs={{0,3},{1,2},{2,1},{3,0},{4,7},{5,6},{6,5},{7,4},{8,11},{9,10},{10,... | collective-permute-start | bytes 638984 | tf_op jit(solution)/shard_map/ppermute | solution.py:59
  27.3 1.9 %collective-permute-start.9 = (bf16[32,3328]{1,0:T(8,128)(2,1)S(1)}, bf16[32,3328]{1,0:T(8,128)(2,1)S(1)}, u32[]{:S(2)}, u32[]{:S(2)}) collective-permute-start(bf16[32,3328]{1,0:T(8,128)(2,1)S(1)} %slice.289), channel_id=1, source_target_pairs={{0,3},{1,2},{2,1},{3,0},{4,7},{5,6},{6,5},{7,4},{8,11},{9,10},{10,... | collective-permute-start | bytes 638984 | tf_op jit(solution)/shard_map/ppermute | solution.py:59
  30.5 2.1 %collective-permute-done.5 = bf16[32,3328]{1,0:T(8,128)(2,1)S(1)} collective-permute-done((bf16[32,3328]{1,0:T(8,128)(2,1)S(1)}, bf16[32,3328]{1,0:T(8,128)(2,1)S(1)}, u32[]{:S(2)}, u32[]{:S(2)}) %collective-permute-start.5) | collective-permute-done | bytes 213024 | tf_op jit(solution)/shard_map/ppermute | solution.py:59
  32.7 2.2 %collective-permute-done.9 = bf16[32,3328]{1,0:T(8,128)(2,1)S(1)} collective-permute-done((bf16[32,3328]{1,0:T(8,128)(2,1)S(1)}, bf16[32,3328]{1,0:T(8,128)(2,1)S(1)}, u32[]{:S(2)}, u32[]{:S(2)}) %collective-permute-start.9) | collective-permute-done | bytes 213024 | tf_op jit(solution)/shard_map/ppermute | solution.py:59
  36.7 3.3 %collective-permute-start.12 = (bf16[4,8,3328]{2,1,0:T(8,128)(2,1)S(1)}, bf16[4,8,3328]{2,1,0:T(8,128)(2,1)S(1)}, u32[]{:S(2)}, u32[]{:S(2)}) collective-permute-start(bf16[4,8,3328]{2,1,0:T(8,128)(2,1)S(1)} %get-tuple-element.21), channel_id=1, source_target_pairs={{0,8},{1,9},{2,10},{3,11},{4,12},{5,13},{6,14},{7,15},{8,0},{9,1},... | collective-permute-start | bytes 638984 | tf_op jit(solution)/shard_map/ppermute | solution.py:59
  42.1 2.0 %collective-permute-done.12 = bf16[4,8,3328]{2,1,0:T(8,128)(2,1)S(1)} collective-permute-done((bf16[4,8,3328]{2,1,0:T(8,128)(2,1)S(1)}, bf16[4,8,3328]{2,1,0:T(8,128)(2,1)S(1)}, u32[]{:S(2)}, u32[]{:S(2)}) %collective-permute-start.12) | collective-permute-done | bytes 213024 | tf_op jit(solution)/shard_map/ppermute | solution.py:59
  44.1 2.6 %collective-permute-done.14 = bf16[4,8,3328]{2,1,0:T(8,128)(2,1)S(1)} collective-permute-done((bf16[4,8,3328]{2,1,0:T(8,128)(2,1)S(1)}, bf16[4,8,3328]{2,1,0:T(8,128)(2,1)S(1)}, u32[]{:S(2)}, u32[]{:S(2)}) %collective-permute-start.14) | collective-permute-done | bytes 213024 | tf_op jit(solution)/shard_map/ppermute | solution.py:59
  48.3 2.8 %collective-permute-start.16 = (bf16[1,8,3328]{2,1,0:T(8,128)(2,1)S(1)}, bf16[1,8,3328]{2,1,0:T(8,128)(2,1)S(1)}, u32[]{:S(2)}, u32[]{:S(2)}) collective-permute-start(bf16[1,8,3328]{2,1,0:T(8,128)(2,1)S(1)} %get-tuple-element.17), channel_id=1, source_target_pairs={{0,8},{1,9},{2,10},{3,11},{4,12},{5,13},{6,14},{7,15},{8,0},{9,1},... | collective-permute-start | bytes 159752 | tf_op jit(solution)/shard_map/ppermute | solution.py:59
  52.5 1.7 %collective-permute-done.17 = bf16[1,8,3328]{2,1,0:T(8,128)(2,1)S(1)} collective-permute-done((bf16[1,8,3328]{2,1,0:T(8,128)(2,1)S(1)}, bf16[1,8,3328]{2,1,0:T(8,128)(2,1)S(1)}, u32[]{:S(2)}, u32[]{:S(2)}) %collective-permute-start.17) | collective-permute-done | bytes 53280 | tf_op jit(solution)/shard_map/ppermute | solution.py:59
  55.6 3.0 %collective-permute-start.19 = (bf16[1,32,3328]{2,1,0:T(8,128)(2,1)S(1)}, bf16[1,32,3328]{2,1,0:T(8,128)(2,1)S(1)}, u32[]{:S(2)}, u32[]{:S(2)}) collective-permute-start(bf16[1,32,3328]{2,1,0:T(8,128)(2,1)S(1)} %pad_maximum_fusion.1), channel_id=1, source_target_pairs={{0,2},{1,3},{2,0},{3,1},{4,6},{5,7},{6,4},{7,5},{8,10},{9,11},{10,... | collective-permute-start | bytes 638984 | tf_op jit(solution)/shard_map/ppermute | solution.py:59
  59.3 6.6 %collective-permute-done.18 = bf16[1,32,3328]{2,1,0:T(8,128)(2,1)S(1)} collective-permute-done((bf16[1,32,3328]{2,1,0:T(8,128)(2,1)S(1)}, bf16[1,32,3328]{2,1,0:T(8,128)(2,1)S(1)}, u32[]{:S(2)}, u32[]{:S(2)}) %collective-permute-start.18) | collective-permute-done | bytes 213024 | tf_op jit(solution)/shard_map/ppermute | solution.py:59
  68.1 1.9 %collective-permute-start.24 = (bf16[64,512]{1,0:T(8,128)(2,1)S(1)}, bf16[64,512]{1,0:T(8,128)(2,1)S(1)}, u32[]{:S(2)}, u32[]{:S(2)}) collective-permute-start(bf16[64,512]{1,0:T(8,128)(2,1)S(1)} %get-tuple-element.14), channel_id=1, source_target_pairs={{0,96},{1,97},{2,98},{3,99},{4,100},{5,101},{6,102},{7,103},{8,104... | collective-permute-start | bytes 196616 | tf_op jit(solution)/shard_map/ppermute | solution.py:59
  71.0 3.3 %collective-permute-start.34 = (bf16[2,8,3328]{2,1,0:T(8,128)(2,1)S(1)}, bf16[2,8,3328]{2,1,0:T(8,128)(2,1)S(1)}, u32[]{:S(2)}, u32[]{:S(2)}) collective-permute-start(bf16[2,8,3328]{2,1,0:T(8,128)(2,1)S(1)} %pad_maximum_fusion.2), channel_id=1, source_target_pairs={{0,4},{1,5},{2,6},{3,7},{4,8},{5,9},{6,10},{7,11},{8,12},{9,13},{1... | collective-permute-start | bytes 319496 | tf_op jit(solution)/shard_map/ppermute | solution.py:59
  74.8 2.3 %collective-permute-start.32 = (bf16[2,8,3328]{2,1,0:T(8,128)(2,1)S(1)}, bf16[2,8,3328]{2,1,0:T(8,128)(2,1)S(1)}, u32[]{:S(2)}, u32[]{:S(2)}) collective-permute-start(bf16[2,8,3328]{2,1,0:T(8,128)(2,1)S(1)} %pad_maximum_fusion.2), channel_id=1, source_target_pairs={{0,12},{1,13},{2,14},{3,15},{4,0},{5,1},{6,2},{7,3},{8,4},{9,5},{1... | collective-permute-start | bytes 319496 | tf_op jit(solution)/shard_map/ppermute | solution.py:59
  77.3 2.3 %collective-permute-done.32 = bf16[2,8,3328]{2,1,0:T(8,128)(2,1)S(1)} collective-permute-done((bf16[2,8,3328]{2,1,0:T(8,128)(2,1)S(1)}, bf16[2,8,3328]{2,1,0:T(8,128)(2,1)S(1)}, u32[]{:S(2)}, u32[]{:S(2)}) %collective-permute-start.32) | collective-permute-done | bytes 106528 | tf_op jit(solution)/shard_map/ppermute | solution.py:59
  82.3 2.1 %collective-permute-start.28 = (bf16[1,32,3328]{2,1,0:T(8,128)(2,1)S(1)}, bf16[1,32,3328]{2,1,0:T(8,128)(2,1)S(1)}, u32[]{:S(2)}, u32[]{:S(2)}) collective-permute-start(bf16[1,32,3328]{2,1,0:T(8,128)(2,1)S(1)} %get-tuple-element.19), channel_id=1, source_target_pairs={{0,3},{1,0},{2,1},{3,2},{4,7},{5,4},{6,5},{7,6},{8,11},{9,8},{10,9... | collective-permute-start | bytes 638984 | tf_op jit(solution)/shard_map/ppermute | solution.py:59
  84.6 3.8 %collective-permute-done.26 = bf16[1,32,3328]{2,1,0:T(8,128)(2,1)S(1)} collective-permute-done((bf16[1,32,3328]{2,1,0:T(8,128)(2,1)S(1)}, bf16[1,32,3328]{2,1,0:T(8,128)(2,1)S(1)}, u32[]{:S(2)}, u32[]{:S(2)}) %collective-permute-start.26) | collective-permute-done | bytes 213024 | tf_op jit(solution)/shard_map/ppermute | solution.py:59
  88.4 2.3 %collective-permute-done.28 = bf16[1,32,3328]{2,1,0:T(8,128)(2,1)S(1)} collective-permute-done((bf16[1,32,3328]{2,1,0:T(8,128)(2,1)S(1)}, bf16[1,32,3328]{2,1,0:T(8,128)(2,1)S(1)}, u32[]{:S(2)}, u32[]{:S(2)}) %collective-permute-start.28) | collective-permute-done | bytes 213024 | tf_op jit(solution)/shard_map/ppermute | solution.py:59
  91.5 2.9 %collective-permute-start.31 = (bf16[32,3328]{1,0:T(8,128)(2,1)S(1)}, bf16[32,3328]{1,0:T(8,128)(2,1)S(1)}, u32[]{:S(2)}, u32[]{:S(2)}) collective-permute-start(bf16[32,3328]{1,0:T(8,128)(2,1)S(1)} %convert_bitcast_fusion), channel_id=1, source_target_pairs={{0,12},{1,13},{2,14},{3,15},{4,0},{5,1},{6,2},{7,3},{8,4},{9,5},{1... | collective-permute-start | bytes 638984 | tf_op jit(solution)/shard_map/ppermute | solution.py:59
  94.5 1.7 %collective-permute-start.29 = (bf16[32,3328]{1,0:T(8,128)(2,1)S(1)}, bf16[32,3328]{1,0:T(8,128)(2,1)S(1)}, u32[]{:S(2)}, u32[]{:S(2)}) collective-permute-start(bf16[32,3328]{1,0:T(8,128)(2,1)S(1)} %convert_bitcast_fusion), channel_id=1, source_target_pairs={{0,8},{1,9},{2,10},{3,11},{4,12},{5,13},{6,14},{7,15},{8,0},{9,1},... | collective-permute-start | bytes 638984 | tf_op jit(solution)/shard_map/ppermute | solution.py:59
  96.2 1.6 %collective-permute-done.31 = bf16[32,3328]{1,0:T(8,128)(2,1)S(1)} collective-permute-done((bf16[32,3328]{1,0:T(8,128)(2,1)S(1)}, bf16[32,3328]{1,0:T(8,128)(2,1)S(1)}, u32[]{:S(2)}, u32[]{:S(2)}) %collective-permute-start.31) | collective-permute-done | bytes 213024 | tf_op jit(solution)/shard_map/ppermute | solution.py:59
  97.8 6.0 %collective-permute-done.30 = bf16[32,3328]{1,0:T(8,128)(2,1)S(1)} collective-permute-done((bf16[32,3328]{1,0:T(8,128)(2,1)S(1)}, bf16[32,3328]{1,0:T(8,128)(2,1)S(1)}, u32[]{:S(2)}, u32[]{:S(2)}) %collective-permute-start.30) | collective-permute-done | bytes 213024 | tf_op jit(solution)/shard_map/ppermute | solution.py:59
  104.2 3.7 %collective-permute-start.39 = (bf16[1,32,3328]{2,1,0:T(8,128)(2,1)S(1)}, bf16[1,32,3328]{2,1,0:T(8,128)(2,1)S(1)}, u32[]{:S(2)}, u32[]{:S(2)}) collective-permute-start(bf16[1,32,3328]{2,1,0:T(8,128)(2,1)S(1)} %get-tuple-element.12), channel_id=1, source_target_pairs={{0,2},{1,3},{2,0},{3,1},{4,6},{5,7},{6,4},{7,5},{8,10},{9,11},{10,... | collective-permute-start | bytes 638984 | tf_op jit(solution)/shard_map/ppermute | solution.py:59
  108.3 1.8 %collective-permute-start.37 = (bf16[1,32,3328]{2,1,0:T(8,128)(2,1)S(1)}, bf16[1,32,3328]{2,1,0:T(8,128)(2,1)S(1)}, u32[]{:S(2)}, u32[]{:S(2)}) collective-permute-start(bf16[1,32,3328]{2,1,0:T(8,128)(2,1)S(1)} %multiply_convert_fusion.1), channel_id=1, source_target_pairs={{0,1},{1,2},{2,3},{3,0},{4,5},{5,6},{6,7},{7,4},{8,9},{9,10},{10,1... | collective-permute-start | bytes 638984 | tf_op jit(solution)/shard_map/ppermute | solution.py:59
  111.3 1.9 %collective-permute-start.35 = (bf16[1,32,3328]{2,1,0:T(8,128)(2,1)S(1)}, bf16[1,32,3328]{2,1,0:T(8,128)(2,1)S(1)}, u32[]{:S(2)}, u32[]{:S(2)}) collective-permute-start(bf16[1,32,3328]{2,1,0:T(8,128)(2,1)S(1)} %multiply_convert_fusion.1), channel_id=1, source_target_pairs={{0,3},{1,0},{2,1},{3,2},{4,7},{5,4},{6,5},{7,6},{8,11},{9,8},{10,9... | collective-permute-start | bytes 638984 | tf_op jit(solution)/shard_map/ppermute | solution.py:59
  114.5 2.2 %product.3 = bf16[512,3328]{1,0:T(8,128)(2,1)} custom-call(bf16[128,512]{1,0:T(8,128)(2,1)S(1)} %fusion.local_ref, bf16[128,3328]{1,0:T(8,128)(2,1)S(1)} %maximum_bitcast_fusion.1.cot_ref), custom_call_target="tpu_custom_call" | custom-call | tf_op jit(solution)/shard_map/product/pallas_call | solution.py:143
  116.7 1.9 %collective-permute-done.36 = bf16[1,32,3328]{2,1,0:T(8,128)(2,1)S(1)} collective-permute-done((bf16[1,32,3328]{2,1,0:T(8,128)(2,1)S(1)}, bf16[1,32,3328]{2,1,0:T(8,128)(2,1)S(1)}, u32[]{:S(2)}, u32[]{:S(2)}) %collective-permute-start.36) | collective-permute-done | bytes 213024 | tf_op jit(solution)/shard_map/ppermute | solution.py:59
  119.0 2.2 %product.2 = bf16[512,3328]{1,0:T(8,128)(2,1)} custom-call(bf16[128,512]{1,0:T(8,128)(2,1)S(1)} %fusion.local_ref, bf16[128,3328]{1,0:T(8,128)(2,1)S(1)} %maximum_bitcast_fusion.cot_ref), custom_call_target="tpu_custom_call" | custom-call | tf_op jit(solution)/shard_map/product/pallas_call | solution.py:143
  (137 shorter events, 35.2 us)
Async XLA Ops:
  0.6 10.5 %collective-permute-start.1 = (bf16[16,512]{1,0:T(8,128)(2,1)}, bf16[16,512]{1,0:T(8,128)(2,1)S(1)}, u32[]{:S(2)}, u32[]{:S(2)}) collective-permute-start(bf16[16,512]{1,0:T(8,128)(2,1)} %param.6), channel_id=1, source_target_pairs={{0,64},{1,65},{2,66},{3,67},{4,68},{5,69},{6,70},{7,71},{8,72},{9,... | collective-permute-start | bytes 49160 | tf_op jit(solution)/shard_map/ppermute | solution.py:59
  4.7 6.5 %collective-permute-start = (bf16[16,512]{1,0:T(8,128)(2,1)}, bf16[16,512]{1,0:T(8,128)(2,1)S(1)}, u32[]{:S(2)}, u32[]{:S(2)}) collective-permute-start(bf16[16,512]{1,0:T(8,128)(2,1)} %param.6), channel_id=1, source_target_pairs={{0,32},{1,33},{2,34},{3,35},{4,36},{5,37},{6,38},{7,39},{8,40},{9,... | collective-permute-start | bytes 49160 | tf_op jit(solution)/shard_map/ppermute | solution.py:59
  13.5 9.0 %collective-permute-start.4 = (bf16[64,3328]{1,0:T(8,128)(2,1)S(1)}, bf16[64,3328]{1,0:T(8,128)(2,1)S(1)}, u32[]{:S(2)}, u32[]{:S(2)}) collective-permute-start(bf16[64,3328]{1,0:T(8,128)(2,1)S(1)} %slice.287), channel_id=1, source_target_pairs={{0,1},{1,0},{2,3},{3,2},{4,5},{5,4},{6,7},{7,6},{8,9},{9,8},{10,11... | collective-permute-start | bytes 1277960 | tf_op jit(solution)/shard_map/ppermute | solution.py:59
  16.0 9.4 %collective-permute-start.6 = (bf16[64,3328]{1,0:T(8,128)(2,1)S(1)}, bf16[64,3328]{1,0:T(8,128)(2,1)S(1)}, u32[]{:S(2)}, u32[]{:S(2)}) collective-permute-start(bf16[64,3328]{1,0:T(8,128)(2,1)S(1)} %slice.286), channel_id=1, source_target_pairs={{0,3},{1,2},{2,1},{3,0},{4,7},{5,6},{6,5},{7,4},{8,11},{9,10},{10,... | collective-permute-start | bytes 1277960 | tf_op jit(solution)/shard_map/ppermute | solution.py:59
  19.0 8.2 %collective-permute-start.8 = (bf16[64,3328]{1,0:T(8,128)(2,1)S(1)}, bf16[64,3328]{1,0:T(8,128)(2,1)S(1)}, u32[]{:S(2)}, u32[]{:S(2)}) collective-permute-start(bf16[64,3328]{1,0:T(8,128)(2,1)S(1)} %slice.285), channel_id=1, source_target_pairs={{0,1},{1,0},{2,3},{3,2},{4,5},{5,4},{6,7},{7,6},{8,9},{9,8},{10,11... | collective-permute-start | bytes 1277960 | tf_op jit(solution)/shard_map/ppermute | solution.py:59
  20.9 9.4 %collective-permute-start.10 = (bf16[64,3328]{1,0:T(8,128)(2,1)S(1)}, bf16[64,3328]{1,0:T(8,128)(2,1)S(1)}, u32[]{:S(2)}, u32[]{:S(2)}) collective-permute-start(bf16[64,3328]{1,0:T(8,128)(2,1)S(1)} %slice.284), channel_id=1, source_target_pairs={{0,3},{1,2},{2,1},{3,0},{4,7},{5,6},{6,5},{7,4},{8,11},{9,10},{10,... | collective-permute-start | bytes 1277960 | tf_op jit(solution)/shard_map/ppermute | solution.py:59
  22.6 10.1 %collective-permute-start.5 = (bf16[32,3328]{1,0:T(8,128)(2,1)S(1)}, bf16[32,3328]{1,0:T(8,128)(2,1)S(1)}, u32[]{:S(2)}, u32[]{:S(2)}) collective-permute-start(bf16[32,3328]{1,0:T(8,128)(2,1)S(1)} %slice.291), channel_id=1, source_target_pairs={{0,3},{1,2},{2,1},{3,0},{4,7},{5,6},{6,5},{7,4},{8,11},{9,10},{10,... | collective-permute-start | bytes 638984 | tf_op jit(solution)/shard_map/ppermute | solution.py:59
  25.5 7.2 %collective-permute-start.7 = (bf16[32,3328]{1,0:T(8,128)(2,1)S(1)}, bf16[32,3328]{1,0:T(8,128)(2,1)S(1)}, u32[]{:S(2)}, u32[]{:S(2)}) collective-permute-start(bf16[32,3328]{1,0:T(8,128)(2,1)S(1)} %slice.290), channel_id=1, source_target_pairs={{0,1},{1,0},{2,3},{3,2},{4,5},{5,4},{6,7},{7,6},{8,9},{9,8},{10,11... | collective-permute-start | bytes 638984 | tf_op jit(solution)/shard_map/ppermute | solution.py:59
  27.3 7.6 %collective-permute-start.9 = (bf16[32,3328]{1,0:T(8,128)(2,1)S(1)}, bf16[32,3328]{1,0:T(8,128)(2,1)S(1)}, u32[]{:S(2)}, u32[]{:S(2)}) collective-permute-start(bf16[32,3328]{1,0:T(8,128)(2,1)S(1)} %slice.289), channel_id=1, source_target_pairs={{0,3},{1,2},{2,1},{3,0},{4,7},{5,6},{6,5},{7,4},{8,11},{9,10},{10,... | collective-permute-start | bytes 638984 | tf_op jit(solution)/shard_map/ppermute | solution.py:59
  36.7 7.4 %collective-permute-start.12 = (bf16[4,8,3328]{2,1,0:T(8,128)(2,1)S(1)}, bf16[4,8,3328]{2,1,0:T(8,128)(2,1)S(1)}, u32[]{:S(2)}, u32[]{:S(2)}) collective-permute-start(bf16[4,8,3328]{2,1,0:T(8,128)(2,1)S(1)} %get-tuple-element.21), channel_id=1, source_target_pairs={{0,8},{1,9},{2,10},{3,11},{4,12},{5,13},{6,14},{7,15},{8,0},{9,1},... | collective-permute-start | bytes 638984 | tf_op jit(solution)/shard_map/ppermute | solution.py:59
  39.9 6.8 %collective-permute-start.14 = (bf16[4,8,3328]{2,1,0:T(8,128)(2,1)S(1)}, bf16[4,8,3328]{2,1,0:T(8,128)(2,1)S(1)}, u32[]{:S(2)}, u32[]{:S(2)}) collective-permute-start(bf16[4,8,3328]{2,1,0:T(8,128)(2,1)S(1)} %get-tuple-element.22), channel_id=1, source_target_pairs={{0,12},{1,13},{2,14},{3,15},{4,0},{5,1},{6,2},{7,3},{8,4},{9,5},{1... | collective-permute-start | bytes 638984 | tf_op jit(solution)/shard_map/ppermute | solution.py:59
  41.0 7.1 %collective-permute-start.13 = (bf16[4,8,3328]{2,1,0:T(8,128)(2,1)S(1)}, bf16[4,8,3328]{2,1,0:T(8,128)(2,1)S(1)}, u32[]{:S(2)}, u32[]{:S(2)}) collective-permute-start(bf16[4,8,3328]{2,1,0:T(8,128)(2,1)S(1)} %get-tuple-element.23), channel_id=1, source_target_pairs={{0,4},{1,5},{2,6},{3,7},{4,8},{5,9},{6,10},{7,11},{8,12},{9,13},{1... | collective-permute-start | bytes 638984 | tf_op jit(solution)/shard_map/ppermute | solution.py:59
  55.6 10.4 %collective-permute-start.20 = (bf16[1,32,3328]{2,1,0:T(8,128)(2,1)S(1)}, bf16[1,32,3328]{2,1,0:T(8,128)(2,1)S(1)}, u32[]{:S(2)}, u32[]{:S(2)}) collective-permute-start(bf16[1,32,3328]{2,1,0:T(8,128)(2,1)S(1)} %pad_maximum_fusion.1), channel_id=1, source_target_pairs={{0,1},{1,2},{2,3},{3,0},{4,5},{5,6},{6,7},{7,4},{8,9},{9,10},{10,1... | collective-permute-start | bytes 638984 | tf_op jit(solution)/shard_map/ppermute | solution.py:59
  55.6 10.2 %collective-permute-start.19 = (bf16[1,32,3328]{2,1,0:T(8,128)(2,1)S(1)}, bf16[1,32,3328]{2,1,0:T(8,128)(2,1)S(1)}, u32[]{:S(2)}, u32[]{:S(2)}) collective-permute-start(bf16[1,32,3328]{2,1,0:T(8,128)(2,1)S(1)} %pad_maximum_fusion.1), channel_id=1, source_target_pairs={{0,2},{1,3},{2,0},{3,1},{4,6},{5,7},{6,4},{7,5},{8,10},{9,11},{10,... | collective-permute-start | bytes 638984 | tf_op jit(solution)/shard_map/ppermute | solution.py:59
  58.6 7.3 %collective-permute-start.18 = (bf16[1,32,3328]{2,1,0:T(8,128)(2,1)S(1)}, bf16[1,32,3328]{2,1,0:T(8,128)(2,1)S(1)}, u32[]{:S(2)}, u32[]{:S(2)}) collective-permute-start(bf16[1,32,3328]{2,1,0:T(8,128)(2,1)S(1)} %pad_maximum_fusion.1), channel_id=1, source_target_pairs={{0,3},{1,0},{2,1},{3,2},{4,7},{5,4},{6,5},{7,6},{8,11},{9,8},{10,9... | collective-permute-start | bytes 638984 | tf_op jit(solution)/shard_map/ppermute | solution.py:59
  68.1 6.6 %collective-permute-start.24 = (bf16[64,512]{1,0:T(8,128)(2,1)S(1)}, bf16[64,512]{1,0:T(8,128)(2,1)S(1)}, u32[]{:S(2)}, u32[]{:S(2)}) collective-permute-start(bf16[64,512]{1,0:T(8,128)(2,1)S(1)} %get-tuple-element.14), channel_id=1, source_target_pairs={{0,96},{1,97},{2,98},{3,99},{4,100},{5,101},{6,102},{7,103},{8,104... | collective-permute-start | bytes 196616 | tf_op jit(solution)/shard_map/ppermute | solution.py:59
  70.1 7.0 %collective-permute-start.23 = (bf16[64,512]{1,0:T(8,128)(2,1)S(1)}, bf16[64,512]{1,0:T(8,128)(2,1)S(1)}, u32[]{:S(2)}, u32[]{:S(2)}) collective-permute-start(bf16[64,512]{1,0:T(8,128)(2,1)S(1)} %get-tuple-element.14), channel_id=1, source_target_pairs={{0,64},{1,65},{2,66},{3,67},{4,68},{5,69},{6,70},{7,71},{8,72},{9,... | collective-permute-start | bytes 196616 | tf_op jit(solution)/shard_map/ppermute | solution.py:59
  70.1 7.0 %collective-permute-start.22 = (bf16[64,512]{1,0:T(8,128)(2,1)S(1)}, bf16[64,512]{1,0:T(8,128)(2,1)S(1)}, u32[]{:S(2)}, u32[]{:S(2)}) collective-permute-start(bf16[64,512]{1,0:T(8,128)(2,1)S(1)} %get-tuple-element.14), channel_id=1, source_target_pairs={{0,32},{1,33},{2,34},{3,35},{4,36},{5,37},{6,38},{7,39},{8,40},{9,... | collective-permute-start | bytes 196616 | tf_op jit(solution)/shard_map/ppermute | solution.py:59
  71.0 23.4 %collective-permute-start.34 = (bf16[2,8,3328]{2,1,0:T(8,128)(2,1)S(1)}, bf16[2,8,3328]{2,1,0:T(8,128)(2,1)S(1)}, u32[]{:S(2)}, u32[]{:S(2)}) collective-permute-start(bf16[2,8,3328]{2,1,0:T(8,128)(2,1)S(1)} %pad_maximum_fusion.2), channel_id=1, source_target_pairs={{0,4},{1,5},{2,6},{3,7},{4,8},{5,9},{6,10},{7,11},{8,12},{9,13},{1... | collective-permute-start | bytes 319496 | tf_op jit(solution)/shard_map/ppermute | solution.py:59
  74.4 10.2 %collective-permute-start.33 = (bf16[2,8,3328]{2,1,0:T(8,128)(2,1)S(1)}, bf16[2,8,3328]{2,1,0:T(8,128)(2,1)S(1)}, u32[]{:S(2)}, u32[]{:S(2)}) collective-permute-start(bf16[2,8,3328]{2,1,0:T(8,128)(2,1)S(1)} %pad_maximum_fusion.2), channel_id=1, source_target_pairs={{0,8},{1,9},{2,10},{3,11},{4,12},{5,13},{6,14},{7,15},{8,0},{9,1},... | collective-permute-start | bytes 319496 | tf_op jit(solution)/shard_map/ppermute | solution.py:59
  81.0 7.4 %collective-permute-start.26 = (bf16[1,32,3328]{2,1,0:T(8,128)(2,1)S(1)}, bf16[1,32,3328]{2,1,0:T(8,128)(2,1)S(1)}, u32[]{:S(2)}, u32[]{:S(2)}) collective-permute-start(bf16[1,32,3328]{2,1,0:T(8,128)(2,1)S(1)} %get-tuple-element.18), channel_id=1, source_target_pairs={{0,2},{1,3},{2,0},{3,1},{4,6},{5,7},{6,4},{7,5},{8,10},{9,11},{10,... | collective-permute-start | bytes 638984 | tf_op jit(solution)/shard_map/ppermute | solution.py:59
  82.3 8.4 %collective-permute-start.28 = (bf16[1,32,3328]{2,1,0:T(8,128)(2,1)S(1)}, bf16[1,32,3328]{2,1,0:T(8,128)(2,1)S(1)}, u32[]{:S(2)}, u32[]{:S(2)}) collective-permute-start(bf16[1,32,3328]{2,1,0:T(8,128)(2,1)S(1)} %get-tuple-element.19), channel_id=1, source_target_pairs={{0,3},{1,0},{2,1},{3,2},{4,7},{5,4},{6,5},{7,6},{8,11},{9,8},{10,9... | collective-permute-start | bytes 638984 | tf_op jit(solution)/shard_map/ppermute | solution.py:59
  84.4 7.1 %collective-permute-start.27 = (bf16[1,32,3328]{2,1,0:T(8,128)(2,1)S(1)}, bf16[1,32,3328]{2,1,0:T(8,128)(2,1)S(1)}, u32[]{:S(2)}, u32[]{:S(2)}) collective-permute-start(bf16[1,32,3328]{2,1,0:T(8,128)(2,1)S(1)} %get-tuple-element.20), channel_id=1, source_target_pairs={{0,1},{1,2},{2,3},{3,0},{4,5},{5,6},{6,7},{7,4},{8,9},{9,10},{10,1... | collective-permute-start | bytes 638984 | tf_op jit(solution)/shard_map/ppermute | solution.py:59
  91.5 6.3 %collective-permute-start.31 = (bf16[32,3328]{1,0:T(8,128)(2,1)S(1)}, bf16[32,3328]{1,0:T(8,128)(2,1)S(1)}, u32[]{:S(2)}, u32[]{:S(2)}) collective-permute-start(bf16[32,3328]{1,0:T(8,128)(2,1)S(1)} %convert_bitcast_fusion), channel_id=1, source_target_pairs={{0,12},{1,13},{2,14},{3,15},{4,0},{5,1},{6,2},{7,3},{8,4},{9,5},{1... | collective-permute-start | bytes 638984 | tf_op jit(solution)/shard_map/ppermute | solution.py:59
  94.4 9.4 %collective-permute-start.30 = (bf16[32,3328]{1,0:T(8,128)(2,1)S(1)}, bf16[32,3328]{1,0:T(8,128)(2,1)S(1)}, u32[]{:S(2)}, u32[]{:S(2)}) collective-permute-start(bf16[32,3328]{1,0:T(8,128)(2,1)S(1)} %convert_bitcast_fusion), channel_id=1, source_target_pairs={{0,4},{1,5},{2,6},{3,7},{4,8},{5,9},{6,10},{7,11},{8,12},{9,13},{1... | collective-permute-start | bytes 638984 | tf_op jit(solution)/shard_map/ppermute | solution.py:59
  94.5 9.4 %collective-permute-start.29 = (bf16[32,3328]{1,0:T(8,128)(2,1)S(1)}, bf16[32,3328]{1,0:T(8,128)(2,1)S(1)}, u32[]{:S(2)}, u32[]{:S(2)}) collective-permute-start(bf16[32,3328]{1,0:T(8,128)(2,1)S(1)} %convert_bitcast_fusion), channel_id=1, source_target_pairs={{0,8},{1,9},{2,10},{3,11},{4,12},{5,13},{6,14},{7,15},{8,0},{9,1},... | collective-permute-start | bytes 638984 | tf_op jit(solution)/shard_map/ppermute | solution.py:59
  104.1 7.1 %collective-permute-start.40 = (bf16[1,32,3328]{2,1,0:T(8,128)(2,1)S(1)}, bf16[1,32,3328]{2,1,0:T(8,128)(2,1)S(1)}, u32[]{:S(2)}, u32[]{:S(2)}) collective-permute-start(bf16[1,32,3328]{2,1,0:T(8,128)(2,1)S(1)} %get-tuple-element.12), channel_id=1, source_target_pairs={{0,1},{1,2},{2,3},{3,0},{4,5},{5,6},{6,7},{7,4},{8,9},{9,10},{10,1... | collective-permute-start | bytes 638984 | tf_op jit(solution)/shard_map/ppermute | solution.py:59
  104.2 9.9 %collective-permute-start.39 = (bf16[1,32,3328]{2,1,0:T(8,128)(2,1)S(1)}, bf16[1,32,3328]{2,1,0:T(8,128)(2,1)S(1)}, u32[]{:S(2)}, u32[]{:S(2)}) collective-permute-start(bf16[1,32,3328]{2,1,0:T(8,128)(2,1)S(1)} %get-tuple-element.12), channel_id=1, source_target_pairs={{0,2},{1,3},{2,0},{3,1},{4,6},{5,7},{6,4},{7,5},{8,10},{9,11},{10,... | collective-permute-start | bytes 638984 | tf_op jit(solution)/shard_map/ppermute | solution.py:59
  107.9 6.5 %collective-permute-start.38 = (bf16[1,32,3328]{2,1,0:T(8,128)(2,1)S(1)}, bf16[1,32,3328]{2,1,0:T(8,128)(2,1)S(1)}, u32[]{:S(2)}, u32[]{:S(2)}) collective-permute-start(bf16[1,32,3328]{2,1,0:T(8,128)(2,1)S(1)} %get-tuple-element.12), channel_id=1, source_target_pairs={{0,3},{1,0},{2,1},{3,2},{4,7},{5,4},{6,5},{7,6},{8,11},{9,8},{10,9... | collective-permute-start | bytes 638984 | tf_op jit(solution)/shard_map/ppermute | solution.py:59
  108.3 8.4 %collective-permute-start.37 = (bf16[1,32,3328]{2,1,0:T(8,128)(2,1)S(1)}, bf16[1,32,3328]{2,1,0:T(8,128)(2,1)S(1)}, u32[]{:S(2)}, u32[]{:S(2)}) collective-permute-start(bf16[1,32,3328]{2,1,0:T(8,128)(2,1)S(1)} %multiply_convert_fusion.1), channel_id=1, source_target_pairs={{0,1},{1,2},{2,3},{3,0},{4,5},{5,6},{6,7},{7,4},{8,9},{9,10},{10,1... | collective-permute-start | bytes 638984 | tf_op jit(solution)/shard_map/ppermute | solution.py:59
  110.1 8.5 %collective-permute-start.36 = (bf16[1,32,3328]{2,1,0:T(8,128)(2,1)S(1)}, bf16[1,32,3328]{2,1,0:T(8,128)(2,1)S(1)}, u32[]{:S(2)}, u32[]{:S(2)}) collective-permute-start(bf16[1,32,3328]{2,1,0:T(8,128)(2,1)S(1)} %multiply_convert_fusion.1), channel_id=1, source_target_pairs={{0,2},{1,3},{2,0},{3,1},{4,6},{5,7},{6,4},{7,5},{8,10},{9,11},{10,... | collective-permute-start | bytes 638984 | tf_op jit(solution)/shard_map/ppermute | solution.py:59
  111.3 7.7 %collective-permute-start.35 = (bf16[1,32,3328]{2,1,0:T(8,128)(2,1)S(1)}, bf16[1,32,3328]{2,1,0:T(8,128)(2,1)S(1)}, u32[]{:S(2)}, u32[]{:S(2)}) collective-permute-start(bf16[1,32,3328]{2,1,0:T(8,128)(2,1)S(1)} %multiply_convert_fusion.1), channel_id=1, source_target_pairs={{0,3},{1,0},{2,1},{3,2},{4,7},{5,4},{6,5},{7,6},{8,11},{9,8},{10,9... | collective-permute-start | bytes 638984 | tf_op jit(solution)/shard_map/ppermute | solution.py:59
  (15 other events, 113.0 us)

commit v4 on v3

--- a/solution.py
+++ b/solution.py
@@ -187,6 +187,14 @@
     return jnp.concatenate([own, got[1], got[2], got[3]], axis=1)
 
 
+def gather_second_pairs(own, next_, even):
+    both = send(jnp.concatenate([own, next_], axis=1), along_second(far))
+    before, across = both[:, :8], both[:, 8:]
+    return jnp.concatenate(
+        [own, jnp.where(even, next_, before), across, jnp.where(even, before, next_)], axis=1
+    )
+
+
 def gather_first(own):
     got = {d: send(own, first_shift(-d)) for d in (2, 1, 3)}
     return jnp.concatenate([own, got[1], got[2], got[3]], axis=1)
@@ -196,14 +204,14 @@
     return value.reshape(4, 4, 8, -1).swapaxes(0, 1).reshape(value.shape)
 
 
-def sum_rows(part, factors, k):
+def sum_rows(part, factors, next_, k, even):
     part = jnp.where(k == 0, part, swap_axes(part))
     mine = jnp.where(k == 0, part[:64], part[64:])
     other = jnp.where(k == 0, part[64:], part[:64])
     mine = mine + send(other, CORE)
     rounded = mine.astype(BF)
     got = [send(rounded, z_shift(d)) for d in (1, 2, 3)]
-    factors = gather_second(after(factors, rounded))
+    factors = gather_second_pairs(factors, after(next_, mine), even)
     return mine + got[0] + got[1] + got[2], factors[0], factors[1]
 
 
@@ -216,6 +224,7 @@
 def body(tokens, gate_weight, up_weight, down_weight, gate_tangent, up_tangent):
     row, col = lax.axis_index("row"), lax.axis_index("col")
     z, k, y, x = row // 2, row % 2, col // 4, col % 4
+    even = jnp.where(k == 0, y, x) & 1 == 0
     out_scale = 128.0 ** (-0.5)
     gate_weight = into_vmem(gate_weight)
     own, other = gather_tokens(tokens, gate_weight)
@@ -241,10 +250,11 @@
     up_slopes = up_sum * (sigmoid * (1.0 + gate_sum * (1.0 - sigmoid)))
     hidden = (up_slopes * gate_dir + activated * up_dir).astype(BF)
 
-    hidden = gather_first(gather_second(hidden[None]))[0]
-    half, up_slopes, activated = sum_rows(
-        matmul(hidden, down_weight), jnp.stack([up_slopes, activated]).astype(BF), k
-    )
+    factors = jnp.stack([up_slopes, activated]).astype(BF)
+    hidden = gather_second(hidden[None])
+    next_ = send(after(factors, hidden), along_second(near))
+    hidden = after(gather_first(hidden)[0], next_)
+    half, up_slopes, activated = sum_rows(matmul(hidden, down_weight), factors, next_, k, even)
     output_dir = join_halves((half * out_scale).astype(BF), k)
     back = sum_second(scatter_first(against_rows(output_dir, down_weight)[None])[0])
     gate_cot = gather_first((back * up_slopes).astype(BF)[None])[0]

time: 122 us -> 120 us (0.984)
  waiting for transfers between devices: 47.9 us -> 46.5 us
    ppermute x41 -> x40, waiting for transfers between devices: 47.9 us -> 46.5 us  [send(): return lax.ppermute(value, RC, to)]
    ppermute x41 -> x40, starting transfers between devices: 55.9 us -> 55.4 us  [send(): return lax.ppermute(value, RC, to)]
    unnamed x20 -> x17, local copies, waits for them, and re-layouts: 2.85 us -> 2.83 us
  transfers between devices with their start and end apart: 41 -> 40, of which waited for: 25 -> 28; matrix products, arithmetic and copies ran while one was open for 5% -> 5% of each run, Pallas kernels for 2% -> 2%
where the time goes in v4:
time: 120 us; the launch traced here: 119 us
  starting transfers between devices  55.4 us (46%)
  waiting for transfers between devices  46.5 us (39%)
  matrix products  5.5 us (5%)
  Pallas kernels  4.9 us (4%)
  local copies, waits for them, and re-layouts  3.29 us (3%)
  other arithmetic  2.37 us (2%)
  between operations  1.46 us (1%)
    ppermute x40, starting transfers between devices, send(): return lax.ppermute(value, RC, to)  55.4 us
    ppermute x40, waiting for transfers between devices, send(): return lax.ppermute(value, RC, to)  46.5 us
    pallas_call x2, Pallas kernels, product(): pl.pallas_call(kernel, out_shape=jax.ShapeDtypeStruct((features, width),...  4.31 us
    dot_general x11, matrix products, matmul(): return jnp.dot(left, right, preferred_element_type=F32)  4.27 us
    unnamed x17, local copies, waits for them, and re-layouts  2.83 us
  transfers between devices with their start and end apart: 40, of which 28 were waited for; matrix products, arithmetic and copies ran while one was open for 5% of the time, Pallas kernels for 2%

profile of v4, /device:TPU:0, one launch (start us, length us, event | category | flops | bytes accessed | tf_op | source)
XLA Modules:
  0.0 119.4 jit_solution(15409570215195591466)
XLA Ops:
  0.6 4.0 %collective-permute-start.1 = (bf16[16,512]{1,0:T(8,128)(2,1)}, bf16[16,512]{1,0:T(8,128)(2,1)S(1)}, u32[]{:S(2)}, u32[]{:S(2)}) collective-permute-start(bf16[16,512]{1,0:T(8,128)(2,1)} %param.6), channel_id=1, source_target_pairs={{0,64},{1,65},{2,66},{3,67},{4,68},{5,69},{6,70},{7,71},{8,72},{9,... | collective-permute-start | bytes 49160 | tf_op jit(solution)/shard_map/ppermute | solution.py:59
  5.7 2.2 %collective-permute-start.2 = (bf16[16,512]{1,0:T(8,128)(2,1)}, bf16[16,512]{1,0:T(8,128)(2,1)S(1)}, u32[]{:S(2)}, u32[]{:S(2)}) collective-permute-start(bf16[16,512]{1,0:T(8,128)(2,1)} %param.6), channel_id=1, source_target_pairs={{0,96},{1,97},{2,98},{3,99},{4,100},{5,101},{6,102},{7,103},{8,104... | collective-permute-start | bytes 49160 | tf_op jit(solution)/shard_map/ppermute | solution.py:59
  8.6 2.0 %copy-done.1 = bf16[512,3328]{1,0:T(8,128)(2,1)S(1)} copy-done((bf16[512,3328]{1,0:T(8,128)(2,1)S(1)}, bf16[512,3328]{1,0:T(8,128)(2,1)}, u32[]{:S(2)}) %copy-start.1) | copy-done | bytes 3407896
  16.0 2.3 %collective-permute-start.6 = (bf16[64,3328]{1,0:T(8,128)(2,1)S(1)}, bf16[64,3328]{1,0:T(8,128)(2,1)S(1)}, u32[]{:S(2)}, u32[]{:S(2)}) collective-permute-start(bf16[64,3328]{1,0:T(8,128)(2,1)S(1)} %slice.298), channel_id=1, source_target_pairs={{0,3},{1,2},{2,1},{3,0},{4,7},{5,6},{6,5},{7,4},{8,11},{9,10},{10,... | collective-permute-start | bytes 1277960 | tf_op jit(solution)/shard_map/ppermute | solution.py:59
  22.3 2.3 %collective-permute-start.5 = (bf16[32,3328]{1,0:T(8,128)(2,1)S(1)}, bf16[32,3328]{1,0:T(8,128)(2,1)S(1)}, u32[]{:S(2)}, u32[]{:S(2)}) collective-permute-start(bf16[32,3328]{1,0:T(8,128)(2,1)S(1)} %slice.303), channel_id=1, source_target_pairs={{0,3},{1,2},{2,1},{3,0},{4,7},{5,6},{6,5},{7,4},{8,11},{9,10},{10,... | collective-permute-start | bytes 638984 | tf_op jit(solution)/shard_map/ppermute | solution.py:59
  27.3 1.9 %collective-permute-start.9 = (bf16[32,3328]{1,0:T(8,128)(2,1)S(1)}, bf16[32,3328]{1,0:T(8,128)(2,1)S(1)}, u32[]{:S(2)}, u32[]{:S(2)}) collective-permute-start(bf16[32,3328]{1,0:T(8,128)(2,1)S(1)} %slice.301), channel_id=1, source_target_pairs={{0,3},{1,2},{2,1},{3,0},{4,7},{5,6},{6,5},{7,4},{8,11},{9,10},{10,... | collective-permute-start | bytes 638984 | tf_op jit(solution)/shard_map/ppermute | solution.py:59
  30.5 2.1 %collective-permute-done.5 = bf16[32,3328]{1,0:T(8,128)(2,1)S(1)} collective-permute-done((bf16[32,3328]{1,0:T(8,128)(2,1)S(1)}, bf16[32,3328]{1,0:T(8,128)(2,1)S(1)}, u32[]{:S(2)}, u32[]{:S(2)}) %collective-permute-start.5) | collective-permute-done | bytes 213024 | tf_op jit(solution)/shard_map/ppermute | solution.py:59
  32.7 2.2 %collective-permute-done.9 = bf16[32,3328]{1,0:T(8,128)(2,1)S(1)} collective-permute-done((bf16[32,3328]{1,0:T(8,128)(2,1)S(1)}, bf16[32,3328]{1,0:T(8,128)(2,1)S(1)}, u32[]{:S(2)}, u32[]{:S(2)}) %collective-permute-start.9) | collective-permute-done | bytes 213024 | tf_op jit(solution)/shard_map/ppermute | solution.py:59
  36.7 3.3 %collective-permute-start.12 = (bf16[4,8,3328]{2,1,0:T(8,128)(2,1)S(1)}, bf16[4,8,3328]{2,1,0:T(8,128)(2,1)S(1)}, u32[]{:S(2)}, u32[]{:S(2)}) collective-permute-start(bf16[4,8,3328]{2,1,0:T(8,128)(2,1)S(1)} %get-tuple-element.25), channel_id=1, source_target_pairs={{0,8},{1,9},{2,10},{3,11},{4,12},{5,13},{6,14},{7,15},{8,0},{9,1},... | collective-permute-start | bytes 638984 | tf_op jit(solution)/shard_map/ppermute | solution.py:59
  42.1 2.0 %collective-permute-done.12 = bf16[4,8,3328]{2,1,0:T(8,128)(2,1)S(1)} collective-permute-done((bf16[4,8,3328]{2,1,0:T(8,128)(2,1)S(1)}, bf16[4,8,3328]{2,1,0:T(8,128)(2,1)S(1)}, u32[]{:S(2)}, u32[]{:S(2)}) %collective-permute-start.12) | collective-permute-done | bytes 213024 | tf_op jit(solution)/shard_map/ppermute | solution.py:59
  44.1 2.6 %collective-permute-done.14 = bf16[4,8,3328]{2,1,0:T(8,128)(2,1)S(1)} collective-permute-done((bf16[4,8,3328]{2,1,0:T(8,128)(2,1)S(1)}, bf16[4,8,3328]{2,1,0:T(8,128)(2,1)S(1)}, u32[]{:S(2)}, u32[]{:S(2)}) %collective-permute-start.14) | collective-permute-done | bytes 213024 | tf_op jit(solution)/shard_map/ppermute | solution.py:59
  48.4 2.8 %collective-permute-start.16 = (bf16[1,8,3328]{2,1,0:T(8,128)(2,1)S(1)}, bf16[1,8,3328]{2,1,0:T(8,128)(2,1)S(1)}, u32[]{:S(2)}, u32[]{:S(2)}) collective-permute-start(bf16[1,8,3328]{2,1,0:T(8,128)(2,1)S(1)} %get-tuple-element.21), channel_id=1, source_target_pairs={{0,8},{1,9},{2,10},{3,11},{4,12},{5,13},{6,14},{7,15},{8,0},{9,1},... | collective-permute-start | bytes 159752 | tf_op jit(solution)/shard_map/ppermute | solution.py:59
  52.5 1.7 %collective-permute-done.17 = bf16[1,8,3328]{2,1,0:T(8,128)(2,1)S(1)} collective-permute-done((bf16[1,8,3328]{2,1,0:T(8,128)(2,1)S(1)}, bf16[1,8,3328]{2,1,0:T(8,128)(2,1)S(1)}, u32[]{:S(2)}, u32[]{:S(2)}) %collective-permute-start.17) | collective-permute-done | bytes 53280 | tf_op jit(solution)/shard_map/ppermute | solution.py:59
  55.7 3.0 %collective-permute-start.19 = (bf16[1,32,3328]{2,1,0:T(8,128)(2,1)S(1)}, bf16[1,32,3328]{2,1,0:T(8,128)(2,1)S(1)}, u32[]{:S(2)}, u32[]{:S(2)}) collective-permute-start(bf16[1,32,3328]{2,1,0:T(8,128)(2,1)S(1)} %pad_maximum_fusion.2), channel_id=1, source_target_pairs={{0,2},{1,3},{2,0},{3,1},{4,6},{5,7},{6,4},{7,5},{8,10},{9,11},{10,... | collective-permute-start | bytes 638984 | tf_op jit(solution)/shard_map/ppermute | solution.py:59
  59.3 3.0 %collective-permute-start.21 = (bf16[2,8,3328]{2,1,0:T(8,128)(2,1)S(1)}, bf16[2,8,3328]{2,1,0:T(8,128)(2,1)S(1)}, u32[]{:S(2)}, u32[]{:S(2)}) collective-permute-start(bf16[2,8,3328]{2,1,0:T(8,128)(2,1)S(1)} %pad_maximum_fusion.4), channel_id=1, source_target_pairs={{0,4},{1,5},{2,6},{3,7},{4,0},{5,1},{6,2},{7,3},{8,12},{9,13},{10,... | collective-permute-start | bytes 319496 | tf_op jit(solution)/shard_map/ppermute | solution.py:59
  62.3 3.6 %collective-permute-done.18 = bf16[1,32,3328]{2,1,0:T(8,128)(2,1)S(1)} collective-permute-done((bf16[1,32,3328]{2,1,0:T(8,128)(2,1)S(1)}, bf16[1,32,3328]{2,1,0:T(8,128)(2,1)S(1)}, u32[]{:S(2)}, u32[]{:S(2)}) %collective-permute-start.18) | collective-permute-done | bytes 213024 | tf_op jit(solution)/shard_map/ppermute | solution.py:59
  68.2 1.9 %collective-permute-start.25 = (bf16[64,512]{1,0:T(8,128)(2,1)S(1)}, bf16[64,512]{1,0:T(8,128)(2,1)S(1)}, u32[]{:S(2)}, u32[]{:S(2)}) collective-permute-start(bf16[64,512]{1,0:T(8,128)(2,1)S(1)} %get-tuple-element.18), channel_id=1, source_target_pairs={{0,96},{1,97},{2,98},{3,99},{4,100},{5,101},{6,102},{7,103},{8,104... | collective-permute-start | bytes 196616 | tf_op jit(solution)/shard_map/ppermute | solution.py:59
  71.4 1.9 %collective-permute-done.25 = bf16[64,512]{1,0:T(8,128)(2,1)S(1)} collective-permute-done((bf16[64,512]{1,0:T(8,128)(2,1)S(1)}, bf16[64,512]{1,0:T(8,128)(2,1)S(1)}, u32[]{:S(2)}, u32[]{:S(2)}) %collective-permute-start.25) | collective-permute-done | bytes 65568 | tf_op jit(solution)/shard_map/ppermute | solution.py:59
  73.3 3.0 %collective-permute-done.24 = bf16[64,512]{1,0:T(8,128)(2,1)S(1)} collective-permute-done((bf16[64,512]{1,0:T(8,128)(2,1)S(1)}, bf16[64,512]{1,0:T(8,128)(2,1)S(1)}, u32[]{:S(2)}, u32[]{:S(2)}) %collective-permute-start.24) | collective-permute-done | bytes 65568 | tf_op jit(solution)/shard_map/ppermute | solution.py:59
  76.8 2.3 %collective-permute-start.33 = (bf16[2,16,3328]{2,1,0:T(8,128)(2,1)S(1)}, bf16[2,16,3328]{2,1,0:T(8,128)(2,1)S(1)}, u32[]{:S(2)}, u32[]{:S(2)}) collective-permute-start(bf16[2,16,3328]{2,1,0:T(8,128)(2,1)S(1)} %pad_maximum_fusion.3), channel_id=1, source_target_pairs={{0,12},{1,13},{2,14},{3,15},{4,8},{5,9},{6,10},{7,11},{8,4},{9,5},... | collective-permute-start | bytes 638984 | tf_op jit(solution)/shard_map/ppermute | solution.py:59
  81.9 2.1 %collective-permute-start.29 = (bf16[1,32,3328]{2,1,0:T(8,128)(2,1)S(1)}, bf16[1,32,3328]{2,1,0:T(8,128)(2,1)S(1)}, u32[]{:S(2)}, u32[]{:S(2)}) collective-permute-start(bf16[1,32,3328]{2,1,0:T(8,128)(2,1)S(1)} %get-tuple-element.23), channel_id=1, source_target_pairs={{0,3},{1,0},{2,1},{3,2},{4,7},{5,4},{6,5},{7,6},{8,11},{9,8},{10,9... | collective-permute-start | bytes 638984 | tf_op jit(solution)/shard_map/ppermute | solution.py:59
  84.2 3.8 %collective-permute-done.27 = bf16[1,32,3328]{2,1,0:T(8,128)(2,1)S(1)} collective-permute-done((bf16[1,32,3328]{2,1,0:T(8,128)(2,1)S(1)}, bf16[1,32,3328]{2,1,0:T(8,128)(2,1)S(1)}, u32[]{:S(2)}, u32[]{:S(2)}) %collective-permute-start.27) | collective-permute-done | bytes 213024 | tf_op jit(solution)/shard_map/ppermute | solution.py:59
  88.0 2.3 %collective-permute-done.29 = bf16[1,32,3328]{2,1,0:T(8,128)(2,1)S(1)} collective-permute-done((bf16[1,32,3328]{2,1,0:T(8,128)(2,1)S(1)}, bf16[1,32,3328]{2,1,0:T(8,128)(2,1)S(1)}, u32[]{:S(2)}, u32[]{:S(2)}) %collective-permute-start.29) | collective-permute-done | bytes 213024 | tf_op jit(solution)/shard_map/ppermute | solution.py:59
  93.3 2.5 %collective-permute-start.30 = (bf16[32,3328]{1,0:T(8,128)(2,1)S(1)}, bf16[32,3328]{1,0:T(8,128)(2,1)S(1)}, u32[]{:S(2)}, u32[]{:S(2)}) collective-permute-start(bf16[32,3328]{1,0:T(8,128)(2,1)S(1)} %convert_bitcast_fusion), channel_id=1, source_target_pairs={{0,8},{1,9},{2,10},{3,11},{4,12},{5,13},{6,14},{7,15},{8,0},{9,1},... | collective-permute-start | bytes 638984 | tf_op jit(solution)/shard_map/ppermute | solution.py:59
  97.0 2.4 %collective-permute-done.31 = bf16[32,3328]{1,0:T(8,128)(2,1)S(1)} collective-permute-done((bf16[32,3328]{1,0:T(8,128)(2,1)S(1)}, bf16[32,3328]{1,0:T(8,128)(2,1)S(1)}, u32[]{:S(2)}, u32[]{:S(2)}) %collective-permute-start.31) | collective-permute-done | bytes 213024 | tf_op jit(solution)/shard_map/ppermute | solution.py:59
  99.5 2.4 %collective-permute-done.30 = bf16[32,3328]{1,0:T(8,128)(2,1)S(1)} collective-permute-done((bf16[32,3328]{1,0:T(8,128)(2,1)S(1)}, bf16[32,3328]{1,0:T(8,128)(2,1)S(1)}, u32[]{:S(2)}, u32[]{:S(2)}) %collective-permute-start.30) | collective-permute-done | bytes 213024 | tf_op jit(solution)/shard_map/ppermute | solution.py:59
  102.2 3.7 %collective-permute-start.38 = (bf16[1,32,3328]{2,1,0:T(8,128)(2,1)S(1)}, bf16[1,32,3328]{2,1,0:T(8,128)(2,1)S(1)}, u32[]{:S(2)}, u32[]{:S(2)}) collective-permute-start(bf16[1,32,3328]{2,1,0:T(8,128)(2,1)S(1)} %get-tuple-element.16), channel_id=1, source_target_pairs={{0,2},{1,3},{2,0},{3,1},{4,6},{5,7},{6,4},{7,5},{8,10},{9,11},{10,... | collective-permute-start | bytes 638984 | tf_op jit(solution)/shard_map/ppermute | solution.py:59
  106.3 1.8 %collective-permute-start.36 = (bf16[1,32,3328]{2,1,0:T(8,128)(2,1)S(1)}, bf16[1,32,3328]{2,1,0:T(8,128)(2,1)S(1)}, u32[]{:S(2)}, u32[]{:S(2)}) collective-permute-start(bf16[1,32,3328]{2,1,0:T(8,128)(2,1)S(1)} %multiply_convert_fusion.1), channel_id=1, source_target_pairs={{0,1},{1,2},{2,3},{3,0},{4,5},{5,6},{6,7},{7,4},{8,9},{9,10},{10,1... | collective-permute-start | bytes 638984 | tf_op jit(solution)/shard_map/ppermute | solution.py:59
  109.3 1.9 %collective-permute-start.34 = (bf16[1,32,3328]{2,1,0:T(8,128)(2,1)S(1)}, bf16[1,32,3328]{2,1,0:T(8,128)(2,1)S(1)}, u32[]{:S(2)}, u32[]{:S(2)}) collective-permute-start(bf16[1,32,3328]{2,1,0:T(8,128)(2,1)S(1)} %multiply_convert_fusion.1), channel_id=1, source_target_pairs={{0,3},{1,0},{2,1},{3,2},{4,7},{5,4},{6,5},{7,6},{8,11},{9,8},{10,9... | collective-permute-start | bytes 638984 | tf_op jit(solution)/shard_map/ppermute | solution.py:59
  112.5 2.2 %product.3 = bf16[512,3328]{1,0:T(8,128)(2,1)} custom-call(bf16[128,512]{1,0:T(8,128)(2,1)S(1)} %fusion.local_ref, bf16[128,3328]{1,0:T(8,128)(2,1)S(1)} %maximum_bitcast_fusion.1.cot_ref), custom_call_target="tpu_custom_call" | custom-call | tf_op jit(solution)/shard_map/product/pallas_call | solution.py:143
  114.7 1.9 %collective-permute-done.35 = bf16[1,32,3328]{2,1,0:T(8,128)(2,1)S(1)} collective-permute-done((bf16[1,32,3328]{2,1,0:T(8,128)(2,1)S(1)}, bf16[1,32,3328]{2,1,0:T(8,128)(2,1)S(1)}, u32[]{:S(2)}, u32[]{:S(2)}) %collective-permute-start.35) | collective-permute-done | bytes 213024 | tf_op jit(solution)/shard_map/ppermute | solution.py:59
  117.0 2.2 %product.2 = bf16[512,3328]{1,0:T(8,128)(2,1)} custom-call(bf16[128,512]{1,0:T(8,128)(2,1)S(1)} %fusion.local_ref, bf16[128,3328]{1,0:T(8,128)(2,1)S(1)} %maximum_bitcast_fusion.cot_ref), custom_call_target="tpu_custom_call" | custom-call | tf_op jit(solution)/shard_map/product/pallas_call | solution.py:143
  (134 shorter events, 38.6 us)
Async XLA Ops:
  0.6 10.5 %collective-permute-start.1 = (bf16[16,512]{1,0:T(8,128)(2,1)}, bf16[16,512]{1,0:T(8,128)(2,1)S(1)}, u32[]{:S(2)}, u32[]{:S(2)}) collective-permute-start(bf16[16,512]{1,0:T(8,128)(2,1)} %param.6), channel_id=1, source_target_pairs={{0,64},{1,65},{2,66},{3,67},{4,68},{5,69},{6,70},{7,71},{8,72},{9,... | collective-permute-start | bytes 49160 | tf_op jit(solution)/shard_map/ppermute | solution.py:59
  4.7 6.5 %collective-permute-start = (bf16[16,512]{1,0:T(8,128)(2,1)}, bf16[16,512]{1,0:T(8,128)(2,1)S(1)}, u32[]{:S(2)}, u32[]{:S(2)}) collective-permute-start(bf16[16,512]{1,0:T(8,128)(2,1)} %param.6), channel_id=1, source_target_pairs={{0,32},{1,33},{2,34},{3,35},{4,36},{5,37},{6,38},{7,39},{8,40},{9,... | collective-permute-start | bytes 49160 | tf_op jit(solution)/shard_map/ppermute | solution.py:59
  13.5 8.7 %collective-permute-start.4 = (bf16[64,3328]{1,0:T(8,128)(2,1)S(1)}, bf16[64,3328]{1,0:T(8,128)(2,1)S(1)}, u32[]{:S(2)}, u32[]{:S(2)}) collective-permute-start(bf16[64,3328]{1,0:T(8,128)(2,1)S(1)} %slice.299), channel_id=1, source_target_pairs={{0,1},{1,0},{2,3},{3,2},{4,5},{5,4},{6,7},{7,6},{8,9},{9,8},{10,11... | collective-permute-start | bytes 1277960 | tf_op jit(solution)/shard_map/ppermute | solution.py:59
  16.0 9.4 %collective-permute-start.6 = (bf16[64,3328]{1,0:T(8,128)(2,1)S(1)}, bf16[64,3328]{1,0:T(8,128)(2,1)S(1)}, u32[]{:S(2)}, u32[]{:S(2)}) collective-permute-start(bf16[64,3328]{1,0:T(8,128)(2,1)S(1)} %slice.298), channel_id=1, source_target_pairs={{0,3},{1,2},{2,1},{3,0},{4,7},{5,6},{6,5},{7,4},{8,11},{9,10},{10,... | collective-permute-start | bytes 1277960 | tf_op jit(solution)/shard_map/ppermute | solution.py:59
  19.0 8.2 %collective-permute-start.8 = (bf16[64,3328]{1,0:T(8,128)(2,1)S(1)}, bf16[64,3328]{1,0:T(8,128)(2,1)S(1)}, u32[]{:S(2)}, u32[]{:S(2)}) collective-permute-start(bf16[64,3328]{1,0:T(8,128)(2,1)S(1)} %slice.297), channel_id=1, source_target_pairs={{0,1},{1,0},{2,3},{3,2},{4,5},{5,4},{6,7},{7,6},{8,9},{9,8},{10,11... | collective-permute-start | bytes 1277960 | tf_op jit(solution)/shard_map/ppermute | solution.py:59
  20.9 9.4 %collective-permute-start.10 = (bf16[64,3328]{1,0:T(8,128)(2,1)S(1)}, bf16[64,3328]{1,0:T(8,128)(2,1)S(1)}, u32[]{:S(2)}, u32[]{:S(2)}) collective-permute-start(bf16[64,3328]{1,0:T(8,128)(2,1)S(1)} %slice.296), channel_id=1, source_target_pairs={{0,3},{1,2},{2,1},{3,0},{4,7},{5,6},{6,5},{7,4},{8,11},{9,10},{10,... | collective-permute-start | bytes 1277960 | tf_op jit(solution)/shard_map/ppermute | solution.py:59
  22.3 10.3 %collective-permute-start.5 = (bf16[32,3328]{1,0:T(8,128)(2,1)S(1)}, bf16[32,3328]{1,0:T(8,128)(2,1)S(1)}, u32[]{:S(2)}, u32[]{:S(2)}) collective-permute-start(bf16[32,3328]{1,0:T(8,128)(2,1)S(1)} %slice.303), channel_id=1, source_target_pairs={{0,3},{1,2},{2,1},{3,0},{4,7},{5,6},{6,5},{7,4},{8,11},{9,10},{10,... | collective-permute-start | bytes 638984 | tf_op jit(solution)/shard_map/ppermute | solution.py:59
  25.5 7.1 %collective-permute-start.7 = (bf16[32,3328]{1,0:T(8,128)(2,1)S(1)}, bf16[32,3328]{1,0:T(8,128)(2,1)S(1)}, u32[]{:S(2)}, u32[]{:S(2)}) collective-permute-start(bf16[32,3328]{1,0:T(8,128)(2,1)S(1)} %slice.302), channel_id=1, source_target_pairs={{0,1},{1,0},{2,3},{3,2},{4,5},{5,4},{6,7},{7,6},{8,9},{9,8},{10,11... | collective-permute-start | bytes 638984 | tf_op jit(solution)/shard_map/ppermute | solution.py:59
  27.3 7.6 %collective-permute-start.9 = (bf16[32,3328]{1,0:T(8,128)(2,1)S(1)}, bf16[32,3328]{1,0:T(8,128)(2,1)S(1)}, u32[]{:S(2)}, u32[]{:S(2)}) collective-permute-start(bf16[32,3328]{1,0:T(8,128)(2,1)S(1)} %slice.301), channel_id=1, source_target_pairs={{0,3},{1,2},{2,1},{3,0},{4,7},{5,6},{6,5},{7,4},{8,11},{9,10},{10,... | collective-permute-start | bytes 638984 | tf_op jit(solution)/shard_map/ppermute | solution.py:59
  30.5 5.9 %collective-permute-start.11 = (bf16[32,3328]{1,0:T(8,128)(2,1)S(1)}, bf16[32,3328]{1,0:T(8,128)(2,1)S(1)}, u32[]{:S(2)}, u32[]{:S(2)}) collective-permute-start(bf16[32,3328]{1,0:T(8,128)(2,1)S(1)} %slice.300), channel_id=1, source_target_pairs={{0,1},{1,0},{2,3},{3,2},{4,5},{5,4},{6,7},{7,6},{8,9},{9,8},{10,11... | collective-permute-start | bytes 638984 | tf_op jit(solution)/shard_map/ppermute | solution.py:59
  36.7 7.4 %collective-permute-start.12 = (bf16[4,8,3328]{2,1,0:T(8,128)(2,1)S(1)}, bf16[4,8,3328]{2,1,0:T(8,128)(2,1)S(1)}, u32[]{:S(2)}, u32[]{:S(2)}) collective-permute-start(bf16[4,8,3328]{2,1,0:T(8,128)(2,1)S(1)} %get-tuple-element.25), channel_id=1, source_target_pairs={{0,8},{1,9},{2,10},{3,11},{4,12},{5,13},{6,14},{7,15},{8,0},{9,1},... | collective-permute-start | bytes 638984 | tf_op jit(solution)/shard_map/ppermute | solution.py:59
  40.0 6.8 %collective-permute-start.14 = (bf16[4,8,3328]{2,1,0:T(8,128)(2,1)S(1)}, bf16[4,8,3328]{2,1,0:T(8,128)(2,1)S(1)}, u32[]{:S(2)}, u32[]{:S(2)}) collective-permute-start(bf16[4,8,3328]{2,1,0:T(8,128)(2,1)S(1)} %get-tuple-element.26), channel_id=1, source_target_pairs={{0,12},{1,13},{2,14},{3,15},{4,0},{5,1},{6,2},{7,3},{8,4},{9,5},{1... | collective-permute-start | bytes 638984 | tf_op jit(solution)/shard_map/ppermute | solution.py:59
  41.0 7.1 %collective-permute-start.13 = (bf16[4,8,3328]{2,1,0:T(8,128)(2,1)S(1)}, bf16[4,8,3328]{2,1,0:T(8,128)(2,1)S(1)}, u32[]{:S(2)}, u32[]{:S(2)}) collective-permute-start(bf16[4,8,3328]{2,1,0:T(8,128)(2,1)S(1)} %get-tuple-element.27), channel_id=1, source_target_pairs={{0,4},{1,5},{2,6},{3,7},{4,8},{5,9},{6,10},{7,11},{8,12},{9,13},{1... | collective-permute-start | bytes 638984 | tf_op jit(solution)/shard_map/ppermute | solution.py:59
  48.3 6.0 %collective-permute-start.17 = (bf16[1,8,3328]{2,1,0:T(8,128)(2,1)S(1)}, bf16[1,8,3328]{2,1,0:T(8,128)(2,1)S(1)}, u32[]{:S(2)}, u32[]{:S(2)}) collective-permute-start(bf16[1,8,3328]{2,1,0:T(8,128)(2,1)S(1)} %get-tuple-element.21), channel_id=1, source_target_pairs={{0,4},{1,5},{2,6},{3,7},{4,8},{5,9},{6,10},{7,11},{8,12},{9,13},{1... | collective-permute-start | bytes 159752 | tf_op jit(solution)/shard_map/ppermute | solution.py:59
  55.6 10.4 %collective-permute-start.20 = (bf16[1,32,3328]{2,1,0:T(8,128)(2,1)S(1)}, bf16[1,32,3328]{2,1,0:T(8,128)(2,1)S(1)}, u32[]{:S(2)}, u32[]{:S(2)}) collective-permute-start(bf16[1,32,3328]{2,1,0:T(8,128)(2,1)S(1)} %pad_maximum_fusion.2), channel_id=1, source_target_pairs={{0,1},{1,2},{2,3},{3,0},{4,5},{5,6},{6,7},{7,4},{8,9},{9,10},{10,1... | collective-permute-start | bytes 638984 | tf_op jit(solution)/shard_map/ppermute | solution.py:59
  55.7 10.2 %collective-permute-start.19 = (bf16[1,32,3328]{2,1,0:T(8,128)(2,1)S(1)}, bf16[1,32,3328]{2,1,0:T(8,128)(2,1)S(1)}, u32[]{:S(2)}, u32[]{:S(2)}) collective-permute-start(bf16[1,32,3328]{2,1,0:T(8,128)(2,1)S(1)} %pad_maximum_fusion.2), channel_id=1, source_target_pairs={{0,2},{1,3},{2,0},{3,1},{4,6},{5,7},{6,4},{7,5},{8,10},{9,11},{10,... | collective-permute-start | bytes 638984 | tf_op jit(solution)/shard_map/ppermute | solution.py:59
  58.7 7.3 %collective-permute-start.18 = (bf16[1,32,3328]{2,1,0:T(8,128)(2,1)S(1)}, bf16[1,32,3328]{2,1,0:T(8,128)(2,1)S(1)}, u32[]{:S(2)}, u32[]{:S(2)}) collective-permute-start(bf16[1,32,3328]{2,1,0:T(8,128)(2,1)S(1)} %pad_maximum_fusion.2), channel_id=1, source_target_pairs={{0,3},{1,0},{2,1},{3,2},{4,7},{5,4},{6,5},{7,6},{8,11},{9,8},{10,9... | collective-permute-start | bytes 638984 | tf_op jit(solution)/shard_map/ppermute | solution.py:59
  59.3 6.7 %collective-permute-start.21 = (bf16[2,8,3328]{2,1,0:T(8,128)(2,1)S(1)}, bf16[2,8,3328]{2,1,0:T(8,128)(2,1)S(1)}, u32[]{:S(2)}, u32[]{:S(2)}) collective-permute-start(bf16[2,8,3328]{2,1,0:T(8,128)(2,1)S(1)} %pad_maximum_fusion.4), channel_id=1, source_target_pairs={{0,4},{1,5},{2,6},{3,7},{4,0},{5,1},{6,2},{7,3},{8,12},{9,13},{10,... | collective-permute-start | bytes 319496 | tf_op jit(solution)/shard_map/ppermute | solution.py:59
  70.2 6.1 %collective-permute-start.24 = (bf16[64,512]{1,0:T(8,128)(2,1)S(1)}, bf16[64,512]{1,0:T(8,128)(2,1)S(1)}, u32[]{:S(2)}, u32[]{:S(2)}) collective-permute-start(bf16[64,512]{1,0:T(8,128)(2,1)S(1)} %get-tuple-element.18), channel_id=1, source_target_pairs={{0,64},{1,65},{2,66},{3,67},{4,68},{5,69},{6,70},{7,71},{8,72},{9,... | collective-permute-start | bytes 196616 | tf_op jit(solution)/shard_map/ppermute | solution.py:59
  70.2 6.5 %collective-permute-start.23 = (bf16[64,512]{1,0:T(8,128)(2,1)S(1)}, bf16[64,512]{1,0:T(8,128)(2,1)S(1)}, u32[]{:S(2)}, u32[]{:S(2)}) collective-permute-start(bf16[64,512]{1,0:T(8,128)(2,1)S(1)} %get-tuple-element.18), channel_id=1, source_target_pairs={{0,32},{1,33},{2,34},{3,35},{4,36},{5,37},{6,38},{7,39},{8,40},{9,... | collective-permute-start | bytes 196616 | tf_op jit(solution)/shard_map/ppermute | solution.py:59
  76.8 7.3 %collective-permute-start.33 = (bf16[2,16,3328]{2,1,0:T(8,128)(2,1)S(1)}, bf16[2,16,3328]{2,1,0:T(8,128)(2,1)S(1)}, u32[]{:S(2)}, u32[]{:S(2)}) collective-permute-start(bf16[2,16,3328]{2,1,0:T(8,128)(2,1)S(1)} %pad_maximum_fusion.3), channel_id=1, source_target_pairs={{0,12},{1,13},{2,14},{3,15},{4,8},{5,9},{6,10},{7,11},{8,4},{9,5},... | collective-permute-start | bytes 638984 | tf_op jit(solution)/shard_map/ppermute | solution.py:59
  80.6 7.4 %collective-permute-start.27 = (bf16[1,32,3328]{2,1,0:T(8,128)(2,1)S(1)}, bf16[1,32,3328]{2,1,0:T(8,128)(2,1)S(1)}, u32[]{:S(2)}, u32[]{:S(2)}) collective-permute-start(bf16[1,32,3328]{2,1,0:T(8,128)(2,1)S(1)} %get-tuple-element.22), channel_id=1, source_target_pairs={{0,2},{1,3},{2,0},{3,1},{4,6},{5,7},{6,4},{7,5},{8,10},{9,11},{10,... | collective-permute-start | bytes 638984 | tf_op jit(solution)/shard_map/ppermute | solution.py:59
  81.9 8.4 %collective-permute-start.29 = (bf16[1,32,3328]{2,1,0:T(8,128)(2,1)S(1)}, bf16[1,32,3328]{2,1,0:T(8,128)(2,1)S(1)}, u32[]{:S(2)}, u32[]{:S(2)}) collective-permute-start(bf16[1,32,3328]{2,1,0:T(8,128)(2,1)S(1)} %get-tuple-element.23), channel_id=1, source_target_pairs={{0,3},{1,0},{2,1},{3,2},{4,7},{5,4},{6,5},{7,6},{8,11},{9,8},{10,9... | collective-permute-start | bytes 638984 | tf_op jit(solution)/shard_map/ppermute | solution.py:59
  83.9 7.1 %collective-permute-start.28 = (bf16[1,32,3328]{2,1,0:T(8,128)(2,1)S(1)}, bf16[1,32,3328]{2,1,0:T(8,128)(2,1)S(1)}, u32[]{:S(2)}, u32[]{:S(2)}) collective-permute-start(bf16[1,32,3328]{2,1,0:T(8,128)(2,1)S(1)} %get-tuple-element.24), channel_id=1, source_target_pairs={{0,1},{1,2},{2,3},{3,0},{4,5},{5,6},{6,7},{7,4},{8,9},{9,10},{10,1... | collective-permute-start | bytes 638984 | tf_op jit(solution)/shard_map/ppermute | solution.py:59
  92.3 7.1 %collective-permute-start.31 = (bf16[32,3328]{1,0:T(8,128)(2,1)S(1)}, bf16[32,3328]{1,0:T(8,128)(2,1)S(1)}, u32[]{:S(2)}, u32[]{:S(2)}) collective-permute-start(bf16[32,3328]{1,0:T(8,128)(2,1)S(1)} %convert_bitcast_fusion), channel_id=1, source_target_pairs={{0,4},{1,5},{2,6},{3,7},{4,8},{5,9},{6,10},{7,11},{8,12},{9,13},{1... | collective-permute-start | bytes 638984 | tf_op jit(solution)/shard_map/ppermute | solution.py:59
  93.3 8.6 %collective-permute-start.30 = (bf16[32,3328]{1,0:T(8,128)(2,1)S(1)}, bf16[32,3328]{1,0:T(8,128)(2,1)S(1)}, u32[]{:S(2)}, u32[]{:S(2)}) collective-permute-start(bf16[32,3328]{1,0:T(8,128)(2,1)S(1)} %convert_bitcast_fusion), channel_id=1, source_target_pairs={{0,8},{1,9},{2,10},{3,11},{4,12},{5,13},{6,14},{7,15},{8,0},{9,1},... | collective-permute-start | bytes 638984 | tf_op jit(solution)/shard_map/ppermute | solution.py:59
  102.1 7.1 %collective-permute-start.39 = (bf16[1,32,3328]{2,1,0:T(8,128)(2,1)S(1)}, bf16[1,32,3328]{2,1,0:T(8,128)(2,1)S(1)}, u32[]{:S(2)}, u32[]{:S(2)}) collective-permute-start(bf16[1,32,3328]{2,1,0:T(8,128)(2,1)S(1)} %get-tuple-element.16), channel_id=1, source_target_pairs={{0,1},{1,2},{2,3},{3,0},{4,5},{5,6},{6,7},{7,4},{8,9},{9,10},{10,1... | collective-permute-start | bytes 638984 | tf_op jit(solution)/shard_map/ppermute | solution.py:59
  102.2 9.9 %collective-permute-start.38 = (bf16[1,32,3328]{2,1,0:T(8,128)(2,1)S(1)}, bf16[1,32,3328]{2,1,0:T(8,128)(2,1)S(1)}, u32[]{:S(2)}, u32[]{:S(2)}) collective-permute-start(bf16[1,32,3328]{2,1,0:T(8,128)(2,1)S(1)} %get-tuple-element.16), channel_id=1, source_target_pairs={{0,2},{1,3},{2,0},{3,1},{4,6},{5,7},{6,4},{7,5},{8,10},{9,11},{10,... | collective-permute-start | bytes 638984 | tf_op jit(solution)/shard_map/ppermute | solution.py:59
  105.9 6.5 %collective-permute-start.37 = (bf16[1,32,3328]{2,1,0:T(8,128)(2,1)S(1)}, bf16[1,32,3328]{2,1,0:T(8,128)(2,1)S(1)}, u32[]{:S(2)}, u32[]{:S(2)}) collective-permute-start(bf16[1,32,3328]{2,1,0:T(8,128)(2,1)S(1)} %get-tuple-element.16), channel_id=1, source_target_pairs={{0,3},{1,0},{2,1},{3,2},{4,7},{5,4},{6,5},{7,6},{8,11},{9,8},{10,9... | collective-permute-start | bytes 638984 | tf_op jit(solution)/shard_map/ppermute | solution.py:59
  106.3 8.4 %collective-permute-start.36 = (bf16[1,32,3328]{2,1,0:T(8,128)(2,1)S(1)}, bf16[1,32,3328]{2,1,0:T(8,128)(2,1)S(1)}, u32[]{:S(2)}, u32[]{:S(2)}) collective-permute-start(bf16[1,32,3328]{2,1,0:T(8,128)(2,1)S(1)} %multiply_convert_fusion.1), channel_id=1, source_target_pairs={{0,1},{1,2},{2,3},{3,0},{4,5},{5,6},{6,7},{7,4},{8,9},{9,10},{10,1... | collective-permute-start | bytes 638984 | tf_op jit(solution)/shard_map/ppermute | solution.py:59
  108.1 8.5 %collective-permute-start.35 = (bf16[1,32,3328]{2,1,0:T(8,128)(2,1)S(1)}, bf16[1,32,3328]{2,1,0:T(8,128)(2,1)S(1)}, u32[]{:S(2)}, u32[]{:S(2)}) collective-permute-start(bf16[1,32,3328]{2,1,0:T(8,128)(2,1)S(1)} %multiply_convert_fusion.1), channel_id=1, source_target_pairs={{0,2},{1,3},{2,0},{3,1},{4,6},{5,7},{6,4},{7,5},{8,10},{9,11},{10,... | collective-permute-start | bytes 638984 | tf_op jit(solution)/shard_map/ppermute | solution.py:59
  109.3 7.7 %collective-permute-start.34 = (bf16[1,32,3328]{2,1,0:T(8,128)(2,1)S(1)}, bf16[1,32,3328]{2,1,0:T(8,128)(2,1)S(1)}, u32[]{:S(2)}, u32[]{:S(2)}) collective-permute-start(bf16[1,32,3328]{2,1,0:T(8,128)(2,1)S(1)} %multiply_convert_fusion.1), channel_id=1, source_target_pairs={{0,3},{1,0},{2,1},{3,2},{4,7},{5,4},{6,5},{7,6},{8,11},{9,8},{10,9... | collective-permute-start | bytes 638984 | tf_op jit(solution)/shard_map/ppermute | solution.py:59
  (14 other events, 107.5 us)

commit v5 on v4

--- a/solution.py
+++ b/solution.py
@@ -205,20 +205,11 @@
 
 
 def sum_rows(part, factors, next_, k, even):
-    part = jnp.where(k == 0, part, swap_axes(part))
-    mine = jnp.where(k == 0, part[:64], part[64:])
-    other = jnp.where(k == 0, part[64:], part[:64])
-    mine = mine + send(other, CORE)
-    rounded = mine.astype(BF)
-    got = [send(rounded, z_shift(d)) for d in (1, 2, 3)]
-    factors = gather_second_pairs(factors, after(next_, mine), even)
-    return mine + got[0] + got[1] + got[2], factors[0], factors[1]
-
-
-def join_halves(half, k):
-    other = send(half, CORE)
-    full = jnp.where(k == 0, jnp.concatenate([half, other]), jnp.concatenate([other, half]))
-    return jnp.where(k == 0, full, swap_axes(full))
+    rounded = part.astype(BF)
+    got = [send(rounded, z_shift(d)) for d in (1, 3, 2)]
+    factors = gather_second_pairs(factors, after(next_, part), even)
+    chips = part + got[0] + got[1] + got[2]
+    return chips + swap_axes(send(chips, CORE)), factors[0], factors[1]
 
 
 def body(tokens, gate_weight, up_weight, down_weight, gate_tangent, up_tangent):
@@ -255,7 +246,7 @@
     next_ = send(after(factors, hidden), along_second(near))
     hidden = after(gather_first(hidden)[0], next_)
     half, up_slopes, activated = sum_rows(matmul(hidden, down_weight), factors, next_, k, even)
-    output_dir = join_halves((half * out_scale).astype(BF), k)
+    output_dir = (half * out_scale).astype(BF)
     back = sum_second(scatter_first(against_rows(output_dir, down_weight)[None])[0])
     gate_cot = gather_first((back * up_slopes).astype(BF)[None])[0]
     up_cot = gather_first((back * activated).astype(BF)[None])[0]

time: 120 us -> 119 us (level)
    ppermute x40 -> x39, waiting for transfers between devices: 46.5 us -> 45.7 us  [send(): return lax.ppermute(value, RC, to)]
    ppermute x40 -> x39, starting transfers between devices: 55.4 us -> 55.2 us  [send(): return lax.ppermute(value, RC, to)]
  transfers between devices with their start and end apart: 40 -> 39, of which waited for: 28 -> 26; matrix products, arithmetic and copies ran while one was open for 5% -> 5% of each run, Pallas kernels for 2% -> 2%
where the time goes in v5:
time: 119 us; the launch traced here: 118 us
  starting transfers between devices  55.2 us (46%)
  waiting for transfers between devices  45.7 us (38%)
  matrix products  5.49 us (5%)
  Pallas kernels  4.9 us (4%)
  local copies, waits for them, and re-layouts  3.28 us (3%)
  other arithmetic  2.26 us (2%)
  between operations  1.43 us (1%)
    ppermute x39, starting transfers between devices, send(): return lax.ppermute(value, RC, to)  55.2 us
    ppermute x39, waiting for transfers between devices, send(): return lax.ppermute(value, RC, to)  45.7 us
    pallas_call x2, Pallas kernels, product(): pl.pallas_call(kernel, out_shape=jax.ShapeDtypeStruct((features, width),...  4.31 us
    dot_general x11, matrix products, matmul(): return jnp.dot(left, right, preferred_element_type=F32)  4.27 us
    unnamed x17, local copies, waits for them, and re-layouts  2.83 us
  transfers between devices with their start and end apart: 39, of which 26 were waited for; matrix products, arithmetic and copies ran while one was open for 5% of the time, Pallas kernels for 2%

profile of v5, /device:TPU:0, one launch (start us, length us, event | category | flops | bytes accessed | tf_op | source)
XLA Modules:
  0.0 118.3 jit_solution(2144593071035678620)
XLA Ops:
  0.6 4.0 %collective-permute-start.1 = (bf16[16,512]{1,0:T(8,128)(2,1)}, bf16[16,512]{1,0:T(8,128)(2,1)S(1)}, u32[]{:S(2)}, u32[]{:S(2)}) collective-permute-start(bf16[16,512]{1,0:T(8,128)(2,1)} %param.6), channel_id=1, source_target_pairs={{0,64},{1,65},{2,66},{3,67},{4,68},{5,69},{6,70},{7,71},{8,72},{9,... | collective-permute-start | bytes 49160 | tf_op jit(solution)/shard_map/ppermute | solution.py:59
  5.7 2.2 %collective-permute-start.2 = (bf16[16,512]{1,0:T(8,128)(2,1)}, bf16[16,512]{1,0:T(8,128)(2,1)S(1)}, u32[]{:S(2)}, u32[]{:S(2)}) collective-permute-start(bf16[16,512]{1,0:T(8,128)(2,1)} %param.6), channel_id=1, source_target_pairs={{0,96},{1,97},{2,98},{3,99},{4,100},{5,101},{6,102},{7,103},{8,104... | collective-permute-start | bytes 49160 | tf_op jit(solution)/shard_map/ppermute | solution.py:59
  8.6 2.0 %copy-done.1 = bf16[512,3328]{1,0:T(8,128)(2,1)S(1)} copy-done((bf16[512,3328]{1,0:T(8,128)(2,1)S(1)}, bf16[512,3328]{1,0:T(8,128)(2,1)}, u32[]{:S(2)}) %copy-start.1) | copy-done | bytes 3407896
  13.5 1.6 %collective-permute-start.4 = (bf16[64,3328]{1,0:T(8,128)(2,1)S(1)}, bf16[64,3328]{1,0:T(8,128)(2,1)S(1)}, u32[]{:S(2)}, u32[]{:S(2)}) collective-permute-start(bf16[64,3328]{1,0:T(8,128)(2,1)S(1)} %slice.283), channel_id=1, source_target_pairs={{0,1},{1,0},{2,3},{3,2},{4,5},{5,4},{6,7},{7,6},{8,9},{9,8},{10,11... | collective-permute-start | bytes 1277960 | tf_op jit(solution)/shard_map/ppermute | solution.py:59
  16.0 2.3 %collective-permute-start.6 = (bf16[64,3328]{1,0:T(8,128)(2,1)S(1)}, bf16[64,3328]{1,0:T(8,128)(2,1)S(1)}, u32[]{:S(2)}, u32[]{:S(2)}) collective-permute-start(bf16[64,3328]{1,0:T(8,128)(2,1)S(1)} %slice.282), channel_id=1, source_target_pairs={{0,3},{1,2},{2,1},{3,0},{4,7},{5,6},{6,5},{7,4},{8,11},{9,10},{10,... | collective-permute-start | bytes 1277960 | tf_op jit(solution)/shard_map/ppermute | solution.py:59
  22.3 2.3 %collective-permute-start.5 = (bf16[32,3328]{1,0:T(8,128)(2,1)S(1)}, bf16[32,3328]{1,0:T(8,128)(2,1)S(1)}, u32[]{:S(2)}, u32[]{:S(2)}) collective-permute-start(bf16[32,3328]{1,0:T(8,128)(2,1)S(1)} %slice.287), channel_id=1, source_target_pairs={{0,3},{1,2},{2,1},{3,0},{4,7},{5,6},{6,5},{7,4},{8,11},{9,10},{10,... | collective-permute-start | bytes 638984 | tf_op jit(solution)/shard_map/ppermute | solution.py:59
  27.3 1.9 %collective-permute-start.9 = (bf16[32,3328]{1,0:T(8,128)(2,1)S(1)}, bf16[32,3328]{1,0:T(8,128)(2,1)S(1)}, u32[]{:S(2)}, u32[]{:S(2)}) collective-permute-start(bf16[32,3328]{1,0:T(8,128)(2,1)S(1)} %slice.285), channel_id=1, source_target_pairs={{0,3},{1,2},{2,1},{3,0},{4,7},{5,6},{6,5},{7,4},{8,11},{9,10},{10,... | collective-permute-start | bytes 638984 | tf_op jit(solution)/shard_map/ppermute | solution.py:59
  30.5 2.1 %collective-permute-done.5 = bf16[32,3328]{1,0:T(8,128)(2,1)S(1)} collective-permute-done((bf16[32,3328]{1,0:T(8,128)(2,1)S(1)}, bf16[32,3328]{1,0:T(8,128)(2,1)S(1)}, u32[]{:S(2)}, u32[]{:S(2)}) %collective-permute-start.5) | collective-permute-done | bytes 213024 | tf_op jit(solution)/shard_map/ppermute | solution.py:59
  32.7 2.2 %collective-permute-done.9 = bf16[32,3328]{1,0:T(8,128)(2,1)S(1)} collective-permute-done((bf16[32,3328]{1,0:T(8,128)(2,1)S(1)}, bf16[32,3328]{1,0:T(8,128)(2,1)S(1)}, u32[]{:S(2)}, u32[]{:S(2)}) %collective-permute-start.9) | collective-permute-done | bytes 213024 | tf_op jit(solution)/shard_map/ppermute | solution.py:59
  36.7 3.3 %collective-permute-start.12 = (bf16[4,8,3328]{2,1,0:T(8,128)(2,1)S(1)}, bf16[4,8,3328]{2,1,0:T(8,128)(2,1)S(1)}, u32[]{:S(2)}, u32[]{:S(2)}) collective-permute-start(bf16[4,8,3328]{2,1,0:T(8,128)(2,1)S(1)} %get-tuple-element.23), channel_id=1, source_target_pairs={{0,8},{1,9},{2,10},{3,11},{4,12},{5,13},{6,14},{7,15},{8,0},{9,1},... | collective-permute-start | bytes 638984 | tf_op jit(solution)/shard_map/ppermute | solution.py:59
  42.1 2.0 %collective-permute-done.12 = bf16[4,8,3328]{2,1,0:T(8,128)(2,1)S(1)} collective-permute-done((bf16[4,8,3328]{2,1,0:T(8,128)(2,1)S(1)}, bf16[4,8,3328]{2,1,0:T(8,128)(2,1)S(1)}, u32[]{:S(2)}, u32[]{:S(2)}) %collective-permute-start.12) | collective-permute-done | bytes 213024 | tf_op jit(solution)/shard_map/ppermute | solution.py:59
  44.1 2.6 %collective-permute-done.14 = bf16[4,8,3328]{2,1,0:T(8,128)(2,1)S(1)} collective-permute-done((bf16[4,8,3328]{2,1,0:T(8,128)(2,1)S(1)}, bf16[4,8,3328]{2,1,0:T(8,128)(2,1)S(1)}, u32[]{:S(2)}, u32[]{:S(2)}) %collective-permute-start.14) | collective-permute-done | bytes 213024 | tf_op jit(solution)/shard_map/ppermute | solution.py:59
  48.4 2.8 %collective-permute-start.16 = (bf16[1,8,3328]{2,1,0:T(8,128)(2,1)S(1)}, bf16[1,8,3328]{2,1,0:T(8,128)(2,1)S(1)}, u32[]{:S(2)}, u32[]{:S(2)}) collective-permute-start(bf16[1,8,3328]{2,1,0:T(8,128)(2,1)S(1)} %get-tuple-element.19), channel_id=1, source_target_pairs={{0,8},{1,9},{2,10},{3,11},{4,12},{5,13},{6,14},{7,15},{8,0},{9,1},... | collective-permute-start | bytes 159752 | tf_op jit(solution)/shard_map/ppermute | solution.py:59
  52.5 1.7 %collective-permute-done.17 = bf16[1,8,3328]{2,1,0:T(8,128)(2,1)S(1)} collective-permute-done((bf16[1,8,3328]{2,1,0:T(8,128)(2,1)S(1)}, bf16[1,8,3328]{2,1,0:T(8,128)(2,1)S(1)}, u32[]{:S(2)}, u32[]{:S(2)}) %collective-permute-start.17) | collective-permute-done | bytes 53280 | tf_op jit(solution)/shard_map/ppermute | solution.py:59
  55.7 3.0 %collective-permute-start.19 = (bf16[1,32,3328]{2,1,0:T(8,128)(2,1)S(1)}, bf16[1,32,3328]{2,1,0:T(8,128)(2,1)S(1)}, u32[]{:S(2)}, u32[]{:S(2)}) collective-permute-start(bf16[1,32,3328]{2,1,0:T(8,128)(2,1)S(1)} %pad_maximum_fusion.2), channel_id=1, source_target_pairs={{0,2},{1,3},{2,0},{3,1},{4,6},{5,7},{6,4},{7,5},{8,10},{9,11},{10,... | collective-permute-start | bytes 638984 | tf_op jit(solution)/shard_map/ppermute | solution.py:59
  59.3 3.0 %collective-permute-start.21 = (bf16[2,8,3328]{2,1,0:T(8,128)(2,1)S(1)}, bf16[2,8,3328]{2,1,0:T(8,128)(2,1)S(1)}, u32[]{:S(2)}, u32[]{:S(2)}) collective-permute-start(bf16[2,8,3328]{2,1,0:T(8,128)(2,1)S(1)} %pad_maximum_fusion.4), channel_id=1, source_target_pairs={{0,4},{1,5},{2,6},{3,7},{4,0},{5,1},{6,2},{7,3},{8,12},{9,13},{10,... | collective-permute-start | bytes 319496 | tf_op jit(solution)/shard_map/ppermute | solution.py:59
  62.3 3.6 %collective-permute-done.18 = bf16[1,32,3328]{2,1,0:T(8,128)(2,1)S(1)} collective-permute-done((bf16[1,32,3328]{2,1,0:T(8,128)(2,1)S(1)}, bf16[1,32,3328]{2,1,0:T(8,128)(2,1)S(1)}, u32[]{:S(2)}, u32[]{:S(2)}) %collective-permute-start.18) | collective-permute-done | bytes 213024 | tf_op jit(solution)/shard_map/ppermute | solution.py:59
  66.9 2.3 %collective-permute-start.23 = (bf16[128,512]{1,0:T(8,128)(2,1)S(1)}, bf16[128,512]{1,0:T(8,128)(2,1)S(1)}, u32[]{:S(2)}, u32[]{:S(2)}) collective-permute-start(bf16[128,512]{1,0:T(8,128)(2,1)S(1)} %get-tuple-element.36), channel_id=1, source_target_pairs={{0,96},{1,97},{2,98},{3,99},{4,100},{5,101},{6,102},{7,103},{8,104... | collective-permute-start | bytes 393224 | tf_op jit(solution)/shard_map/ppermute | solution.py:59
  69.7 3.5 %collective-permute-done.24 = bf16[128,512]{1,0:T(8,128)(2,1)S(1)} collective-permute-done((bf16[128,512]{1,0:T(8,128)(2,1)S(1)}, bf16[128,512]{1,0:T(8,128)(2,1)S(1)}, u32[]{:S(2)}, u32[]{:S(2)}) %collective-permute-start.24) | collective-permute-done | bytes 131104 | tf_op jit(solution)/shard_map/ppermute | solution.py:59
  73.8 1.6 %collective-permute-done.22 = bf16[128,512]{1,0:T(8,128)(2,1)S(1)} collective-permute-done((bf16[128,512]{1,0:T(8,128)(2,1)S(1)}, bf16[128,512]{1,0:T(8,128)(2,1)S(1)}, u32[]{:S(2)}, u32[]{:S(2)}) %collective-permute-start.22) | collective-permute-done | bytes 131104 | tf_op jit(solution)/shard_map/ppermute | solution.py:59
  75.6 2.3 %collective-permute-start.32 = (bf16[2,16,3328]{2,1,0:T(8,128)(2,1)S(1)}, bf16[2,16,3328]{2,1,0:T(8,128)(2,1)S(1)}, u32[]{:S(2)}, u32[]{:S(2)}) collective-permute-start(bf16[2,16,3328]{2,1,0:T(8,128)(2,1)S(1)} %pad_maximum_fusion.3), channel_id=1, source_target_pairs={{0,12},{1,13},{2,14},{3,15},{4,8},{5,9},{6,10},{7,11},{8,4},{9,5},... | collective-permute-start | bytes 638984 | tf_op jit(solution)/shard_map/ppermute | solution.py:59
  80.6 2.1 %collective-permute-start.28 = (bf16[1,32,3328]{2,1,0:T(8,128)(2,1)S(1)}, bf16[1,32,3328]{2,1,0:T(8,128)(2,1)S(1)}, u32[]{:S(2)}, u32[]{:S(2)}) collective-permute-start(bf16[1,32,3328]{2,1,0:T(8,128)(2,1)S(1)} %get-tuple-element.21), channel_id=1, source_target_pairs={{0,3},{1,0},{2,1},{3,2},{4,7},{5,4},{6,5},{7,6},{8,11},{9,8},{10,9... | collective-permute-start | bytes 638984 | tf_op jit(solution)/shard_map/ppermute | solution.py:59
  82.9 3.8 %collective-permute-done.26 = bf16[1,32,3328]{2,1,0:T(8,128)(2,1)S(1)} collective-permute-done((bf16[1,32,3328]{2,1,0:T(8,128)(2,1)S(1)}, bf16[1,32,3328]{2,1,0:T(8,128)(2,1)S(1)}, u32[]{:S(2)}, u32[]{:S(2)}) %collective-permute-start.26) | collective-permute-done | bytes 213024 | tf_op jit(solution)/shard_map/ppermute | solution.py:59
  86.7 2.3 %collective-permute-done.28 = bf16[1,32,3328]{2,1,0:T(8,128)(2,1)S(1)} collective-permute-done((bf16[1,32,3328]{2,1,0:T(8,128)(2,1)S(1)}, bf16[1,32,3328]{2,1,0:T(8,128)(2,1)S(1)}, u32[]{:S(2)}, u32[]{:S(2)}) %collective-permute-start.28) | collective-permute-done | bytes 213024 | tf_op jit(solution)/shard_map/ppermute | solution.py:59
  92.0 2.5 %collective-permute-start.29 = (bf16[32,3328]{1,0:T(8,128)(2,1)S(1)}, bf16[32,3328]{1,0:T(8,128)(2,1)S(1)}, u32[]{:S(2)}, u32[]{:S(2)}) collective-permute-start(bf16[32,3328]{1,0:T(8,128)(2,1)S(1)} %convert_bitcast_fusion), channel_id=1, source_target_pairs={{0,8},{1,9},{2,10},{3,11},{4,12},{5,13},{6,14},{7,15},{8,0},{9,1},... | collective-permute-start | bytes 638984 | tf_op jit(solution)/shard_map/ppermute | solution.py:59
  95.8 5.0 %collective-permute-done.30 = bf16[32,3328]{1,0:T(8,128)(2,1)S(1)} collective-permute-done((bf16[32,3328]{1,0:T(8,128)(2,1)S(1)}, bf16[32,3328]{1,0:T(8,128)(2,1)S(1)}, u32[]{:S(2)}, u32[]{:S(2)}) %collective-permute-start.30) | collective-permute-done | bytes 213024 | tf_op jit(solution)/shard_map/ppermute | solution.py:59
  101.1 3.5 %collective-permute-start.37 = (bf16[1,32,3328]{2,1,0:T(8,128)(2,1)S(1)}, bf16[1,32,3328]{2,1,0:T(8,128)(2,1)S(1)}, u32[]{:S(2)}, u32[]{:S(2)}) collective-permute-start(bf16[1,32,3328]{2,1,0:T(8,128)(2,1)S(1)} %get-tuple-element.16), channel_id=1, source_target_pairs={{0,2},{1,3},{2,0},{3,1},{4,6},{5,7},{6,4},{7,5},{8,10},{9,11},{10,... | collective-permute-start | bytes 638984 | tf_op jit(solution)/shard_map/ppermute | solution.py:59
  105.0 1.8 %collective-permute-start.35 = (bf16[1,32,3328]{2,1,0:T(8,128)(2,1)S(1)}, bf16[1,32,3328]{2,1,0:T(8,128)(2,1)S(1)}, u32[]{:S(2)}, u32[]{:S(2)}) collective-permute-start(bf16[1,32,3328]{2,1,0:T(8,128)(2,1)S(1)} %multiply_convert_fusion.1), channel_id=1, source_target_pairs={{0,1},{1,2},{2,3},{3,0},{4,5},{5,6},{6,7},{7,4},{8,9},{9,10},{10,1... | collective-permute-start | bytes 638984 | tf_op jit(solution)/shard_map/ppermute | solution.py:59
  108.2 1.9 %collective-permute-start.33 = (bf16[1,32,3328]{2,1,0:T(8,128)(2,1)S(1)}, bf16[1,32,3328]{2,1,0:T(8,128)(2,1)S(1)}, u32[]{:S(2)}, u32[]{:S(2)}) collective-permute-start(bf16[1,32,3328]{2,1,0:T(8,128)(2,1)S(1)} %multiply_convert_fusion.1), channel_id=1, source_target_pairs={{0,3},{1,0},{2,1},{3,2},{4,7},{5,4},{6,5},{7,6},{8,11},{9,8},{10,9... | collective-permute-start | bytes 638984 | tf_op jit(solution)/shard_map/ppermute | solution.py:59
  111.4 2.2 %product.3 = bf16[512,3328]{1,0:T(8,128)(2,1)} custom-call(bf16[128,512]{1,0:T(8,128)(2,1)S(1)} %fusion.local_ref, bf16[128,3328]{1,0:T(8,128)(2,1)S(1)} %maximum_bitcast_fusion.1.cot_ref), custom_call_target="tpu_custom_call" | custom-call | tf_op jit(solution)/shard_map/product/pallas_call | solution.py:143
  113.6 1.8 %collective-permute-done.34 = bf16[1,32,3328]{2,1,0:T(8,128)(2,1)S(1)} collective-permute-done((bf16[1,32,3328]{2,1,0:T(8,128)(2,1)S(1)}, bf16[1,32,3328]{2,1,0:T(8,128)(2,1)S(1)}, u32[]{:S(2)}, u32[]{:S(2)}) %collective-permute-start.34) | collective-permute-done | bytes 213024 | tf_op jit(solution)/shard_map/ppermute | solution.py:59
  116.0 2.2 %product.2 = bf16[512,3328]{1,0:T(8,128)(2,1)} custom-call(bf16[128,512]{1,0:T(8,128)(2,1)S(1)} %fusion.local_ref, bf16[128,3328]{1,0:T(8,128)(2,1)S(1)} %maximum_bitcast_fusion.cot_ref), custom_call_target="tpu_custom_call" | custom-call | tf_op jit(solution)/shard_map/product/pallas_call | solution.py:143
  (127 shorter events, 35.6 us)
Async XLA Ops:
  0.6 10.5 %collective-permute-start.1 = (bf16[16,512]{1,0:T(8,128)(2,1)}, bf16[16,512]{1,0:T(8,128)(2,1)S(1)}, u32[]{:S(2)}, u32[]{:S(2)}) collective-permute-start(bf16[16,512]{1,0:T(8,128)(2,1)} %param.6), channel_id=1, source_target_pairs={{0,64},{1,65},{2,66},{3,67},{4,68},{5,69},{6,70},{7,71},{8,72},{9,... | collective-permute-start | bytes 49160 | tf_op jit(solution)/shard_map/ppermute | solution.py:59
  4.7 6.5 %collective-permute-start = (bf16[16,512]{1,0:T(8,128)(2,1)}, bf16[16,512]{1,0:T(8,128)(2,1)S(1)}, u32[]{:S(2)}, u32[]{:S(2)}) collective-permute-start(bf16[16,512]{1,0:T(8,128)(2,1)} %param.6), channel_id=1, source_target_pairs={{0,32},{1,33},{2,34},{3,35},{4,36},{5,37},{6,38},{7,39},{8,40},{9,... | collective-permute-start | bytes 49160 | tf_op jit(solution)/shard_map/ppermute | solution.py:59
  13.5 8.7 %collective-permute-start.4 = (bf16[64,3328]{1,0:T(8,128)(2,1)S(1)}, bf16[64,3328]{1,0:T(8,128)(2,1)S(1)}, u32[]{:S(2)}, u32[]{:S(2)}) collective-permute-start(bf16[64,3328]{1,0:T(8,128)(2,1)S(1)} %slice.283), channel_id=1, source_target_pairs={{0,1},{1,0},{2,3},{3,2},{4,5},{5,4},{6,7},{7,6},{8,9},{9,8},{10,11... | collective-permute-start | bytes 1277960 | tf_op jit(solution)/shard_map/ppermute | solution.py:59
  16.0 9.4 %collective-permute-start.6 = (bf16[64,3328]{1,0:T(8,128)(2,1)S(1)}, bf16[64,3328]{1,0:T(8,128)(2,1)S(1)}, u32[]{:S(2)}, u32[]{:S(2)}) collective-permute-start(bf16[64,3328]{1,0:T(8,128)(2,1)S(1)} %slice.282), channel_id=1, source_target_pairs={{0,3},{1,2},{2,1},{3,0},{4,7},{5,6},{6,5},{7,4},{8,11},{9,10},{10,... | collective-permute-start | bytes 1277960 | tf_op jit(solution)/shard_map/ppermute | solution.py:59
  19.0 8.2 %collective-permute-start.8 = (bf16[64,3328]{1,0:T(8,128)(2,1)S(1)}, bf16[64,3328]{1,0:T(8,128)(2,1)S(1)}, u32[]{:S(2)}, u32[]{:S(2)}) collective-permute-start(bf16[64,3328]{1,0:T(8,128)(2,1)S(1)} %slice.281), channel_id=1, source_target_pairs={{0,1},{1,0},{2,3},{3,2},{4,5},{5,4},{6,7},{7,6},{8,9},{9,8},{10,11... | collective-permute-start | bytes 1277960 | tf_op jit(solution)/shard_map/ppermute | solution.py:59
  20.9 9.4 %collective-permute-start.10 = (bf16[64,3328]{1,0:T(8,128)(2,1)S(1)}, bf16[64,3328]{1,0:T(8,128)(2,1)S(1)}, u32[]{:S(2)}, u32[]{:S(2)}) collective-permute-start(bf16[64,3328]{1,0:T(8,128)(2,1)S(1)} %slice.280), channel_id=1, source_target_pairs={{0,3},{1,2},{2,1},{3,0},{4,7},{5,6},{6,5},{7,4},{8,11},{9,10},{10,... | collective-permute-start | bytes 1277960 | tf_op jit(solution)/shard_map/ppermute | solution.py:59
  22.3 10.3 %collective-permute-start.5 = (bf16[32,3328]{1,0:T(8,128)(2,1)S(1)}, bf16[32,3328]{1,0:T(8,128)(2,1)S(1)}, u32[]{:S(2)}, u32[]{:S(2)}) collective-permute-start(bf16[32,3328]{1,0:T(8,128)(2,1)S(1)} %slice.287), channel_id=1, source_target_pairs={{0,3},{1,2},{2,1},{3,0},{4,7},{5,6},{6,5},{7,4},{8,11},{9,10},{10,... | collective-permute-start | bytes 638984 | tf_op jit(solution)/shard_map/ppermute | solution.py:59
  25.5 7.1 %collective-permute-start.7 = (bf16[32,3328]{1,0:T(8,128)(2,1)S(1)}, bf16[32,3328]{1,0:T(8,128)(2,1)S(1)}, u32[]{:S(2)}, u32[]{:S(2)}) collective-permute-start(bf16[32,3328]{1,0:T(8,128)(2,1)S(1)} %slice.286), channel_id=1, source_target_pairs={{0,1},{1,0},{2,3},{3,2},{4,5},{5,4},{6,7},{7,6},{8,9},{9,8},{10,11... | collective-permute-start | bytes 638984 | tf_op jit(solution)/shard_map/ppermute | solution.py:59
  27.3 7.6 %collective-permute-start.9 = (bf16[32,3328]{1,0:T(8,128)(2,1)S(1)}, bf16[32,3328]{1,0:T(8,128)(2,1)S(1)}, u32[]{:S(2)}, u32[]{:S(2)}) collective-permute-start(bf16[32,3328]{1,0:T(8,128)(2,1)S(1)} %slice.285), channel_id=1, source_target_pairs={{0,3},{1,2},{2,1},{3,0},{4,7},{5,6},{6,5},{7,4},{8,11},{9,10},{10,... | collective-permute-start | bytes 638984 | tf_op jit(solution)/shard_map/ppermute | solution.py:59
  36.7 7.4 %collective-permute-start.12 = (bf16[4,8,3328]{2,1,0:T(8,128)(2,1)S(1)}, bf16[4,8,3328]{2,1,0:T(8,128)(2,1)S(1)}, u32[]{:S(2)}, u32[]{:S(2)}) collective-permute-start(bf16[4,8,3328]{2,1,0:T(8,128)(2,1)S(1)} %get-tuple-element.23), channel_id=1, source_target_pairs={{0,8},{1,9},{2,10},{3,11},{4,12},{5,13},{6,14},{7,15},{8,0},{9,1},... | collective-permute-start | bytes 638984 | tf_op jit(solution)/shard_map/ppermute | solution.py:59
  40.0 6.8 %collective-permute-start.14 = (bf16[4,8,3328]{2,1,0:T(8,128)(2,1)S(1)}, bf16[4,8,3328]{2,1,0:T(8,128)(2,1)S(1)}, u32[]{:S(2)}, u32[]{:S(2)}) collective-permute-start(bf16[4,8,3328]{2,1,0:T(8,128)(2,1)S(1)} %get-tuple-element.24), channel_id=1, source_target_pairs={{0,12},{1,13},{2,14},{3,15},{4,0},{5,1},{6,2},{7,3},{8,4},{9,5},{1... | collective-permute-start | bytes 638984 | tf_op jit(solution)/shard_map/ppermute | solution.py:59
  41.0 7.1 %collective-permute-start.13 = (bf16[4,8,3328]{2,1,0:T(8,128)(2,1)S(1)}, bf16[4,8,3328]{2,1,0:T(8,128)(2,1)S(1)}, u32[]{:S(2)}, u32[]{:S(2)}) collective-permute-start(bf16[4,8,3328]{2,1,0:T(8,128)(2,1)S(1)} %get-tuple-element.25), channel_id=1, source_target_pairs={{0,4},{1,5},{2,6},{3,7},{4,8},{5,9},{6,10},{7,11},{8,12},{9,13},{1... | collective-permute-start | bytes 638984 | tf_op jit(solution)/shard_map/ppermute | solution.py:59
  48.3 6.0 %collective-permute-start.17 = (bf16[1,8,3328]{2,1,0:T(8,128)(2,1)S(1)}, bf16[1,8,3328]{2,1,0:T(8,128)(2,1)S(1)}, u32[]{:S(2)}, u32[]{:S(2)}) collective-permute-start(bf16[1,8,3328]{2,1,0:T(8,128)(2,1)S(1)} %get-tuple-element.19), channel_id=1, source_target_pairs={{0,4},{1,5},{2,6},{3,7},{4,8},{5,9},{6,10},{7,11},{8,12},{9,13},{1... | collective-permute-start | bytes 159752 | tf_op jit(solution)/shard_map/ppermute | solution.py:59
  55.6 10.4 %collective-permute-start.20 = (bf16[1,32,3328]{2,1,0:T(8,128)(2,1)S(1)}, bf16[1,32,3328]{2,1,0:T(8,128)(2,1)S(1)}, u32[]{:S(2)}, u32[]{:S(2)}) collective-permute-start(bf16[1,32,3328]{2,1,0:T(8,128)(2,1)S(1)} %pad_maximum_fusion.2), channel_id=1, source_target_pairs={{0,1},{1,2},{2,3},{3,0},{4,5},{5,6},{6,7},{7,4},{8,9},{9,10},{10,1... | collective-permute-start | bytes 638984 | tf_op jit(solution)/shard_map/ppermute | solution.py:59
  55.7 10.2 %collective-permute-start.19 = (bf16[1,32,3328]{2,1,0:T(8,128)(2,1)S(1)}, bf16[1,32,3328]{2,1,0:T(8,128)(2,1)S(1)}, u32[]{:S(2)}, u32[]{:S(2)}) collective-permute-start(bf16[1,32,3328]{2,1,0:T(8,128)(2,1)S(1)} %pad_maximum_fusion.2), channel_id=1, source_target_pairs={{0,2},{1,3},{2,0},{3,1},{4,6},{5,7},{6,4},{7,5},{8,10},{9,11},{10,... | collective-permute-start | bytes 638984 | tf_op jit(solution)/shard_map/ppermute | solution.py:59
  58.7 7.3 %collective-permute-start.18 = (bf16[1,32,3328]{2,1,0:T(8,128)(2,1)S(1)}, bf16[1,32,3328]{2,1,0:T(8,128)(2,1)S(1)}, u32[]{:S(2)}, u32[]{:S(2)}) collective-permute-start(bf16[1,32,3328]{2,1,0:T(8,128)(2,1)S(1)} %pad_maximum_fusion.2), channel_id=1, source_target_pairs={{0,3},{1,0},{2,1},{3,2},{4,7},{5,4},{6,5},{7,6},{8,11},{9,8},{10,9... | collective-permute-start | bytes 638984 | tf_op jit(solution)/shard_map/ppermute | solution.py:59
  59.3 6.7 %collective-permute-start.21 = (bf16[2,8,3328]{2,1,0:T(8,128)(2,1)S(1)}, bf16[2,8,3328]{2,1,0:T(8,128)(2,1)S(1)}, u32[]{:S(2)}, u32[]{:S(2)}) collective-permute-start(bf16[2,8,3328]{2,1,0:T(8,128)(2,1)S(1)} %pad_maximum_fusion.4), channel_id=1, source_target_pairs={{0,4},{1,5},{2,6},{3,7},{4,0},{5,1},{6,2},{7,3},{8,12},{9,13},{10,... | collective-permute-start | bytes 319496 | tf_op jit(solution)/shard_map/ppermute | solution.py:59
  66.7 6.6 %collective-permute-start.24 = (bf16[128,512]{1,0:T(8,128)(2,1)S(1)}, bf16[128,512]{1,0:T(8,128)(2,1)S(1)}, u32[]{:S(2)}, u32[]{:S(2)}) collective-permute-start(bf16[128,512]{1,0:T(8,128)(2,1)S(1)} %get-tuple-element.36), channel_id=1, source_target_pairs={{0,64},{1,65},{2,66},{3,67},{4,68},{5,69},{6,70},{7,71},{8,72},{9,... | collective-permute-start | bytes 393224 | tf_op jit(solution)/shard_map/ppermute | solution.py:59
  66.9 6.9 %collective-permute-start.23 = (bf16[128,512]{1,0:T(8,128)(2,1)S(1)}, bf16[128,512]{1,0:T(8,128)(2,1)S(1)}, u32[]{:S(2)}, u32[]{:S(2)}) collective-permute-start(bf16[128,512]{1,0:T(8,128)(2,1)S(1)} %get-tuple-element.36), channel_id=1, source_target_pairs={{0,96},{1,97},{2,98},{3,99},{4,100},{5,101},{6,102},{7,103},{8,104... | collective-permute-start | bytes 393224 | tf_op jit(solution)/shard_map/ppermute | solution.py:59
  69.2 6.2 %collective-permute-start.22 = (bf16[128,512]{1,0:T(8,128)(2,1)S(1)}, bf16[128,512]{1,0:T(8,128)(2,1)S(1)}, u32[]{:S(2)}, u32[]{:S(2)}) collective-permute-start(bf16[128,512]{1,0:T(8,128)(2,1)S(1)} %get-tuple-element.36), channel_id=1, source_target_pairs={{0,32},{1,33},{2,34},{3,35},{4,36},{5,37},{6,38},{7,39},{8,40},{9,... | collective-permute-start | bytes 393224 | tf_op jit(solution)/shard_map/ppermute | solution.py:59
  75.6 7.3 %collective-permute-start.32 = (bf16[2,16,3328]{2,1,0:T(8,128)(2,1)S(1)}, bf16[2,16,3328]{2,1,0:T(8,128)(2,1)S(1)}, u32[]{:S(2)}, u32[]{:S(2)}) collective-permute-start(bf16[2,16,3328]{2,1,0:T(8,128)(2,1)S(1)} %pad_maximum_fusion.3), channel_id=1, source_target_pairs={{0,12},{1,13},{2,14},{3,15},{4,8},{5,9},{6,10},{7,11},{8,4},{9,5},... | collective-permute-start | bytes 638984 | tf_op jit(solution)/shard_map/ppermute | solution.py:59
  79.3 7.4 %collective-permute-start.26 = (bf16[1,32,3328]{2,1,0:T(8,128)(2,1)S(1)}, bf16[1,32,3328]{2,1,0:T(8,128)(2,1)S(1)}, u32[]{:S(2)}, u32[]{:S(2)}) collective-permute-start(bf16[1,32,3328]{2,1,0:T(8,128)(2,1)S(1)} %get-tuple-element.20), channel_id=1, source_target_pairs={{0,2},{1,3},{2,0},{3,1},{4,6},{5,7},{6,4},{7,5},{8,10},{9,11},{10,... | collective-permute-start | bytes 638984 | tf_op jit(solution)/shard_map/ppermute | solution.py:59
  80.6 8.4 %collective-permute-start.28 = (bf16[1,32,3328]{2,1,0:T(8,128)(2,1)S(1)}, bf16[1,32,3328]{2,1,0:T(8,128)(2,1)S(1)}, u32[]{:S(2)}, u32[]{:S(2)}) collective-permute-start(bf16[1,32,3328]{2,1,0:T(8,128)(2,1)S(1)} %get-tuple-element.21), channel_id=1, source_target_pairs={{0,3},{1,0},{2,1},{3,2},{4,7},{5,4},{6,5},{7,6},{8,11},{9,8},{10,9... | collective-permute-start | bytes 638984 | tf_op jit(solution)/shard_map/ppermute | solution.py:59
  82.7 7.1 %collective-permute-start.27 = (bf16[1,32,3328]{2,1,0:T(8,128)(2,1)S(1)}, bf16[1,32,3328]{2,1,0:T(8,128)(2,1)S(1)}, u32[]{:S(2)}, u32[]{:S(2)}) collective-permute-start(bf16[1,32,3328]{2,1,0:T(8,128)(2,1)S(1)} %get-tuple-element.22), channel_id=1, source_target_pairs={{0,1},{1,2},{2,3},{3,0},{4,5},{5,6},{6,7},{7,4},{8,9},{9,10},{10,1... | collective-permute-start | bytes 638984 | tf_op jit(solution)/shard_map/ppermute | solution.py:59
  91.3 9.4 %collective-permute-start.30 = (bf16[32,3328]{1,0:T(8,128)(2,1)S(1)}, bf16[32,3328]{1,0:T(8,128)(2,1)S(1)}, u32[]{:S(2)}, u32[]{:S(2)}) collective-permute-start(bf16[32,3328]{1,0:T(8,128)(2,1)S(1)} %convert_bitcast_fusion), channel_id=1, source_target_pairs={{0,4},{1,5},{2,6},{3,7},{4,8},{5,9},{6,10},{7,11},{8,12},{9,13},{1... | collective-permute-start | bytes 638984 | tf_op jit(solution)/shard_map/ppermute | solution.py:59
  92.0 8.8 %collective-permute-start.29 = (bf16[32,3328]{1,0:T(8,128)(2,1)S(1)}, bf16[32,3328]{1,0:T(8,128)(2,1)S(1)}, u32[]{:S(2)}, u32[]{:S(2)}) collective-permute-start(bf16[32,3328]{1,0:T(8,128)(2,1)S(1)} %convert_bitcast_fusion), channel_id=1, source_target_pairs={{0,8},{1,9},{2,10},{3,11},{4,12},{5,13},{6,14},{7,15},{8,0},{9,1},... | collective-permute-start | bytes 638984 | tf_op jit(solution)/shard_map/ppermute | solution.py:59
  101.0 7.1 %collective-permute-start.38 = (bf16[1,32,3328]{2,1,0:T(8,128)(2,1)S(1)}, bf16[1,32,3328]{2,1,0:T(8,128)(2,1)S(1)}, u32[]{:S(2)}, u32[]{:S(2)}) collective-permute-start(bf16[1,32,3328]{2,1,0:T(8,128)(2,1)S(1)} %get-tuple-element.16), channel_id=1, source_target_pairs={{0,1},{1,2},{2,3},{3,0},{4,5},{5,6},{6,7},{7,4},{8,9},{9,10},{10,1... | collective-permute-start | bytes 638984 | tf_op jit(solution)/shard_map/ppermute | solution.py:59
  101.1 9.7 %collective-permute-start.37 = (bf16[1,32,3328]{2,1,0:T(8,128)(2,1)S(1)}, bf16[1,32,3328]{2,1,0:T(8,128)(2,1)S(1)}, u32[]{:S(2)}, u32[]{:S(2)}) collective-permute-start(bf16[1,32,3328]{2,1,0:T(8,128)(2,1)S(1)} %get-tuple-element.16), channel_id=1, source_target_pairs={{0,2},{1,3},{2,0},{3,1},{4,6},{5,7},{6,4},{7,5},{8,10},{9,11},{10,... | collective-permute-start | bytes 638984 | tf_op jit(solution)/shard_map/ppermute | solution.py:59
  104.7 6.7 %collective-permute-start.36 = (bf16[1,32,3328]{2,1,0:T(8,128)(2,1)S(1)}, bf16[1,32,3328]{2,1,0:T(8,128)(2,1)S(1)}, u32[]{:S(2)}, u32[]{:S(2)}) collective-permute-start(bf16[1,32,3328]{2,1,0:T(8,128)(2,1)S(1)} %get-tuple-element.16), channel_id=1, source_target_pairs={{0,3},{1,0},{2,1},{3,2},{4,7},{5,4},{6,5},{7,6},{8,11},{9,8},{10,9... | collective-permute-start | bytes 638984 | tf_op jit(solution)/shard_map/ppermute | solution.py:59
  105.0 8.6 %collective-permute-start.35 = (bf16[1,32,3328]{2,1,0:T(8,128)(2,1)S(1)}, bf16[1,32,3328]{2,1,0:T(8,128)(2,1)S(1)}, u32[]{:S(2)}, u32[]{:S(2)}) collective-permute-start(bf16[1,32,3328]{2,1,0:T(8,128)(2,1)S(1)} %multiply_convert_fusion.1), channel_id=1, source_target_pairs={{0,1},{1,2},{2,3},{3,0},{4,5},{5,6},{6,7},{7,4},{8,9},{9,10},{10,1... | collective-permute-start | bytes 638984 | tf_op jit(solution)/shard_map/ppermute | solution.py:59
  106.8 8.5 %collective-permute-start.34 = (bf16[1,32,3328]{2,1,0:T(8,128)(2,1)S(1)}, bf16[1,32,3328]{2,1,0:T(8,128)(2,1)S(1)}, u32[]{:S(2)}, u32[]{:S(2)}) collective-permute-start(bf16[1,32,3328]{2,1,0:T(8,128)(2,1)S(1)} %multiply_convert_fusion.1), channel_id=1, source_target_pairs={{0,2},{1,3},{2,0},{3,1},{4,6},{5,7},{6,4},{7,5},{8,10},{9,11},{10,... | collective-permute-start | bytes 638984 | tf_op jit(solution)/shard_map/ppermute | solution.py:59
  108.2 7.8 %collective-permute-start.33 = (bf16[1,32,3328]{2,1,0:T(8,128)(2,1)S(1)}, bf16[1,32,3328]{2,1,0:T(8,128)(2,1)S(1)}, u32[]{:S(2)}, u32[]{:S(2)}) collective-permute-start(bf16[1,32,3328]{2,1,0:T(8,128)(2,1)S(1)} %multiply_convert_fusion.1), channel_id=1, source_target_pairs={{0,3},{1,0},{2,1},{3,2},{4,7},{5,4},{6,5},{7,6},{8,11},{9,8},{10,9... | collective-permute-start | bytes 638984 | tf_op jit(solution)/shard_map/ppermute | solution.py:59
  (13 other events, 106.9 us)

commit v6 on v5

--- a/solution.py
+++ b/solution.py
@@ -61,14 +61,6 @@
 
 def matmul(left, right):
     return jnp.dot(left, right, preferred_element_type=F32)
-
-
-def against_rows(left, right):
-    return lax.dot_general(left, right, (((1,), (1,)), ((), ())), preferred_element_type=F32)
-
-
-def transposed(left, right):
-    return lax.dot_general(left, right, (((0,), (0,)), ((), ())), preferred_element_type=F32)
 
 
 def gather_tokens(tokens, ready):
@@ -204,7 +196,7 @@
     return value.reshape(4, 4, 8, -1).swapaxes(0, 1).reshape(value.shape)
 
 
-def sum_rows(part, factors, next_, k, even):
+def sum_rows(part, factors, next_, even):
     rounded = part.astype(BF)
     got = [send(rounded, z_shift(d)) for d in (1, 3, 2)]
     factors = gather_second_pairs(factors, after(next_, part), even)
@@ -233,6 +225,8 @@
     up_sum, sent = halve(after(behind, sent), up_weight, *far_near)
     gate_dir, sent = halve(after(ahead, sent), gate_tangent, *near_far)
     up_dir, sent = halve(after(behind, sent), up_tangent, *far_near)
+    down_t = lax.optimization_barrier(after(down_weight, sent).T)
+    gate_dir = after(gate_dir, down_t)
     gate_sum, up_sum, gate_dir, up_dir = scatter_second(
         jnp.stack([gate_sum, up_sum, gate_dir, up_dir])
     )
@@ -245,9 +239,9 @@
     hidden = gather_second(hidden[None])
     next_ = send(after(factors, hidden), along_second(near))
     hidden = after(gather_first(hidden)[0], next_)
-    half, up_slopes, activated = sum_rows(matmul(hidden, down_weight), factors, next_, k, even)
+    half, up_slopes, activated = sum_rows(matmul(hidden, down_weight), factors, next_, even)
     output_dir = (half * out_scale).astype(BF)
-    back = sum_second(scatter_first(against_rows(output_dir, down_weight)[None])[0])
+    back = sum_second(scatter_first(matmul(output_dir, down_t)[None])[0])
     gate_cot = gather_first((back * up_slopes).astype(BF)[None])[0]
     up_cot = gather_first((back * activated).astype(BF)[None])[0]
     return product(local, gate_cot), product(local, up_cot)

time: 119 us -> 119 us (level)
    dot_general x11 -> x12, matrix products: 4.27 us -> 5.51 us  [matmul(): return jnp.dot(left, right, preferred_element_type=F32)]
    dot_general x1 -> x0, matrix products: 1.23 us -> none  [against_rows(): lax.dot_general(left, right, (((1,), (1,)), ((), ())), preferred_element_...]
where the time goes in v6:
time: 119 us; the launch traced here: 118 us
  starting transfers between devices  55.2 us (46%)
  waiting for transfers between devices  45.7 us (38%)
  matrix products  5.51 us (5%)
  Pallas kernels  4.9 us (4%)
  local copies, waits for them, and re-layouts  3.28 us (3%)
  other arithmetic  2.26 us (2%)
  between operations  1.43 us (1%)
    ppermute x39, starting transfers between devices, send(): return lax.ppermute(value, RC, to)  55.2 us
    ppermute x39, waiting for transfers between devices, send(): return lax.ppermute(value, RC, to)  45.7 us
    dot_general x12, matrix products, matmul(): return jnp.dot(left, right, preferred_element_type=F32)  5.51 us
    pallas_call x2, Pallas kernels, product(): pl.pallas_call(kernel, out_shape=jax.ShapeDtypeStruct((features, width),...  4.31 us
    unnamed x17, local copies, waits for them, and re-layouts  2.83 us
  transfers between devices with their start and end apart: 39, of which 26 were waited for; matrix products, arithmetic and copies ran while one was open for 5% of the time, Pallas kernels for 2%

profile of v6, /device:TPU:0, one launch (start us, length us, event | category | flops | bytes accessed | tf_op | source)
XLA Modules:
  0.0 118.3 jit_solution(11334707558191994920)
XLA Ops:
  0.6 4.0 %collective-permute-start.1 = (bf16[16,512]{1,0:T(8,128)(2,1)}, bf16[16,512]{1,0:T(8,128)(2,1)S(1)}, u32[]{:S(2)}, u32[]{:S(2)}) collective-permute-start(bf16[16,512]{1,0:T(8,128)(2,1)} %param.6), channel_id=1, source_target_pairs={{0,64},{1,65},{2,66},{3,67},{4,68},{5,69},{6,70},{7,71},{8,72},{9,... | collective-permute-start | bytes 49160 | tf_op jit(solution)/shard_map/ppermute | solution.py:59
  5.7 2.2 %collective-permute-start.2 = (bf16[16,512]{1,0:T(8,128)(2,1)}, bf16[16,512]{1,0:T(8,128)(2,1)S(1)}, u32[]{:S(2)}, u32[]{:S(2)}) collective-permute-start(bf16[16,512]{1,0:T(8,128)(2,1)} %param.6), channel_id=1, source_target_pairs={{0,96},{1,97},{2,98},{3,99},{4,100},{5,101},{6,102},{7,103},{8,104... | collective-permute-start | bytes 49160 | tf_op jit(solution)/shard_map/ppermute | solution.py:59
  8.6 2.0 %copy-done.1 = bf16[512,3328]{1,0:T(8,128)(2,1)S(1)} copy-done((bf16[512,3328]{1,0:T(8,128)(2,1)S(1)}, bf16[512,3328]{1,0:T(8,128)(2,1)}, u32[]{:S(2)}) %copy-start.1) | copy-done | bytes 3407896
  13.5 1.6 %collective-permute-start.4 = (bf16[64,3328]{1,0:T(8,128)(2,1)S(1)}, bf16[64,3328]{1,0:T(8,128)(2,1)S(1)}, u32[]{:S(2)}, u32[]{:S(2)}) collective-permute-start(bf16[64,3328]{1,0:T(8,128)(2,1)S(1)} %slice.281), channel_id=1, source_target_pairs={{0,1},{1,0},{2,3},{3,2},{4,5},{5,4},{6,7},{7,6},{8,9},{9,8},{10,11... | collective-permute-start | bytes 1277960 | tf_op jit(solution)/shard_map/ppermute | solution.py:59
  16.0 2.3 %collective-permute-start.6 = (bf16[64,3328]{1,0:T(8,128)(2,1)S(1)}, bf16[64,3328]{1,0:T(8,128)(2,1)S(1)}, u32[]{:S(2)}, u32[]{:S(2)}) collective-permute-start(bf16[64,3328]{1,0:T(8,128)(2,1)S(1)} %slice.280), channel_id=1, source_target_pairs={{0,3},{1,2},{2,1},{3,0},{4,7},{5,6},{6,5},{7,4},{8,11},{9,10},{10,... | collective-permute-start | bytes 1277960 | tf_op jit(solution)/shard_map/ppermute | solution.py:59
  22.3 2.3 %collective-permute-start.5 = (bf16[32,3328]{1,0:T(8,128)(2,1)S(1)}, bf16[32,3328]{1,0:T(8,128)(2,1)S(1)}, u32[]{:S(2)}, u32[]{:S(2)}) collective-permute-start(bf16[32,3328]{1,0:T(8,128)(2,1)S(1)} %slice.285), channel_id=1, source_target_pairs={{0,3},{1,2},{2,1},{3,0},{4,7},{5,6},{6,5},{7,4},{8,11},{9,10},{10,... | collective-permute-start | bytes 638984 | tf_op jit(solution)/shard_map/ppermute | solution.py:59
  27.3 1.9 %collective-permute-start.9 = (bf16[32,3328]{1,0:T(8,128)(2,1)S(1)}, bf16[32,3328]{1,0:T(8,128)(2,1)S(1)}, u32[]{:S(2)}, u32[]{:S(2)}) collective-permute-start(bf16[32,3328]{1,0:T(8,128)(2,1)S(1)} %slice.283), channel_id=1, source_target_pairs={{0,3},{1,2},{2,1},{3,0},{4,7},{5,6},{6,5},{7,4},{8,11},{9,10},{10,... | collective-permute-start | bytes 638984 | tf_op jit(solution)/shard_map/ppermute | solution.py:59
  30.5 2.1 %collective-permute-done.5 = bf16[32,3328]{1,0:T(8,128)(2,1)S(1)} collective-permute-done((bf16[32,3328]{1,0:T(8,128)(2,1)S(1)}, bf16[32,3328]{1,0:T(8,128)(2,1)S(1)}, u32[]{:S(2)}, u32[]{:S(2)}) %collective-permute-start.5) | collective-permute-done | bytes 213024 | tf_op jit(solution)/shard_map/ppermute | solution.py:59
  32.7 2.2 %collective-permute-done.9 = bf16[32,3328]{1,0:T(8,128)(2,1)S(1)} collective-permute-done((bf16[32,3328]{1,0:T(8,128)(2,1)S(1)}, bf16[32,3328]{1,0:T(8,128)(2,1)S(1)}, u32[]{:S(2)}, u32[]{:S(2)}) %collective-permute-start.9) | collective-permute-done | bytes 213024 | tf_op jit(solution)/shard_map/ppermute | solution.py:59
  36.7 3.3 %collective-permute-start.12 = (bf16[4,8,3328]{2,1,0:T(8,128)(2,1)S(1)}, bf16[4,8,3328]{2,1,0:T(8,128)(2,1)S(1)}, u32[]{:S(2)}, u32[]{:S(2)}) collective-permute-start(bf16[4,8,3328]{2,1,0:T(8,128)(2,1)S(1)} %get-tuple-element.27), channel_id=1, source_target_pairs={{0,8},{1,9},{2,10},{3,11},{4,12},{5,13},{6,14},{7,15},{8,0},{9,1},... | collective-permute-start | bytes 638984 | tf_op jit(solution)/shard_map/ppermute | solution.py:59
  42.1 2.0 %collective-permute-done.12 = bf16[4,8,3328]{2,1,0:T(8,128)(2,1)S(1)} collective-permute-done((bf16[4,8,3328]{2,1,0:T(8,128)(2,1)S(1)}, bf16[4,8,3328]{2,1,0:T(8,128)(2,1)S(1)}, u32[]{:S(2)}, u32[]{:S(2)}) %collective-permute-start.12) | collective-permute-done | bytes 213024 | tf_op jit(solution)/shard_map/ppermute | solution.py:59
  44.1 2.6 %collective-permute-done.14 = bf16[4,8,3328]{2,1,0:T(8,128)(2,1)S(1)} collective-permute-done((bf16[4,8,3328]{2,1,0:T(8,128)(2,1)S(1)}, bf16[4,8,3328]{2,1,0:T(8,128)(2,1)S(1)}, u32[]{:S(2)}, u32[]{:S(2)}) %collective-permute-start.14) | collective-permute-done | bytes 213024 | tf_op jit(solution)/shard_map/ppermute | solution.py:59
  48.4 2.8 %collective-permute-start.16 = (bf16[1,8,3328]{2,1,0:T(8,128)(2,1)S(1)}, bf16[1,8,3328]{2,1,0:T(8,128)(2,1)S(1)}, u32[]{:S(2)}, u32[]{:S(2)}) collective-permute-start(bf16[1,8,3328]{2,1,0:T(8,128)(2,1)S(1)} %get-tuple-element.23), channel_id=1, source_target_pairs={{0,8},{1,9},{2,10},{3,11},{4,12},{5,13},{6,14},{7,15},{8,0},{9,1},... | collective-permute-start | bytes 159752 | tf_op jit(solution)/shard_map/ppermute | solution.py:59
  52.5 1.7 %collective-permute-done.17 = bf16[1,8,3328]{2,1,0:T(8,128)(2,1)S(1)} collective-permute-done((bf16[1,8,3328]{2,1,0:T(8,128)(2,1)S(1)}, bf16[1,8,3328]{2,1,0:T(8,128)(2,1)S(1)}, u32[]{:S(2)}, u32[]{:S(2)}) %collective-permute-start.17) | collective-permute-done | bytes 53280 | tf_op jit(solution)/shard_map/ppermute | solution.py:59
  55.7 3.0 %collective-permute-start.19 = (bf16[1,32,3328]{2,1,0:T(8,128)(2,1)S(1)}, bf16[1,32,3328]{2,1,0:T(8,128)(2,1)S(1)}, u32[]{:S(2)}, u32[]{:S(2)}) collective-permute-start(bf16[1,32,3328]{2,1,0:T(8,128)(2,1)S(1)} %pad_maximum_fusion.2), channel_id=1, source_target_pairs={{0,2},{1,3},{2,0},{3,1},{4,6},{5,7},{6,4},{7,5},{8,10},{9,11},{10,... | collective-permute-start | bytes 638984 | tf_op jit(solution)/shard_map/ppermute | solution.py:59
  59.3 3.0 %collective-permute-start.21 = (bf16[2,8,3328]{2,1,0:T(8,128)(2,1)S(1)}, bf16[2,8,3328]{2,1,0:T(8,128)(2,1)S(1)}, u32[]{:S(2)}, u32[]{:S(2)}) collective-permute-start(bf16[2,8,3328]{2,1,0:T(8,128)(2,1)S(1)} %pad_maximum_fusion.4), channel_id=1, source_target_pairs={{0,4},{1,5},{2,6},{3,7},{4,0},{5,1},{6,2},{7,3},{8,12},{9,13},{10,... | collective-permute-start | bytes 319496 | tf_op jit(solution)/shard_map/ppermute | solution.py:59
  62.3 3.6 %collective-permute-done.18 = bf16[1,32,3328]{2,1,0:T(8,128)(2,1)S(1)} collective-permute-done((bf16[1,32,3328]{2,1,0:T(8,128)(2,1)S(1)}, bf16[1,32,3328]{2,1,0:T(8,128)(2,1)S(1)}, u32[]{:S(2)}, u32[]{:S(2)}) %collective-permute-start.18) | collective-permute-done | bytes 213024 | tf_op jit(solution)/shard_map/ppermute | solution.py:59
  66.9 2.3 %collective-permute-start.23 = (bf16[128,512]{1,0:T(8,128)(2,1)S(1)}, bf16[128,512]{1,0:T(8,128)(2,1)S(1)}, u32[]{:S(2)}, u32[]{:S(2)}) collective-permute-start(bf16[128,512]{1,0:T(8,128)(2,1)S(1)} %get-tuple-element.40), channel_id=1, source_target_pairs={{0,96},{1,97},{2,98},{3,99},{4,100},{5,101},{6,102},{7,103},{8,104... | collective-permute-start | bytes 393224 | tf_op jit(solution)/shard_map/ppermute | solution.py:59
  69.7 3.5 %collective-permute-done.24 = bf16[128,512]{1,0:T(8,128)(2,1)S(1)} collective-permute-done((bf16[128,512]{1,0:T(8,128)(2,1)S(1)}, bf16[128,512]{1,0:T(8,128)(2,1)S(1)}, u32[]{:S(2)}, u32[]{:S(2)}) %collective-permute-start.24) | collective-permute-done | bytes 131104 | tf_op jit(solution)/shard_map/ppermute | solution.py:59
  73.8 1.6 %collective-permute-done.22 = bf16[128,512]{1,0:T(8,128)(2,1)S(1)} collective-permute-done((bf16[128,512]{1,0:T(8,128)(2,1)S(1)}, bf16[128,512]{1,0:T(8,128)(2,1)S(1)}, u32[]{:S(2)}, u32[]{:S(2)}) %collective-permute-start.22) | collective-permute-done | bytes 131104 | tf_op jit(solution)/shard_map/ppermute | solution.py:59
  75.6 2.3 %collective-permute-start.32 = (bf16[2,16,3328]{2,1,0:T(8,128)(2,1)S(1)}, bf16[2,16,3328]{2,1,0:T(8,128)(2,1)S(1)}, u32[]{:S(2)}, u32[]{:S(2)}) collective-permute-start(bf16[2,16,3328]{2,1,0:T(8,128)(2,1)S(1)} %pad_maximum_fusion.3), channel_id=1, source_target_pairs={{0,12},{1,13},{2,14},{3,15},{4,8},{5,9},{6,10},{7,11},{8,4},{9,5},... | collective-permute-start | bytes 638984 | tf_op jit(solution)/shard_map/ppermute | solution.py:59
  80.6 2.1 %collective-permute-start.28 = (bf16[1,32,3328]{2,1,0:T(8,128)(2,1)S(1)}, bf16[1,32,3328]{2,1,0:T(8,128)(2,1)S(1)}, u32[]{:S(2)}, u32[]{:S(2)}) collective-permute-start(bf16[1,32,3328]{2,1,0:T(8,128)(2,1)S(1)} %get-tuple-element.25), channel_id=1, source_target_pairs={{0,3},{1,0},{2,1},{3,2},{4,7},{5,4},{6,5},{7,6},{8,11},{9,8},{10,9... | collective-permute-start | bytes 638984 | tf_op jit(solution)/shard_map/ppermute | solution.py:59
  82.9 3.8 %collective-permute-done.26 = bf16[1,32,3328]{2,1,0:T(8,128)(2,1)S(1)} collective-permute-done((bf16[1,32,3328]{2,1,0:T(8,128)(2,1)S(1)}, bf16[1,32,3328]{2,1,0:T(8,128)(2,1)S(1)}, u32[]{:S(2)}, u32[]{:S(2)}) %collective-permute-start.26) | collective-permute-done | bytes 213024 | tf_op jit(solution)/shard_map/ppermute | solution.py:59
  86.7 2.3 %collective-permute-done.28 = bf16[1,32,3328]{2,1,0:T(8,128)(2,1)S(1)} collective-permute-done((bf16[1,32,3328]{2,1,0:T(8,128)(2,1)S(1)}, bf16[1,32,3328]{2,1,0:T(8,128)(2,1)S(1)}, u32[]{:S(2)}, u32[]{:S(2)}) %collective-permute-start.28) | collective-permute-done | bytes 213024 | tf_op jit(solution)/shard_map/ppermute | solution.py:59
  92.0 2.5 %collective-permute-start.29 = (bf16[32,3328]{1,0:T(8,128)(2,1)S(1)}, bf16[32,3328]{1,0:T(8,128)(2,1)S(1)}, u32[]{:S(2)}, u32[]{:S(2)}) collective-permute-start(bf16[32,3328]{1,0:T(8,128)(2,1)S(1)} %convert_bitcast_fusion), channel_id=1, source_target_pairs={{0,8},{1,9},{2,10},{3,11},{4,12},{5,13},{6,14},{7,15},{8,0},{9,1},... | collective-permute-start | bytes 638984 | tf_op jit(solution)/shard_map/ppermute | solution.py:59
  95.8 5.0 %collective-permute-done.30 = bf16[32,3328]{1,0:T(8,128)(2,1)S(1)} collective-permute-done((bf16[32,3328]{1,0:T(8,128)(2,1)S(1)}, bf16[32,3328]{1,0:T(8,128)(2,1)S(1)}, u32[]{:S(2)}, u32[]{:S(2)}) %collective-permute-start.30) | collective-permute-done | bytes 213024 | tf_op jit(solution)/shard_map/ppermute | solution.py:59
  101.1 3.5 %collective-permute-start.37 = (bf16[1,32,3328]{2,1,0:T(8,128)(2,1)S(1)}, bf16[1,32,3328]{2,1,0:T(8,128)(2,1)S(1)}, u32[]{:S(2)}, u32[]{:S(2)}) collective-permute-start(bf16[1,32,3328]{2,1,0:T(8,128)(2,1)S(1)} %get-tuple-element.20), channel_id=1, source_target_pairs={{0,2},{1,3},{2,0},{3,1},{4,6},{5,7},{6,4},{7,5},{8,10},{9,11},{10,... | collective-permute-start | bytes 638984 | tf_op jit(solution)/shard_map/ppermute | solution.py:59
  105.0 1.8 %collective-permute-start.35 = (bf16[1,32,3328]{2,1,0:T(8,128)(2,1)S(1)}, bf16[1,32,3328]{2,1,0:T(8,128)(2,1)S(1)}, u32[]{:S(2)}, u32[]{:S(2)}) collective-permute-start(bf16[1,32,3328]{2,1,0:T(8,128)(2,1)S(1)} %multiply_convert_fusion.1), channel_id=1, source_target_pairs={{0,1},{1,2},{2,3},{3,0},{4,5},{5,6},{6,7},{7,4},{8,9},{9,10},{10,1... | collective-permute-start | bytes 638984 | tf_op jit(solution)/shard_map/ppermute | solution.py:59
  108.2 1.9 %collective-permute-start.33 = (bf16[1,32,3328]{2,1,0:T(8,128)(2,1)S(1)}, bf16[1,32,3328]{2,1,0:T(8,128)(2,1)S(1)}, u32[]{:S(2)}, u32[]{:S(2)}) collective-permute-start(bf16[1,32,3328]{2,1,0:T(8,128)(2,1)S(1)} %multiply_convert_fusion.1), channel_id=1, source_target_pairs={{0,3},{1,0},{2,1},{3,2},{4,7},{5,4},{6,5},{7,6},{8,11},{9,8},{10,9... | collective-permute-start | bytes 638984 | tf_op jit(solution)/shard_map/ppermute | solution.py:59
  111.4 2.2 %product.3 = bf16[512,3328]{1,0:T(8,128)(2,1)} custom-call(bf16[128,512]{1,0:T(8,128)(2,1)S(1)} %fusion.local_ref, bf16[128,3328]{1,0:T(8,128)(2,1)S(1)} %maximum_bitcast_fusion.1.cot_ref), custom_call_target="tpu_custom_call" | custom-call | tf_op jit(solution)/shard_map/product/pallas_call | solution.py:135
  113.6 1.8 %collective-permute-done.34 = bf16[1,32,3328]{2,1,0:T(8,128)(2,1)S(1)} collective-permute-done((bf16[1,32,3328]{2,1,0:T(8,128)(2,1)S(1)}, bf16[1,32,3328]{2,1,0:T(8,128)(2,1)S(1)}, u32[]{:S(2)}, u32[]{:S(2)}) %collective-permute-start.34) | collective-permute-done | bytes 213024 | tf_op jit(solution)/shard_map/ppermute | solution.py:59
  116.0 2.2 %product.2 = bf16[512,3328]{1,0:T(8,128)(2,1)} custom-call(bf16[128,512]{1,0:T(8,128)(2,1)S(1)} %fusion.local_ref, bf16[128,3328]{1,0:T(8,128)(2,1)S(1)} %maximum_bitcast_fusion.cot_ref), custom_call_target="tpu_custom_call" | custom-call | tf_op jit(solution)/shard_map/product/pallas_call | solution.py:135
  (127 shorter events, 35.6 us)
Async XLA Ops:
  0.6 10.5 %collective-permute-start.1 = (bf16[16,512]{1,0:T(8,128)(2,1)}, bf16[16,512]{1,0:T(8,128)(2,1)S(1)}, u32[]{:S(2)}, u32[]{:S(2)}) collective-permute-start(bf16[16,512]{1,0:T(8,128)(2,1)} %param.6), channel_id=1, source_target_pairs={{0,64},{1,65},{2,66},{3,67},{4,68},{5,69},{6,70},{7,71},{8,72},{9,... | collective-permute-start | bytes 49160 | tf_op jit(solution)/shard_map/ppermute | solution.py:59
  4.7 6.5 %collective-permute-start = (bf16[16,512]{1,0:T(8,128)(2,1)}, bf16[16,512]{1,0:T(8,128)(2,1)S(1)}, u32[]{:S(2)}, u32[]{:S(2)}) collective-permute-start(bf16[16,512]{1,0:T(8,128)(2,1)} %param.6), channel_id=1, source_target_pairs={{0,32},{1,33},{2,34},{3,35},{4,36},{5,37},{6,38},{7,39},{8,40},{9,... | collective-permute-start | bytes 49160 | tf_op jit(solution)/shard_map/ppermute | solution.py:59
  13.5 8.7 %collective-permute-start.4 = (bf16[64,3328]{1,0:T(8,128)(2,1)S(1)}, bf16[64,3328]{1,0:T(8,128)(2,1)S(1)}, u32[]{:S(2)}, u32[]{:S(2)}) collective-permute-start(bf16[64,3328]{1,0:T(8,128)(2,1)S(1)} %slice.281), channel_id=1, source_target_pairs={{0,1},{1,0},{2,3},{3,2},{4,5},{5,4},{6,7},{7,6},{8,9},{9,8},{10,11... | collective-permute-start | bytes 1277960 | tf_op jit(solution)/shard_map/ppermute | solution.py:59
  16.0 9.4 %collective-permute-start.6 = (bf16[64,3328]{1,0:T(8,128)(2,1)S(1)}, bf16[64,3328]{1,0:T(8,128)(2,1)S(1)}, u32[]{:S(2)}, u32[]{:S(2)}) collective-permute-start(bf16[64,3328]{1,0:T(8,128)(2,1)S(1)} %slice.280), channel_id=1, source_target_pairs={{0,3},{1,2},{2,1},{3,0},{4,7},{5,6},{6,5},{7,4},{8,11},{9,10},{10,... | collective-permute-start | bytes 1277960 | tf_op jit(solution)/shard_map/ppermute | solution.py:59
  19.0 8.2 %collective-permute-start.8 = (bf16[64,3328]{1,0:T(8,128)(2,1)S(1)}, bf16[64,3328]{1,0:T(8,128)(2,1)S(1)}, u32[]{:S(2)}, u32[]{:S(2)}) collective-permute-start(bf16[64,3328]{1,0:T(8,128)(2,1)S(1)} %slice.279), channel_id=1, source_target_pairs={{0,1},{1,0},{2,3},{3,2},{4,5},{5,4},{6,7},{7,6},{8,9},{9,8},{10,11... | collective-permute-start | bytes 1277960 | tf_op jit(solution)/shard_map/ppermute | solution.py:59
  20.9 9.4 %collective-permute-start.10 = (bf16[64,3328]{1,0:T(8,128)(2,1)S(1)}, bf16[64,3328]{1,0:T(8,128)(2,1)S(1)}, u32[]{:S(2)}, u32[]{:S(2)}) collective-permute-start(bf16[64,3328]{1,0:T(8,128)(2,1)S(1)} %slice.278), channel_id=1, source_target_pairs={{0,3},{1,2},{2,1},{3,0},{4,7},{5,6},{6,5},{7,4},{8,11},{9,10},{10,... | collective-permute-start | bytes 1277960 | tf_op jit(solution)/shard_map/ppermute | solution.py:59
  22.3 10.3 %collective-permute-start.5 = (bf16[32,3328]{1,0:T(8,128)(2,1)S(1)}, bf16[32,3328]{1,0:T(8,128)(2,1)S(1)}, u32[]{:S(2)}, u32[]{:S(2)}) collective-permute-start(bf16[32,3328]{1,0:T(8,128)(2,1)S(1)} %slice.285), channel_id=1, source_target_pairs={{0,3},{1,2},{2,1},{3,0},{4,7},{5,6},{6,5},{7,4},{8,11},{9,10},{10,... | collective-permute-start | bytes 638984 | tf_op jit(solution)/shard_map/ppermute | solution.py:59
  25.5 7.1 %collective-permute-start.7 = (bf16[32,3328]{1,0:T(8,128)(2,1)S(1)}, bf16[32,3328]{1,0:T(8,128)(2,1)S(1)}, u32[]{:S(2)}, u32[]{:S(2)}) collective-permute-start(bf16[32,3328]{1,0:T(8,128)(2,1)S(1)} %slice.284), channel_id=1, source_target_pairs={{0,1},{1,0},{2,3},{3,2},{4,5},{5,4},{6,7},{7,6},{8,9},{9,8},{10,11... | collective-permute-start | bytes 638984 | tf_op jit(solution)/shard_map/ppermute | solution.py:59
  27.3 7.6 %collective-permute-start.9 = (bf16[32,3328]{1,0:T(8,128)(2,1)S(1)}, bf16[32,3328]{1,0:T(8,128)(2,1)S(1)}, u32[]{:S(2)}, u32[]{:S(2)}) collective-permute-start(bf16[32,3328]{1,0:T(8,128)(2,1)S(1)} %slice.283), channel_id=1, source_target_pairs={{0,3},{1,2},{2,1},{3,0},{4,7},{5,6},{6,5},{7,4},{8,11},{9,10},{10,... | collective-permute-start | bytes 638984 | tf_op jit(solution)/shard_map/ppermute | solution.py:59
  36.7 7.4 %collective-permute-start.12 = (bf16[4,8,3328]{2,1,0:T(8,128)(2,1)S(1)}, bf16[4,8,3328]{2,1,0:T(8,128)(2,1)S(1)}, u32[]{:S(2)}, u32[]{:S(2)}) collective-permute-start(bf16[4,8,3328]{2,1,0:T(8,128)(2,1)S(1)} %get-tuple-element.27), channel_id=1, source_target_pairs={{0,8},{1,9},{2,10},{3,11},{4,12},{5,13},{6,14},{7,15},{8,0},{9,1},... | collective-permute-start | bytes 638984 | tf_op jit(solution)/shard_map/ppermute | solution.py:59
  40.0 6.8 %collective-permute-start.14 = (bf16[4,8,3328]{2,1,0:T(8,128)(2,1)S(1)}, bf16[4,8,3328]{2,1,0:T(8,128)(2,1)S(1)}, u32[]{:S(2)}, u32[]{:S(2)}) collective-permute-start(bf16[4,8,3328]{2,1,0:T(8,128)(2,1)S(1)} %get-tuple-element.28), channel_id=1, source_target_pairs={{0,12},{1,13},{2,14},{3,15},{4,0},{5,1},{6,2},{7,3},{8,4},{9,5},{1... | collective-permute-start | bytes 638984 | tf_op jit(solution)/shard_map/ppermute | solution.py:59
  41.0 7.1 %collective-permute-start.13 = (bf16[4,8,3328]{2,1,0:T(8,128)(2,1)S(1)}, bf16[4,8,3328]{2,1,0:T(8,128)(2,1)S(1)}, u32[]{:S(2)}, u32[]{:S(2)}) collective-permute-start(bf16[4,8,3328]{2,1,0:T(8,128)(2,1)S(1)} %get-tuple-element.29), channel_id=1, source_target_pairs={{0,4},{1,5},{2,6},{3,7},{4,8},{5,9},{6,10},{7,11},{8,12},{9,13},{1... | collective-permute-start | bytes 638984 | tf_op jit(solution)/shard_map/ppermute | solution.py:59
  48.3 6.0 %collective-permute-start.17 = (bf16[1,8,3328]{2,1,0:T(8,128)(2,1)S(1)}, bf16[1,8,3328]{2,1,0:T(8,128)(2,1)S(1)}, u32[]{:S(2)}, u32[]{:S(2)}) collective-permute-start(bf16[1,8,3328]{2,1,0:T(8,128)(2,1)S(1)} %get-tuple-element.23), channel_id=1, source_target_pairs={{0,4},{1,5},{2,6},{3,7},{4,8},{5,9},{6,10},{7,11},{8,12},{9,13},{1... | collective-permute-start | bytes 159752 | tf_op jit(solution)/shard_map/ppermute | solution.py:59
  55.6 10.4 %collective-permute-start.20 = (bf16[1,32,3328]{2,1,0:T(8,128)(2,1)S(1)}, bf16[1,32,3328]{2,1,0:T(8,128)(2,1)S(1)}, u32[]{:S(2)}, u32[]{:S(2)}) collective-permute-start(bf16[1,32,3328]{2,1,0:T(8,128)(2,1)S(1)} %pad_maximum_fusion.2), channel_id=1, source_target_pairs={{0,1},{1,2},{2,3},{3,0},{4,5},{5,6},{6,7},{7,4},{8,9},{9,10},{10,1... | collective-permute-start | bytes 638984 | tf_op jit(solution)/shard_map/ppermute | solution.py:59
  55.7 10.2 %collective-permute-start.19 = (bf16[1,32,3328]{2,1,0:T(8,128)(2,1)S(1)}, bf16[1,32,3328]{2,1,0:T(8,128)(2,1)S(1)}, u32[]{:S(2)}, u32[]{:S(2)}) collective-permute-start(bf16[1,32,3328]{2,1,0:T(8,128)(2,1)S(1)} %pad_maximum_fusion.2), channel_id=1, source_target_pairs={{0,2},{1,3},{2,0},{3,1},{4,6},{5,7},{6,4},{7,5},{8,10},{9,11},{10,... | collective-permute-start | bytes 638984 | tf_op jit(solution)/shard_map/ppermute | solution.py:59
  58.7 7.3 %collective-permute-start.18 = (bf16[1,32,3328]{2,1,0:T(8,128)(2,1)S(1)}, bf16[1,32,3328]{2,1,0:T(8,128)(2,1)S(1)}, u32[]{:S(2)}, u32[]{:S(2)}) collective-permute-start(bf16[1,32,3328]{2,1,0:T(8,128)(2,1)S(1)} %pad_maximum_fusion.2), channel_id=1, source_target_pairs={{0,3},{1,0},{2,1},{3,2},{4,7},{5,4},{6,5},{7,6},{8,11},{9,8},{10,9... | collective-permute-start | bytes 638984 | tf_op jit(solution)/shard_map/ppermute | solution.py:59
  59.3 6.7 %collective-permute-start.21 = (bf16[2,8,3328]{2,1,0:T(8,128)(2,1)S(1)}, bf16[2,8,3328]{2,1,0:T(8,128)(2,1)S(1)}, u32[]{:S(2)}, u32[]{:S(2)}) collective-permute-start(bf16[2,8,3328]{2,1,0:T(8,128)(2,1)S(1)} %pad_maximum_fusion.4), channel_id=1, source_target_pairs={{0,4},{1,5},{2,6},{3,7},{4,0},{5,1},{6,2},{7,3},{8,12},{9,13},{10,... | collective-permute-start | bytes 319496 | tf_op jit(solution)/shard_map/ppermute | solution.py:59
  66.7 6.6 %collective-permute-start.24 = (bf16[128,512]{1,0:T(8,128)(2,1)S(1)}, bf16[128,512]{1,0:T(8,128)(2,1)S(1)}, u32[]{:S(2)}, u32[]{:S(2)}) collective-permute-start(bf16[128,512]{1,0:T(8,128)(2,1)S(1)} %get-tuple-element.40), channel_id=1, source_target_pairs={{0,64},{1,65},{2,66},{3,67},{4,68},{5,69},{6,70},{7,71},{8,72},{9,... | collective-permute-start | bytes 393224 | tf_op jit(solution)/shard_map/ppermute | solution.py:59
  66.9 6.9 %collective-permute-start.23 = (bf16[128,512]{1,0:T(8,128)(2,1)S(1)}, bf16[128,512]{1,0:T(8,128)(2,1)S(1)}, u32[]{:S(2)}, u32[]{:S(2)}) collective-permute-start(bf16[128,512]{1,0:T(8,128)(2,1)S(1)} %get-tuple-element.40), channel_id=1, source_target_pairs={{0,96},{1,97},{2,98},{3,99},{4,100},{5,101},{6,102},{7,103},{8,104... | collective-permute-start | bytes 393224 | tf_op jit(solution)/shard_map/ppermute | solution.py:59
  69.2 6.2 %collective-permute-start.22 = (bf16[128,512]{1,0:T(8,128)(2,1)S(1)}, bf16[128,512]{1,0:T(8,128)(2,1)S(1)}, u32[]{:S(2)}, u32[]{:S(2)}) collective-permute-start(bf16[128,512]{1,0:T(8,128)(2,1)S(1)} %get-tuple-element.40), channel_id=1, source_target_pairs={{0,32},{1,33},{2,34},{3,35},{4,36},{5,37},{6,38},{7,39},{8,40},{9,... | collective-permute-start | bytes 393224 | tf_op jit(solution)/shard_map/ppermute | solution.py:59
  75.6 7.3 %collective-permute-start.32 = (bf16[2,16,3328]{2,1,0:T(8,128)(2,1)S(1)}, bf16[2,16,3328]{2,1,0:T(8,128)(2,1)S(1)}, u32[]{:S(2)}, u32[]{:S(2)}) collective-permute-start(bf16[2,16,3328]{2,1,0:T(8,128)(2,1)S(1)} %pad_maximum_fusion.3), channel_id=1, source_target_pairs={{0,12},{1,13},{2,14},{3,15},{4,8},{5,9},{6,10},{7,11},{8,4},{9,5},... | collective-permute-start | bytes 638984 | tf_op jit(solution)/shard_map/ppermute | solution.py:59
  79.3 7.4 %collective-permute-start.26 = (bf16[1,32,3328]{2,1,0:T(8,128)(2,1)S(1)}, bf16[1,32,3328]{2,1,0:T(8,128)(2,1)S(1)}, u32[]{:S(2)}, u32[]{:S(2)}) collective-permute-start(bf16[1,32,3328]{2,1,0:T(8,128)(2,1)S(1)} %get-tuple-element.24), channel_id=1, source_target_pairs={{0,2},{1,3},{2,0},{3,1},{4,6},{5,7},{6,4},{7,5},{8,10},{9,11},{10,... | collective-permute-start | bytes 638984 | tf_op jit(solution)/shard_map/ppermute | solution.py:59
  80.6 8.4 %collective-permute-start.28 = (bf16[1,32,3328]{2,1,0:T(8,128)(2,1)S(1)}, bf16[1,32,3328]{2,1,0:T(8,128)(2,1)S(1)}, u32[]{:S(2)}, u32[]{:S(2)}) collective-permute-start(bf16[1,32,3328]{2,1,0:T(8,128)(2,1)S(1)} %get-tuple-element.25), channel_id=1, source_target_pairs={{0,3},{1,0},{2,1},{3,2},{4,7},{5,4},{6,5},{7,6},{8,11},{9,8},{10,9... | collective-permute-start | bytes 638984 | tf_op jit(solution)/shard_map/ppermute | solution.py:59
  82.6 7.1 %collective-permute-start.27 = (bf16[1,32,3328]{2,1,0:T(8,128)(2,1)S(1)}, bf16[1,32,3328]{2,1,0:T(8,128)(2,1)S(1)}, u32[]{:S(2)}, u32[]{:S(2)}) collective-permute-start(bf16[1,32,3328]{2,1,0:T(8,128)(2,1)S(1)} %get-tuple-element.26), channel_id=1, source_target_pairs={{0,1},{1,2},{2,3},{3,0},{4,5},{5,6},{6,7},{7,4},{8,9},{9,10},{10,1... | collective-permute-start | bytes 638984 | tf_op jit(solution)/shard_map/ppermute | solution.py:59
  91.3 9.4 %collective-permute-start.30 = (bf16[32,3328]{1,0:T(8,128)(2,1)S(1)}, bf16[32,3328]{1,0:T(8,128)(2,1)S(1)}, u32[]{:S(2)}, u32[]{:S(2)}) collective-permute-start(bf16[32,3328]{1,0:T(8,128)(2,1)S(1)} %convert_bitcast_fusion), channel_id=1, source_target_pairs={{0,4},{1,5},{2,6},{3,7},{4,8},{5,9},{6,10},{7,11},{8,12},{9,13},{1... | collective-permute-start | bytes 638984 | tf_op jit(solution)/shard_map/ppermute | solution.py:59
  92.0 8.8 %collective-permute-start.29 = (bf16[32,3328]{1,0:T(8,128)(2,1)S(1)}, bf16[32,3328]{1,0:T(8,128)(2,1)S(1)}, u32[]{:S(2)}, u32[]{:S(2)}) collective-permute-start(bf16[32,3328]{1,0:T(8,128)(2,1)S(1)} %convert_bitcast_fusion), channel_id=1, source_target_pairs={{0,8},{1,9},{2,10},{3,11},{4,12},{5,13},{6,14},{7,15},{8,0},{9,1},... | collective-permute-start | bytes 638984 | tf_op jit(solution)/shard_map/ppermute | solution.py:59
  101.0 7.1 %collective-permute-start.38 = (bf16[1,32,3328]{2,1,0:T(8,128)(2,1)S(1)}, bf16[1,32,3328]{2,1,0:T(8,128)(2,1)S(1)}, u32[]{:S(2)}, u32[]{:S(2)}) collective-permute-start(bf16[1,32,3328]{2,1,0:T(8,128)(2,1)S(1)} %get-tuple-element.20), channel_id=1, source_target_pairs={{0,1},{1,2},{2,3},{3,0},{4,5},{5,6},{6,7},{7,4},{8,9},{9,10},{10,1... | collective-permute-start | bytes 638984 | tf_op jit(solution)/shard_map/ppermute | solution.py:59
  101.1 9.7 %collective-permute-start.37 = (bf16[1,32,3328]{2,1,0:T(8,128)(2,1)S(1)}, bf16[1,32,3328]{2,1,0:T(8,128)(2,1)S(1)}, u32[]{:S(2)}, u32[]{:S(2)}) collective-permute-start(bf16[1,32,3328]{2,1,0:T(8,128)(2,1)S(1)} %get-tuple-element.20), channel_id=1, source_target_pairs={{0,2},{1,3},{2,0},{3,1},{4,6},{5,7},{6,4},{7,5},{8,10},{9,11},{10,... | collective-permute-start | bytes 638984 | tf_op jit(solution)/shard_map/ppermute | solution.py:59
  104.7 6.7 %collective-permute-start.36 = (bf16[1,32,3328]{2,1,0:T(8,128)(2,1)S(1)}, bf16[1,32,3328]{2,1,0:T(8,128)(2,1)S(1)}, u32[]{:S(2)}, u32[]{:S(2)}) collective-permute-start(bf16[1,32,3328]{2,1,0:T(8,128)(2,1)S(1)} %get-tuple-element.20), channel_id=1, source_target_pairs={{0,3},{1,0},{2,1},{3,2},{4,7},{5,4},{6,5},{7,6},{8,11},{9,8},{10,9... | collective-permute-start | bytes 638984 | tf_op jit(solution)/shard_map/ppermute | solution.py:59
  105.0 8.6 %collective-permute-start.35 = (bf16[1,32,3328]{2,1,0:T(8,128)(2,1)S(1)}, bf16[1,32,3328]{2,1,0:T(8,128)(2,1)S(1)}, u32[]{:S(2)}, u32[]{:S(2)}) collective-permute-start(bf16[1,32,3328]{2,1,0:T(8,128)(2,1)S(1)} %multiply_convert_fusion.1), channel_id=1, source_target_pairs={{0,1},{1,2},{2,3},{3,0},{4,5},{5,6},{6,7},{7,4},{8,9},{9,10},{10,1... | collective-permute-start | bytes 638984 | tf_op jit(solution)/shard_map/ppermute | solution.py:59
  106.8 8.5 %collective-permute-start.34 = (bf16[1,32,3328]{2,1,0:T(8,128)(2,1)S(1)}, bf16[1,32,3328]{2,1,0:T(8,128)(2,1)S(1)}, u32[]{:S(2)}, u32[]{:S(2)}) collective-permute-start(bf16[1,32,3328]{2,1,0:T(8,128)(2,1)S(1)} %multiply_convert_fusion.1), channel_id=1, source_target_pairs={{0,2},{1,3},{2,0},{3,1},{4,6},{5,7},{6,4},{7,5},{8,10},{9,11},{10,... | collective-permute-start | bytes 638984 | tf_op jit(solution)/shard_map/ppermute | solution.py:59
  108.2 7.8 %collective-permute-start.33 = (bf16[1,32,3328]{2,1,0:T(8,128)(2,1)S(1)}, bf16[1,32,3328]{2,1,0:T(8,128)(2,1)S(1)}, u32[]{:S(2)}, u32[]{:S(2)}) collective-permute-start(bf16[1,32,3328]{2,1,0:T(8,128)(2,1)S(1)} %multiply_convert_fusion.1), channel_id=1, source_target_pairs={{0,3},{1,0},{2,1},{3,2},{4,7},{5,4},{6,5},{7,6},{8,11},{9,8},{10,9... | collective-permute-start | bytes 638984 | tf_op jit(solution)/shard_map/ppermute | solution.py:59
  (13 other events, 63.1 us)

commit v7 on v6

--- a/solution.py
+++ b/solution.py
@@ -33,11 +33,11 @@
 
 
 def along_first(move):
-    return pairs(lambda z, k, y, x: (z, k, y, move(x)) if k == 0 else (z, k, move(y), x))
+    return pairs(lambda z, k, y, x: (z, k, y, move(x)) if k == 0 else (z, k, -move(-y & 3), x))
 
 
 def along_second(move):
-    return pairs(lambda z, k, y, x: (z, k, move(y), x) if k == 0 else (z, k, y, move(x)))
+    return pairs(lambda z, k, y, x: (z, k, move(y), x) if k == 0 else (z, k, y, -move(-x & 3)))
 
 
 CORE = pairs(lambda z, k, y, x: (z, 1 - k, y, x))
@@ -77,8 +77,8 @@
     first = jnp.where(
         block == 1, offsets[1], jnp.where(block == 2, offsets[2], jnp.where(block == 3, offsets[3], offsets[0]))
     )
-    high = (x + jnp.where(k == 0, first, second)) & 3
-    low = (y + jnp.where(k == 0, second, first)) & 3
+    high = (x + jnp.where(k == 0, first, -second)) & 3
+    low = (y + jnp.where(k == 0, second, -first)) & 3
     token = (high * 4 + low) * 8 + local % 8
     place = ((token // 16 & 1) ^ k) * 64 + ((z - token // 32) & 3) * 16 + token % 16
     return (place == column).astype(BF)
@@ -193,7 +193,9 @@
 
 
 def swap_axes(value):
-    return value.reshape(4, 4, 8, -1).swapaxes(0, 1).reshape(value.shape)
+    blocks = value.reshape(4, 4, 8, -1)
+    back = (0, 3, 2, 1)
+    return jnp.concatenate([blocks[i, j] for j in back for i in back])
 
 
 def sum_rows(part, factors, next_, even):
@@ -201,7 +203,7 @@
     got = [send(rounded, z_shift(d)) for d in (1, 3, 2)]
     factors = gather_second_pairs(factors, after(next_, part), even)
     chips = part + got[0] + got[1] + got[2]
-    return chips + swap_axes(send(chips, CORE)), factors[0], factors[1]
+    return chips + swap_axes(send(chips.astype(BF), CORE)), factors[0], factors[1]
 
 
 def body(tokens, gate_weight, up_weight, down_weight, gate_tangent, up_tangent):

time: 119 us -> 119 us (level)
  starting transfers between devices: 55.2 us -> 53.3 us
  waiting for transfers between devices: 45.7 us -> 47.6 us
    ppermute x39, starting transfers between devices: 55.2 us -> 53.3 us  [send(): return lax.ppermute(value, RC, to)]
    ppermute x39, waiting for transfers between devices: 45.7 us -> 47.6 us  [send(): return lax.ppermute(value, RC, to)]
    unnamed x17 -> x32, local copies, waits for them, and re-layouts: 2.83 us -> 2.87 us
where the time goes in v7:
time: 119 us; the launch traced here: 118 us
  starting transfers between devices  53.3 us (45%)
  waiting for transfers between devices  47.6 us (40%)
  matrix products  5.49 us (5%)
  Pallas kernels  4.89 us (4%)
  local copies, waits for them, and re-layouts  3.31 us (3%)
  other arithmetic  2.22 us (2%)
  between operations  1.52 us (1%)
    ppermute x39, starting transfers between devices, send(): return lax.ppermute(value, RC, to)  53.3 us
    ppermute x39, waiting for transfers between devices, send(): return lax.ppermute(value, RC, to)  47.6 us
    dot_general x12, matrix products, matmul(): return jnp.dot(left, right, preferred_element_type=F32)  5.49 us
    pallas_call x2, Pallas kernels, product(): pl.pallas_call(kernel, out_shape=jax.ShapeDtypeStruct((features, width),...  4.31 us
    unnamed x32, local copies, waits for them, and re-layouts  2.87 us
  transfers between devices with their start and end apart: 39, of which 26 were waited for; matrix products, arithmetic and copies ran while one was open for 5% of the time, Pallas kernels for 2%

profile of v7, /device:TPU:0, one launch (start us, length us, event | category | flops | bytes accessed | tf_op | source)
XLA Modules:
  0.0 118.3 jit_solution(11503331939382807571)
XLA Ops:
  0.6 4.0 %collective-permute-start.1 = (bf16[16,512]{1,0:T(8,128)(2,1)}, bf16[16,512]{1,0:T(8,128)(2,1)S(1)}, u32[]{:S(2)}, u32[]{:S(2)}) collective-permute-start(bf16[16,512]{1,0:T(8,128)(2,1)} %param.6), channel_id=1, source_target_pairs={{0,64},{1,65},{2,66},{3,67},{4,68},{5,69},{6,70},{7,71},{8,72},{9,... | collective-permute-start | bytes 49160 | tf_op jit(solution)/shard_map/ppermute | solution.py:59
  5.7 2.2 %collective-permute-start.2 = (bf16[16,512]{1,0:T(8,128)(2,1)}, bf16[16,512]{1,0:T(8,128)(2,1)S(1)}, u32[]{:S(2)}, u32[]{:S(2)}) collective-permute-start(bf16[16,512]{1,0:T(8,128)(2,1)} %param.6), channel_id=1, source_target_pairs={{0,96},{1,97},{2,98},{3,99},{4,100},{5,101},{6,102},{7,103},{8,104... | collective-permute-start | bytes 49160 | tf_op jit(solution)/shard_map/ppermute | solution.py:59
  8.6 2.0 %copy-done.1 = bf16[512,3328]{1,0:T(8,128)(2,1)S(1)} copy-done((bf16[512,3328]{1,0:T(8,128)(2,1)S(1)}, bf16[512,3328]{1,0:T(8,128)(2,1)}, u32[]{:S(2)}) %copy-start.1) | copy-done | bytes 3407896
  13.5 1.6 %collective-permute-start.4 = (bf16[64,3328]{1,0:T(8,128)(2,1)S(1)}, bf16[64,3328]{1,0:T(8,128)(2,1)S(1)}, u32[]{:S(2)}, u32[]{:S(2)}) collective-permute-start(bf16[64,3328]{1,0:T(8,128)(2,1)S(1)} %slice.409), channel_id=1, source_target_pairs={{0,1},{1,0},{2,3},{3,2},{4,5},{5,4},{6,7},{7,6},{8,9},{9,8},{10,11... | collective-permute-start | bytes 1277960 | tf_op jit(solution)/shard_map/ppermute | solution.py:59
  16.0 2.3 %collective-permute-start.6 = (bf16[64,3328]{1,0:T(8,128)(2,1)S(1)}, bf16[64,3328]{1,0:T(8,128)(2,1)S(1)}, u32[]{:S(2)}, u32[]{:S(2)}) collective-permute-start(bf16[64,3328]{1,0:T(8,128)(2,1)S(1)} %slice.408), channel_id=1, source_target_pairs={{0,3},{1,2},{2,1},{3,0},{4,7},{5,6},{6,5},{7,4},{8,11},{9,10},{10,... | collective-permute-start | bytes 1277960 | tf_op jit(solution)/shard_map/ppermute | solution.py:59
  22.3 2.3 %collective-permute-start.5 = (bf16[32,3328]{1,0:T(8,128)(2,1)S(1)}, bf16[32,3328]{1,0:T(8,128)(2,1)S(1)}, u32[]{:S(2)}, u32[]{:S(2)}) collective-permute-start(bf16[32,3328]{1,0:T(8,128)(2,1)S(1)} %slice.413), channel_id=1, source_target_pairs={{0,3},{1,2},{2,1},{3,0},{4,7},{5,6},{6,5},{7,4},{8,11},{9,10},{10,... | collective-permute-start | bytes 638984 | tf_op jit(solution)/shard_map/ppermute | solution.py:59
  25.6 1.6 %collective-permute-done.8 = bf16[64,3328]{1,0:T(8,128)(2,1)S(1)} collective-permute-done((bf16[64,3328]{1,0:T(8,128)(2,1)S(1)}, bf16[64,3328]{1,0:T(8,128)(2,1)S(1)}, u32[]{:S(2)}, u32[]{:S(2)}) %collective-permute-start.8) | collective-permute-done | bytes 426016 | tf_op jit(solution)/shard_map/ppermute | solution.py:59
  27.3 1.9 %collective-permute-start.9 = (bf16[32,3328]{1,0:T(8,128)(2,1)S(1)}, bf16[32,3328]{1,0:T(8,128)(2,1)S(1)}, u32[]{:S(2)}, u32[]{:S(2)}) collective-permute-start(bf16[32,3328]{1,0:T(8,128)(2,1)S(1)} %slice.411), channel_id=1, source_target_pairs={{0,3},{1,2},{2,1},{3,0},{4,7},{5,6},{6,5},{7,4},{8,11},{9,10},{10,... | collective-permute-start | bytes 638984 | tf_op jit(solution)/shard_map/ppermute | solution.py:59
  30.6 2.1 %collective-permute-done.5 = bf16[32,3328]{1,0:T(8,128)(2,1)S(1)} collective-permute-done((bf16[32,3328]{1,0:T(8,128)(2,1)S(1)}, bf16[32,3328]{1,0:T(8,128)(2,1)S(1)}, u32[]{:S(2)}, u32[]{:S(2)}) %collective-permute-start.5) | collective-permute-done | bytes 213024 | tf_op jit(solution)/shard_map/ppermute | solution.py:59
  32.7 2.2 %collective-permute-done.9 = bf16[32,3328]{1,0:T(8,128)(2,1)S(1)} collective-permute-done((bf16[32,3328]{1,0:T(8,128)(2,1)S(1)}, bf16[32,3328]{1,0:T(8,128)(2,1)S(1)}, u32[]{:S(2)}, u32[]{:S(2)}) %collective-permute-start.9) | collective-permute-done | bytes 213024 | tf_op jit(solution)/shard_map/ppermute | solution.py:59
  36.7 3.3 %collective-permute-start.12 = (bf16[4,8,3328]{2,1,0:T(8,128)(2,1)S(1)}, bf16[4,8,3328]{2,1,0:T(8,128)(2,1)S(1)}, u32[]{:S(2)}, u32[]{:S(2)}) collective-permute-start(bf16[4,8,3328]{2,1,0:T(8,128)(2,1)S(1)} %get-tuple-element.27), channel_id=1, source_target_pairs={{0,8},{1,9},{2,10},{3,11},{4,12},{5,13},{6,14},{7,15},{8,0},{9,1},... | collective-permute-start | bytes 638984 | tf_op jit(solution)/shard_map/ppermute | solution.py:59
  42.1 2.0 %collective-permute-done.12 = bf16[4,8,3328]{2,1,0:T(8,128)(2,1)S(1)} collective-permute-done((bf16[4,8,3328]{2,1,0:T(8,128)(2,1)S(1)}, bf16[4,8,3328]{2,1,0:T(8,128)(2,1)S(1)}, u32[]{:S(2)}, u32[]{:S(2)}) %collective-permute-start.12) | collective-permute-done | bytes 213024 | tf_op jit(solution)/shard_map/ppermute | solution.py:59
  44.1 2.6 %collective-permute-done.14 = bf16[4,8,3328]{2,1,0:T(8,128)(2,1)S(1)} collective-permute-done((bf16[4,8,3328]{2,1,0:T(8,128)(2,1)S(1)}, bf16[4,8,3328]{2,1,0:T(8,128)(2,1)S(1)}, u32[]{:S(2)}, u32[]{:S(2)}) %collective-permute-start.14) | collective-permute-done | bytes 213024 | tf_op jit(solution)/shard_map/ppermute | solution.py:59
  48.4 2.8 %collective-permute-start.16 = (bf16[1,8,3328]{2,1,0:T(8,128)(2,1)S(1)}, bf16[1,8,3328]{2,1,0:T(8,128)(2,1)S(1)}, u32[]{:S(2)}, u32[]{:S(2)}) collective-permute-start(bf16[1,8,3328]{2,1,0:T(8,128)(2,1)S(1)} %get-tuple-element.23), channel_id=1, source_target_pairs={{0,8},{1,9},{2,10},{3,11},{4,12},{5,13},{6,14},{7,15},{8,0},{9,1},... | collective-permute-start | bytes 159752 | tf_op jit(solution)/shard_map/ppermute | solution.py:59
  52.5 1.7 %collective-permute-done.17 = bf16[1,8,3328]{2,1,0:T(8,128)(2,1)S(1)} collective-permute-done((bf16[1,8,3328]{2,1,0:T(8,128)(2,1)S(1)}, bf16[1,8,3328]{2,1,0:T(8,128)(2,1)S(1)}, u32[]{:S(2)}, u32[]{:S(2)}) %collective-permute-start.17) | collective-permute-done | bytes 53280 | tf_op jit(solution)/shard_map/ppermute | solution.py:59
  56.0 3.7 %collective-permute-start.19 = (bf16[1,32,3328]{2,1,0:T(8,128)(2,1)S(1)}, bf16[1,32,3328]{2,1,0:T(8,128)(2,1)S(1)}, u32[]{:S(2)}, u32[]{:S(2)}) collective-permute-start(bf16[1,32,3328]{2,1,0:T(8,128)(2,1)S(1)} %pad_maximum_fusion.2), channel_id=1, source_target_pairs={{0,2},{1,3},{2,0},{3,1},{4,6},{5,7},{6,4},{7,5},{8,10},{9,11},{10,... | collective-permute-start | bytes 638984 | tf_op jit(solution)/shard_map/ppermute | solution.py:59
  61.2 4.6 %collective-permute-done.18 = bf16[1,32,3328]{2,1,0:T(8,128)(2,1)S(1)} collective-permute-done((bf16[1,32,3328]{2,1,0:T(8,128)(2,1)S(1)}, bf16[1,32,3328]{2,1,0:T(8,128)(2,1)S(1)}, u32[]{:S(2)}, u32[]{:S(2)}) %collective-permute-start.18) | collective-permute-done | bytes 213024 | tf_op jit(solution)/shard_map/ppermute | solution.py:59
  66.8 2.4 %collective-permute-start.23 = (bf16[128,512]{1,0:T(8,128)(2,1)S(1)}, bf16[128,512]{1,0:T(8,128)(2,1)S(1)}, u32[]{:S(2)}, u32[]{:S(2)}) collective-permute-start(bf16[128,512]{1,0:T(8,128)(2,1)S(1)} %get-tuple-element.40), channel_id=1, source_target_pairs={{0,96},{1,97},{2,98},{3,99},{4,100},{5,101},{6,102},{7,103},{8,104... | collective-permute-start | bytes 393224 | tf_op jit(solution)/shard_map/ppermute | solution.py:59
  69.6 3.5 %collective-permute-done.24 = bf16[128,512]{1,0:T(8,128)(2,1)S(1)} collective-permute-done((bf16[128,512]{1,0:T(8,128)(2,1)S(1)}, bf16[128,512]{1,0:T(8,128)(2,1)S(1)}, u32[]{:S(2)}, u32[]{:S(2)}) %collective-permute-start.24) | collective-permute-done | bytes 131104 | tf_op jit(solution)/shard_map/ppermute | solution.py:59
  73.7 1.6 %collective-permute-done.22 = bf16[128,512]{1,0:T(8,128)(2,1)S(1)} collective-permute-done((bf16[128,512]{1,0:T(8,128)(2,1)S(1)}, bf16[128,512]{1,0:T(8,128)(2,1)S(1)}, u32[]{:S(2)}, u32[]{:S(2)}) %collective-permute-start.22) | collective-permute-done | bytes 131104 | tf_op jit(solution)/shard_map/ppermute | solution.py:59
  75.5 2.5 %collective-permute-start.32 = (bf16[2,16,3328]{2,1,0:T(8,128)(2,1)S(1)}, bf16[2,16,3328]{2,1,0:T(8,128)(2,1)S(1)}, u32[]{:S(2)}, u32[]{:S(2)}) collective-permute-start(bf16[2,16,3328]{2,1,0:T(8,128)(2,1)S(1)} %pad_maximum_fusion.3), channel_id=1, source_target_pairs={{0,12},{1,13},{2,14},{3,15},{4,8},{5,9},{6,10},{7,11},{8,4},{9,5},... | collective-permute-start | bytes 638984 | tf_op jit(solution)/shard_map/ppermute | solution.py:59
  80.8 2.1 %collective-permute-start.28 = (bf16[1,32,3328]{2,1,0:T(8,128)(2,1)S(1)}, bf16[1,32,3328]{2,1,0:T(8,128)(2,1)S(1)}, u32[]{:S(2)}, u32[]{:S(2)}) collective-permute-start(bf16[1,32,3328]{2,1,0:T(8,128)(2,1)S(1)} %get-tuple-element.25), channel_id=1, source_target_pairs={{0,3},{1,0},{2,1},{3,2},{4,7},{5,4},{6,5},{7,6},{8,11},{9,8},{10,9... | collective-permute-start | bytes 638984 | tf_op jit(solution)/shard_map/ppermute | solution.py:59
  83.1 3.8 %collective-permute-done.26 = bf16[1,32,3328]{2,1,0:T(8,128)(2,1)S(1)} collective-permute-done((bf16[1,32,3328]{2,1,0:T(8,128)(2,1)S(1)}, bf16[1,32,3328]{2,1,0:T(8,128)(2,1)S(1)}, u32[]{:S(2)}, u32[]{:S(2)}) %collective-permute-start.26) | collective-permute-done | bytes 213024 | tf_op jit(solution)/shard_map/ppermute | solution.py:59
  86.9 2.3 %collective-permute-done.28 = bf16[1,32,3328]{2,1,0:T(8,128)(2,1)S(1)} collective-permute-done((bf16[1,32,3328]{2,1,0:T(8,128)(2,1)S(1)}, bf16[1,32,3328]{2,1,0:T(8,128)(2,1)S(1)}, u32[]{:S(2)}, u32[]{:S(2)}) %collective-permute-start.28) | collective-permute-done | bytes 213024 | tf_op jit(solution)/shard_map/ppermute | solution.py:59
  93.5 2.4 %collective-permute-done.31 = bf16[32,3328]{1,0:T(8,128)(2,1)S(1)} collective-permute-done((bf16[32,3328]{1,0:T(8,128)(2,1)S(1)}, bf16[32,3328]{1,0:T(8,128)(2,1)S(1)}, u32[]{:S(2)}, u32[]{:S(2)}) %collective-permute-start.31) | collective-permute-done | bytes 213024 | tf_op jit(solution)/shard_map/ppermute | solution.py:59
  95.9 4.8 %collective-permute-done.30 = bf16[32,3328]{1,0:T(8,128)(2,1)S(1)} collective-permute-done((bf16[32,3328]{1,0:T(8,128)(2,1)S(1)}, bf16[32,3328]{1,0:T(8,128)(2,1)S(1)}, u32[]{:S(2)}, u32[]{:S(2)}) %collective-permute-start.30) | collective-permute-done | bytes 213024 | tf_op jit(solution)/shard_map/ppermute | solution.py:59
  101.1 3.4 %collective-permute-start.37 = (bf16[1,32,3328]{2,1,0:T(8,128)(2,1)S(1)}, bf16[1,32,3328]{2,1,0:T(8,128)(2,1)S(1)}, u32[]{:S(2)}, u32[]{:S(2)}) collective-permute-start(bf16[1,32,3328]{2,1,0:T(8,128)(2,1)S(1)} %get-tuple-element.20), channel_id=1, source_target_pairs={{0,2},{1,3},{2,0},{3,1},{4,6},{5,7},{6,4},{7,5},{8,10},{9,11},{10,... | collective-permute-start | bytes 638984 | tf_op jit(solution)/shard_map/ppermute | solution.py:59
  104.8 1.8 %collective-permute-start.35 = (bf16[1,32,3328]{2,1,0:T(8,128)(2,1)S(1)}, bf16[1,32,3328]{2,1,0:T(8,128)(2,1)S(1)}, u32[]{:S(2)}, u32[]{:S(2)}) collective-permute-start(bf16[1,32,3328]{2,1,0:T(8,128)(2,1)S(1)} %multiply_convert_fusion.1), channel_id=1, source_target_pairs={{0,1},{1,2},{2,3},{3,0},{4,5},{5,6},{6,7},{7,4},{8,9},{9,10},{10,1... | collective-permute-start | bytes 638984 | tf_op jit(solution)/shard_map/ppermute | solution.py:59
  108.1 1.9 %collective-permute-start.33 = (bf16[1,32,3328]{2,1,0:T(8,128)(2,1)S(1)}, bf16[1,32,3328]{2,1,0:T(8,128)(2,1)S(1)}, u32[]{:S(2)}, u32[]{:S(2)}) collective-permute-start(bf16[1,32,3328]{2,1,0:T(8,128)(2,1)S(1)} %multiply_convert_fusion.1), channel_id=1, source_target_pairs={{0,3},{1,0},{2,1},{3,2},{4,7},{5,4},{6,5},{7,6},{8,11},{9,8},{10,9... | collective-permute-start | bytes 638984 | tf_op jit(solution)/shard_map/ppermute | solution.py:59
  111.4 2.2 %product.3 = bf16[512,3328]{1,0:T(8,128)(2,1)} custom-call(bf16[128,512]{1,0:T(8,128)(2,1)S(1)} %fusion.local_ref, bf16[128,3328]{1,0:T(8,128)(2,1)S(1)} %maximum_bitcast_fusion.1.cot_ref), custom_call_target="tpu_custom_call" | custom-call | tf_op jit(solution)/shard_map/product/pallas_call | solution.py:135
  113.6 1.6 %collective-permute-done.34 = bf16[1,32,3328]{2,1,0:T(8,128)(2,1)S(1)} collective-permute-done((bf16[1,32,3328]{2,1,0:T(8,128)(2,1)S(1)}, bf16[1,32,3328]{2,1,0:T(8,128)(2,1)S(1)}, u32[]{:S(2)}, u32[]{:S(2)}) %collective-permute-start.34) | collective-permute-done | bytes 213024 | tf_op jit(solution)/shard_map/ppermute | solution.py:59
  116.0 2.1 %product.2 = bf16[512,3328]{1,0:T(8,128)(2,1)} custom-call(bf16[128,512]{1,0:T(8,128)(2,1)S(1)} %fusion.local_ref, bf16[128,3328]{1,0:T(8,128)(2,1)S(1)} %maximum_bitcast_fusion.cot_ref), custom_call_target="tpu_custom_call" | custom-call | tf_op jit(solution)/shard_map/product/pallas_call | solution.py:135
  (141 shorter events, 35.5 us)
Async XLA Ops:
  0.6 10.5 %collective-permute-start.1 = (bf16[16,512]{1,0:T(8,128)(2,1)}, bf16[16,512]{1,0:T(8,128)(2,1)S(1)}, u32[]{:S(2)}, u32[]{:S(2)}) collective-permute-start(bf16[16,512]{1,0:T(8,128)(2,1)} %param.6), channel_id=1, source_target_pairs={{0,64},{1,65},{2,66},{3,67},{4,68},{5,69},{6,70},{7,71},{8,72},{9,... | collective-permute-start | bytes 49160 | tf_op jit(solution)/shard_map/ppermute | solution.py:59
  4.7 6.5 %collective-permute-start = (bf16[16,512]{1,0:T(8,128)(2,1)}, bf16[16,512]{1,0:T(8,128)(2,1)S(1)}, u32[]{:S(2)}, u32[]{:S(2)}) collective-permute-start(bf16[16,512]{1,0:T(8,128)(2,1)} %param.6), channel_id=1, source_target_pairs={{0,32},{1,33},{2,34},{3,35},{4,36},{5,37},{6,38},{7,39},{8,40},{9,... | collective-permute-start | bytes 49160 | tf_op jit(solution)/shard_map/ppermute | solution.py:59
  13.5 8.7 %collective-permute-start.4 = (bf16[64,3328]{1,0:T(8,128)(2,1)S(1)}, bf16[64,3328]{1,0:T(8,128)(2,1)S(1)}, u32[]{:S(2)}, u32[]{:S(2)}) collective-permute-start(bf16[64,3328]{1,0:T(8,128)(2,1)S(1)} %slice.409), channel_id=1, source_target_pairs={{0,1},{1,0},{2,3},{3,2},{4,5},{5,4},{6,7},{7,6},{8,9},{9,8},{10,11... | collective-permute-start | bytes 1277960 | tf_op jit(solution)/shard_map/ppermute | solution.py:59
  16.0 9.4 %collective-permute-start.6 = (bf16[64,3328]{1,0:T(8,128)(2,1)S(1)}, bf16[64,3328]{1,0:T(8,128)(2,1)S(1)}, u32[]{:S(2)}, u32[]{:S(2)}) collective-permute-start(bf16[64,3328]{1,0:T(8,128)(2,1)S(1)} %slice.408), channel_id=1, source_target_pairs={{0,3},{1,2},{2,1},{3,0},{4,7},{5,6},{6,5},{7,4},{8,11},{9,10},{10,... | collective-permute-start | bytes 1277960 | tf_op jit(solution)/shard_map/ppermute | solution.py:59
  19.0 8.2 %collective-permute-start.8 = (bf16[64,3328]{1,0:T(8,128)(2,1)S(1)}, bf16[64,3328]{1,0:T(8,128)(2,1)S(1)}, u32[]{:S(2)}, u32[]{:S(2)}) collective-permute-start(bf16[64,3328]{1,0:T(8,128)(2,1)S(1)} %slice.407), channel_id=1, source_target_pairs={{0,1},{1,0},{2,3},{3,2},{4,5},{5,4},{6,7},{7,6},{8,9},{9,8},{10,11... | collective-permute-start | bytes 1277960 | tf_op jit(solution)/shard_map/ppermute | solution.py:59
  20.9 9.4 %collective-permute-start.10 = (bf16[64,3328]{1,0:T(8,128)(2,1)S(1)}, bf16[64,3328]{1,0:T(8,128)(2,1)S(1)}, u32[]{:S(2)}, u32[]{:S(2)}) collective-permute-start(bf16[64,3328]{1,0:T(8,128)(2,1)S(1)} %slice.406), channel_id=1, source_target_pairs={{0,3},{1,2},{2,1},{3,0},{4,7},{5,6},{6,5},{7,4},{8,11},{9,10},{10,... | collective-permute-start | bytes 1277960 | tf_op jit(solution)/shard_map/ppermute | solution.py:59
  22.3 10.3 %collective-permute-start.5 = (bf16[32,3328]{1,0:T(8,128)(2,1)S(1)}, bf16[32,3328]{1,0:T(8,128)(2,1)S(1)}, u32[]{:S(2)}, u32[]{:S(2)}) collective-permute-start(bf16[32,3328]{1,0:T(8,128)(2,1)S(1)} %slice.413), channel_id=1, source_target_pairs={{0,3},{1,2},{2,1},{3,0},{4,7},{5,6},{6,5},{7,4},{8,11},{9,10},{10,... | collective-permute-start | bytes 638984 | tf_op jit(solution)/shard_map/ppermute | solution.py:59
  25.5 7.1 %collective-permute-start.7 = (bf16[32,3328]{1,0:T(8,128)(2,1)S(1)}, bf16[32,3328]{1,0:T(8,128)(2,1)S(1)}, u32[]{:S(2)}, u32[]{:S(2)}) collective-permute-start(bf16[32,3328]{1,0:T(8,128)(2,1)S(1)} %slice.412), channel_id=1, source_target_pairs={{0,1},{1,0},{2,3},{3,2},{4,5},{5,4},{6,7},{7,6},{8,9},{9,8},{10,11... | collective-permute-start | bytes 638984 | tf_op jit(solution)/shard_map/ppermute | solution.py:59
  27.3 7.6 %collective-permute-start.9 = (bf16[32,3328]{1,0:T(8,128)(2,1)S(1)}, bf16[32,3328]{1,0:T(8,128)(2,1)S(1)}, u32[]{:S(2)}, u32[]{:S(2)}) collective-permute-start(bf16[32,3328]{1,0:T(8,128)(2,1)S(1)} %slice.411), channel_id=1, source_target_pairs={{0,3},{1,2},{2,1},{3,0},{4,7},{5,6},{6,5},{7,4},{8,11},{9,10},{10,... | collective-permute-start | bytes 638984 | tf_op jit(solution)/shard_map/ppermute | solution.py:59
  36.7 7.4 %collective-permute-start.12 = (bf16[4,8,3328]{2,1,0:T(8,128)(2,1)S(1)}, bf16[4,8,3328]{2,1,0:T(8,128)(2,1)S(1)}, u32[]{:S(2)}, u32[]{:S(2)}) collective-permute-start(bf16[4,8,3328]{2,1,0:T(8,128)(2,1)S(1)} %get-tuple-element.27), channel_id=1, source_target_pairs={{0,8},{1,9},{2,10},{3,11},{4,12},{5,13},{6,14},{7,15},{8,0},{9,1},... | collective-permute-start | bytes 638984 | tf_op jit(solution)/shard_map/ppermute | solution.py:59
  40.0 6.8 %collective-permute-start.14 = (bf16[4,8,3328]{2,1,0:T(8,128)(2,1)S(1)}, bf16[4,8,3328]{2,1,0:T(8,128)(2,1)S(1)}, u32[]{:S(2)}, u32[]{:S(2)}) collective-permute-start(bf16[4,8,3328]{2,1,0:T(8,128)(2,1)S(1)} %get-tuple-element.28), channel_id=1, source_target_pairs={{0,12},{1,13},{2,14},{3,15},{4,0},{5,1},{6,2},{7,3},{8,4},{9,5},{1... | collective-permute-start | bytes 638984 | tf_op jit(solution)/shard_map/ppermute | solution.py:59
  41.0 7.1 %collective-permute-start.13 = (bf16[4,8,3328]{2,1,0:T(8,128)(2,1)S(1)}, bf16[4,8,3328]{2,1,0:T(8,128)(2,1)S(1)}, u32[]{:S(2)}, u32[]{:S(2)}) collective-permute-start(bf16[4,8,3328]{2,1,0:T(8,128)(2,1)S(1)} %get-tuple-element.29), channel_id=1, source_target_pairs={{0,4},{1,5},{2,6},{3,7},{4,8},{5,9},{6,10},{7,11},{8,12},{9,13},{1... | collective-permute-start | bytes 638984 | tf_op jit(solution)/shard_map/ppermute | solution.py:59
  48.3 6.0 %collective-permute-start.17 = (bf16[1,8,3328]{2,1,0:T(8,128)(2,1)S(1)}, bf16[1,8,3328]{2,1,0:T(8,128)(2,1)S(1)}, u32[]{:S(2)}, u32[]{:S(2)}) collective-permute-start(bf16[1,8,3328]{2,1,0:T(8,128)(2,1)S(1)} %get-tuple-element.23), channel_id=1, source_target_pairs={{0,4},{1,5},{2,6},{3,7},{4,8},{5,9},{6,10},{7,11},{8,12},{9,13},{1... | collective-permute-start | bytes 159752 | tf_op jit(solution)/shard_map/ppermute | solution.py:59
  55.6 10.4 %collective-permute-start.20 = (bf16[1,32,3328]{2,1,0:T(8,128)(2,1)S(1)}, bf16[1,32,3328]{2,1,0:T(8,128)(2,1)S(1)}, u32[]{:S(2)}, u32[]{:S(2)}) collective-permute-start(bf16[1,32,3328]{2,1,0:T(8,128)(2,1)S(1)} %pad_maximum_fusion.2), channel_id=1, source_target_pairs={{0,1},{1,2},{2,3},{3,0},{4,5},{5,6},{6,7},{7,4},{8,9},{9,10},{10,1... | collective-permute-start | bytes 638984 | tf_op jit(solution)/shard_map/ppermute | solution.py:59
  56.0 9.9 %collective-permute-start.19 = (bf16[1,32,3328]{2,1,0:T(8,128)(2,1)S(1)}, bf16[1,32,3328]{2,1,0:T(8,128)(2,1)S(1)}, u32[]{:S(2)}, u32[]{:S(2)}) collective-permute-start(bf16[1,32,3328]{2,1,0:T(8,128)(2,1)S(1)} %pad_maximum_fusion.2), channel_id=1, source_target_pairs={{0,2},{1,3},{2,0},{3,1},{4,6},{5,7},{6,4},{7,5},{8,10},{9,11},{10,... | collective-permute-start | bytes 638984 | tf_op jit(solution)/shard_map/ppermute | solution.py:59
  59.7 6.2 %collective-permute-start.18 = (bf16[1,32,3328]{2,1,0:T(8,128)(2,1)S(1)}, bf16[1,32,3328]{2,1,0:T(8,128)(2,1)S(1)}, u32[]{:S(2)}, u32[]{:S(2)}) collective-permute-start(bf16[1,32,3328]{2,1,0:T(8,128)(2,1)S(1)} %pad_maximum_fusion.2), channel_id=1, source_target_pairs={{0,3},{1,0},{2,1},{3,2},{4,7},{5,4},{6,5},{7,6},{8,11},{9,8},{10,9... | collective-permute-start | bytes 638984 | tf_op jit(solution)/shard_map/ppermute | solution.py:59
  59.7 6.3 %collective-permute-start.21 = (bf16[2,8,3328]{2,1,0:T(8,128)(2,1)S(1)}, bf16[2,8,3328]{2,1,0:T(8,128)(2,1)S(1)}, u32[]{:S(2)}, u32[]{:S(2)}) collective-permute-start(bf16[2,8,3328]{2,1,0:T(8,128)(2,1)S(1)} %pad_maximum_fusion.4), channel_id=1, source_target_pairs={{0,4},{1,5},{2,6},{3,7},{4,0},{5,1},{6,2},{7,3},{8,12},{9,13},{10,... | collective-permute-start | bytes 319496 | tf_op jit(solution)/shard_map/ppermute | solution.py:59
  66.6 6.6 %collective-permute-start.24 = (bf16[128,512]{1,0:T(8,128)(2,1)S(1)}, bf16[128,512]{1,0:T(8,128)(2,1)S(1)}, u32[]{:S(2)}, u32[]{:S(2)}) collective-permute-start(bf16[128,512]{1,0:T(8,128)(2,1)S(1)} %get-tuple-element.40), channel_id=1, source_target_pairs={{0,64},{1,65},{2,66},{3,67},{4,68},{5,69},{6,70},{7,71},{8,72},{9,... | collective-permute-start | bytes 393224 | tf_op jit(solution)/shard_map/ppermute | solution.py:59
  66.8 6.9 %collective-permute-start.23 = (bf16[128,512]{1,0:T(8,128)(2,1)S(1)}, bf16[128,512]{1,0:T(8,128)(2,1)S(1)}, u32[]{:S(2)}, u32[]{:S(2)}) collective-permute-start(bf16[128,512]{1,0:T(8,128)(2,1)S(1)} %get-tuple-element.40), channel_id=1, source_target_pairs={{0,96},{1,97},{2,98},{3,99},{4,100},{5,101},{6,102},{7,103},{8,104... | collective-permute-start | bytes 393224 | tf_op jit(solution)/shard_map/ppermute | solution.py:59
  69.1 6.2 %collective-permute-start.22 = (bf16[128,512]{1,0:T(8,128)(2,1)S(1)}, bf16[128,512]{1,0:T(8,128)(2,1)S(1)}, u32[]{:S(2)}, u32[]{:S(2)}) collective-permute-start(bf16[128,512]{1,0:T(8,128)(2,1)S(1)} %get-tuple-element.40), channel_id=1, source_target_pairs={{0,32},{1,33},{2,34},{3,35},{4,36},{5,37},{6,38},{7,39},{8,40},{9,... | collective-permute-start | bytes 393224 | tf_op jit(solution)/shard_map/ppermute | solution.py:59
  75.5 7.5 %collective-permute-start.32 = (bf16[2,16,3328]{2,1,0:T(8,128)(2,1)S(1)}, bf16[2,16,3328]{2,1,0:T(8,128)(2,1)S(1)}, u32[]{:S(2)}, u32[]{:S(2)}) collective-permute-start(bf16[2,16,3328]{2,1,0:T(8,128)(2,1)S(1)} %pad_maximum_fusion.3), channel_id=1, source_target_pairs={{0,12},{1,13},{2,14},{3,15},{4,8},{5,9},{6,10},{7,11},{8,4},{9,5},... | collective-permute-start | bytes 638984 | tf_op jit(solution)/shard_map/ppermute | solution.py:59
  79.5 7.4 %collective-permute-start.26 = (bf16[1,32,3328]{2,1,0:T(8,128)(2,1)S(1)}, bf16[1,32,3328]{2,1,0:T(8,128)(2,1)S(1)}, u32[]{:S(2)}, u32[]{:S(2)}) collective-permute-start(bf16[1,32,3328]{2,1,0:T(8,128)(2,1)S(1)} %get-tuple-element.24), channel_id=1, source_target_pairs={{0,2},{1,3},{2,0},{3,1},{4,6},{5,7},{6,4},{7,5},{8,10},{9,11},{10,... | collective-permute-start | bytes 638984 | tf_op jit(solution)/shard_map/ppermute | solution.py:59
  80.8 8.4 %collective-permute-start.28 = (bf16[1,32,3328]{2,1,0:T(8,128)(2,1)S(1)}, bf16[1,32,3328]{2,1,0:T(8,128)(2,1)S(1)}, u32[]{:S(2)}, u32[]{:S(2)}) collective-permute-start(bf16[1,32,3328]{2,1,0:T(8,128)(2,1)S(1)} %get-tuple-element.25), channel_id=1, source_target_pairs={{0,3},{1,0},{2,1},{3,2},{4,7},{5,4},{6,5},{7,6},{8,11},{9,8},{10,9... | collective-permute-start | bytes 638984 | tf_op jit(solution)/shard_map/ppermute | solution.py:59
  82.8 7.1 %collective-permute-start.27 = (bf16[1,32,3328]{2,1,0:T(8,128)(2,1)S(1)}, bf16[1,32,3328]{2,1,0:T(8,128)(2,1)S(1)}, u32[]{:S(2)}, u32[]{:S(2)}) collective-permute-start(bf16[1,32,3328]{2,1,0:T(8,128)(2,1)S(1)} %get-tuple-element.26), channel_id=1, source_target_pairs={{0,1},{1,2},{2,3},{3,0},{4,5},{5,6},{6,7},{7,4},{8,9},{9,10},{10,1... | collective-permute-start | bytes 638984 | tf_op jit(solution)/shard_map/ppermute | solution.py:59
  91.3 9.4 %collective-permute-start.30 = (bf16[32,3328]{1,0:T(8,128)(2,1)S(1)}, bf16[32,3328]{1,0:T(8,128)(2,1)S(1)}, u32[]{:S(2)}, u32[]{:S(2)}) collective-permute-start(bf16[32,3328]{1,0:T(8,128)(2,1)S(1)} %convert_bitcast_fusion), channel_id=1, source_target_pairs={{0,4},{1,5},{2,6},{3,7},{4,8},{5,9},{6,10},{7,11},{8,12},{9,13},{1... | collective-permute-start | bytes 638984 | tf_op jit(solution)/shard_map/ppermute | solution.py:59
  92.2 8.6 %collective-permute-start.29 = (bf16[32,3328]{1,0:T(8,128)(2,1)S(1)}, bf16[32,3328]{1,0:T(8,128)(2,1)S(1)}, u32[]{:S(2)}, u32[]{:S(2)}) collective-permute-start(bf16[32,3328]{1,0:T(8,128)(2,1)S(1)} %convert_bitcast_fusion), channel_id=1, source_target_pairs={{0,8},{1,9},{2,10},{3,11},{4,12},{5,13},{6,14},{7,15},{8,0},{9,1},... | collective-permute-start | bytes 638984 | tf_op jit(solution)/shard_map/ppermute | solution.py:59
  101.0 7.1 %collective-permute-start.38 = (bf16[1,32,3328]{2,1,0:T(8,128)(2,1)S(1)}, bf16[1,32,3328]{2,1,0:T(8,128)(2,1)S(1)}, u32[]{:S(2)}, u32[]{:S(2)}) collective-permute-start(bf16[1,32,3328]{2,1,0:T(8,128)(2,1)S(1)} %get-tuple-element.20), channel_id=1, source_target_pairs={{0,1},{1,2},{2,3},{3,0},{4,5},{5,6},{6,7},{7,4},{8,9},{9,10},{10,1... | collective-permute-start | bytes 638984 | tf_op jit(solution)/shard_map/ppermute | solution.py:59
  101.1 9.6 %collective-permute-start.37 = (bf16[1,32,3328]{2,1,0:T(8,128)(2,1)S(1)}, bf16[1,32,3328]{2,1,0:T(8,128)(2,1)S(1)}, u32[]{:S(2)}, u32[]{:S(2)}) collective-permute-start(bf16[1,32,3328]{2,1,0:T(8,128)(2,1)S(1)} %get-tuple-element.20), channel_id=1, source_target_pairs={{0,2},{1,3},{2,0},{3,1},{4,6},{5,7},{6,4},{7,5},{8,10},{9,11},{10,... | collective-permute-start | bytes 638984 | tf_op jit(solution)/shard_map/ppermute | solution.py:59
  104.5 6.8 %collective-permute-start.36 = (bf16[1,32,3328]{2,1,0:T(8,128)(2,1)S(1)}, bf16[1,32,3328]{2,1,0:T(8,128)(2,1)S(1)}, u32[]{:S(2)}, u32[]{:S(2)}) collective-permute-start(bf16[1,32,3328]{2,1,0:T(8,128)(2,1)S(1)} %get-tuple-element.20), channel_id=1, source_target_pairs={{0,3},{1,0},{2,1},{3,2},{4,7},{5,4},{6,5},{7,6},{8,11},{9,8},{10,9... | collective-permute-start | bytes 638984 | tf_op jit(solution)/shard_map/ppermute | solution.py:59
  104.8 8.7 %collective-permute-start.35 = (bf16[1,32,3328]{2,1,0:T(8,128)(2,1)S(1)}, bf16[1,32,3328]{2,1,0:T(8,128)(2,1)S(1)}, u32[]{:S(2)}, u32[]{:S(2)}) collective-permute-start(bf16[1,32,3328]{2,1,0:T(8,128)(2,1)S(1)} %multiply_convert_fusion.1), channel_id=1, source_target_pairs={{0,1},{1,2},{2,3},{3,0},{4,5},{5,6},{6,7},{7,4},{8,9},{9,10},{10,1... | collective-permute-start | bytes 638984 | tf_op jit(solution)/shard_map/ppermute | solution.py:59
  106.6 8.5 %collective-permute-start.34 = (bf16[1,32,3328]{2,1,0:T(8,128)(2,1)S(1)}, bf16[1,32,3328]{2,1,0:T(8,128)(2,1)S(1)}, u32[]{:S(2)}, u32[]{:S(2)}) collective-permute-start(bf16[1,32,3328]{2,1,0:T(8,128)(2,1)S(1)} %multiply_convert_fusion.1), channel_id=1, source_target_pairs={{0,2},{1,3},{2,0},{3,1},{4,6},{5,7},{6,4},{7,5},{8,10},{9,11},{10,... | collective-permute-start | bytes 638984 | tf_op jit(solution)/shard_map/ppermute | solution.py:59
  108.1 7.8 %collective-permute-start.33 = (bf16[1,32,3328]{2,1,0:T(8,128)(2,1)S(1)}, bf16[1,32,3328]{2,1,0:T(8,128)(2,1)S(1)}, u32[]{:S(2)}, u32[]{:S(2)}) collective-permute-start(bf16[1,32,3328]{2,1,0:T(8,128)(2,1)S(1)} %multiply_convert_fusion.1), channel_id=1, source_target_pairs={{0,3},{1,0},{2,1},{3,2},{4,7},{5,4},{6,5},{7,6},{8,11},{9,8},{10,9... | collective-permute-start | bytes 638984 | tf_op jit(solution)/shard_map/ppermute | solution.py:59
  (13 other events, 63.2 us)

commit v8 on v7

--- a/solution.py
+++ b/solution.py
@@ -169,9 +169,8 @@
 
 def sum_second(part):
     rounded = part.astype(BF)
-    for e in (2, 1, 3):
-        part = part + jnp.roll(send(rounded, second_shift(e)), -8 * e, axis=0)
-    return part
+    got = [jnp.roll(send(rounded, second_shift(e)), -8 * e, axis=0) for e in (2, 1, 3)]
+    return part + got[0] + got[1] + got[2]
 
 
 def gather_second(own):

time: 119 us -> 119 us (level)
  no operation moved by 1% of the time
where the time goes in v8:
time: 119 us; the launch traced here: 118 us
  starting transfers between devices  53.3 us (45%)
  waiting for transfers between devices  47.6 us (40%)
  matrix products  5.49 us (5%)
  Pallas kernels  4.89 us (4%)
  local copies, waits for them, and re-layouts  3.31 us (3%)
  other arithmetic  2.22 us (2%)
  between operations  1.52 us (1%)
    ppermute x39, starting transfers between devices, send(): return lax.ppermute(value, RC, to)  53.3 us
    ppermute x39, waiting for transfers between devices, send(): return lax.ppermute(value, RC, to)  47.6 us
    dot_general x12, matrix products, matmul(): return jnp.dot(left, right, preferred_element_type=F32)  5.49 us
    pallas_call x2, Pallas kernels, product(): pl.pallas_call(kernel, out_shape=jax.ShapeDtypeStruct((features, width),...  4.31 us
    unnamed x32, local copies, waits for them, and re-layouts  2.87 us
  transfers between devices with their start and end apart: 39, of which 26 were waited for; matrix products, arithmetic and copies ran while one was open for 5% of the time, Pallas kernels for 2%

profile of v8, /device:TPU:0, one launch (start us, length us, event | category | flops | bytes accessed | tf_op | source)
XLA Modules:
  0.0 118.3 jit_solution(11503331939382807571)
XLA Ops:
  0.6 4.0 %collective-permute-start.1 = (bf16[16,512]{1,0:T(8,128)(2,1)}, bf16[16,512]{1,0:T(8,128)(2,1)S(1)}, u32[]{:S(2)}, u32[]{:S(2)}) collective-permute-start(bf16[16,512]{1,0:T(8,128)(2,1)} %param.6), channel_id=1, source_target_pairs={{0,64},{1,65},{2,66},{3,67},{4,68},{5,69},{6,70},{7,71},{8,72},{9,... | collective-permute-start | bytes 49160 | tf_op jit(solution)/shard_map/ppermute | solution.py:59
  5.7 2.2 %collective-permute-start.2 = (bf16[16,512]{1,0:T(8,128)(2,1)}, bf16[16,512]{1,0:T(8,128)(2,1)S(1)}, u32[]{:S(2)}, u32[]{:S(2)}) collective-permute-start(bf16[16,512]{1,0:T(8,128)(2,1)} %param.6), channel_id=1, source_target_pairs={{0,96},{1,97},{2,98},{3,99},{4,100},{5,101},{6,102},{7,103},{8,104... | collective-permute-start | bytes 49160 | tf_op jit(solution)/shard_map/ppermute | solution.py:59
  8.6 2.0 %copy-done.1 = bf16[512,3328]{1,0:T(8,128)(2,1)S(1)} copy-done((bf16[512,3328]{1,0:T(8,128)(2,1)S(1)}, bf16[512,3328]{1,0:T(8,128)(2,1)}, u32[]{:S(2)}) %copy-start.1) | copy-done | bytes 3407896
  13.5 1.6 %collective-permute-start.4 = (bf16[64,3328]{1,0:T(8,128)(2,1)S(1)}, bf16[64,3328]{1,0:T(8,128)(2,1)S(1)}, u32[]{:S(2)}, u32[]{:S(2)}) collective-permute-start(bf16[64,3328]{1,0:T(8,128)(2,1)S(1)} %slice.409), channel_id=1, source_target_pairs={{0,1},{1,0},{2,3},{3,2},{4,5},{5,4},{6,7},{7,6},{8,9},{9,8},{10,11... | collective-permute-start | bytes 1277960 | tf_op jit(solution)/shard_map/ppermute | solution.py:59
  16.0 2.3 %collective-permute-start.6 = (bf16[64,3328]{1,0:T(8,128)(2,1)S(1)}, bf16[64,3328]{1,0:T(8,128)(2,1)S(1)}, u32[]{:S(2)}, u32[]{:S(2)}) collective-permute-start(bf16[64,3328]{1,0:T(8,128)(2,1)S(1)} %slice.408), channel_id=1, source_target_pairs={{0,3},{1,2},{2,1},{3,0},{4,7},{5,6},{6,5},{7,4},{8,11},{9,10},{10,... | collective-permute-start | bytes 1277960 | tf_op jit(solution)/shard_map/ppermute | solution.py:59
  22.3 2.3 %collective-permute-start.5 = (bf16[32,3328]{1,0:T(8,128)(2,1)S(1)}, bf16[32,3328]{1,0:T(8,128)(2,1)S(1)}, u32[]{:S(2)}, u32[]{:S(2)}) collective-permute-start(bf16[32,3328]{1,0:T(8,128)(2,1)S(1)} %slice.413), channel_id=1, source_target_pairs={{0,3},{1,2},{2,1},{3,0},{4,7},{5,6},{6,5},{7,4},{8,11},{9,10},{10,... | collective-permute-start | bytes 638984 | tf_op jit(solution)/shard_map/ppermute | solution.py:59
  25.6 1.6 %collective-permute-done.8 = bf16[64,3328]{1,0:T(8,128)(2,1)S(1)} collective-permute-done((bf16[64,3328]{1,0:T(8,128)(2,1)S(1)}, bf16[64,3328]{1,0:T(8,128)(2,1)S(1)}, u32[]{:S(2)}, u32[]{:S(2)}) %collective-permute-start.8) | collective-permute-done | bytes 426016 | tf_op jit(solution)/shard_map/ppermute | solution.py:59
  27.3 1.9 %collective-permute-start.9 = (bf16[32,3328]{1,0:T(8,128)(2,1)S(1)}, bf16[32,3328]{1,0:T(8,128)(2,1)S(1)}, u32[]{:S(2)}, u32[]{:S(2)}) collective-permute-start(bf16[32,3328]{1,0:T(8,128)(2,1)S(1)} %slice.411), channel_id=1, source_target_pairs={{0,3},{1,2},{2,1},{3,0},{4,7},{5,6},{6,5},{7,4},{8,11},{9,10},{10,... | collective-permute-start | bytes 638984 | tf_op jit(solution)/shard_map/ppermute | solution.py:59
  30.6 2.1 %collective-permute-done.5 = bf16[32,3328]{1,0:T(8,128)(2,1)S(1)} collective-permute-done((bf16[32,3328]{1,0:T(8,128)(2,1)S(1)}, bf16[32,3328]{1,0:T(8,128)(2,1)S(1)}, u32[]{:S(2)}, u32[]{:S(2)}) %collective-permute-start.5) | collective-permute-done | bytes 213024 | tf_op jit(solution)/shard_map/ppermute | solution.py:59
  32.7 2.2 %collective-permute-done.9 = bf16[32,3328]{1,0:T(8,128)(2,1)S(1)} collective-permute-done((bf16[32,3328]{1,0:T(8,128)(2,1)S(1)}, bf16[32,3328]{1,0:T(8,128)(2,1)S(1)}, u32[]{:S(2)}, u32[]{:S(2)}) %collective-permute-start.9) | collective-permute-done | bytes 213024 | tf_op jit(solution)/shard_map/ppermute | solution.py:59
  36.7 3.3 %collective-permute-start.12 = (bf16[4,8,3328]{2,1,0:T(8,128)(2,1)S(1)}, bf16[4,8,3328]{2,1,0:T(8,128)(2,1)S(1)}, u32[]{:S(2)}, u32[]{:S(2)}) collective-permute-start(bf16[4,8,3328]{2,1,0:T(8,128)(2,1)S(1)} %get-tuple-element.27), channel_id=1, source_target_pairs={{0,8},{1,9},{2,10},{3,11},{4,12},{5,13},{6,14},{7,15},{8,0},{9,1},... | collective-permute-start | bytes 638984 | tf_op jit(solution)/shard_map/ppermute | solution.py:59
  42.1 2.0 %collective-permute-done.12 = bf16[4,8,3328]{2,1,0:T(8,128)(2,1)S(1)} collective-permute-done((bf16[4,8,3328]{2,1,0:T(8,128)(2,1)S(1)}, bf16[4,8,3328]{2,1,0:T(8,128)(2,1)S(1)}, u32[]{:S(2)}, u32[]{:S(2)}) %collective-permute-start.12) | collective-permute-done | bytes 213024 | tf_op jit(solution)/shard_map/ppermute | solution.py:59
  44.1 2.6 %collective-permute-done.14 = bf16[4,8,3328]{2,1,0:T(8,128)(2,1)S(1)} collective-permute-done((bf16[4,8,3328]{2,1,0:T(8,128)(2,1)S(1)}, bf16[4,8,3328]{2,1,0:T(8,128)(2,1)S(1)}, u32[]{:S(2)}, u32[]{:S(2)}) %collective-permute-start.14) | collective-permute-done | bytes 213024 | tf_op jit(solution)/shard_map/ppermute | solution.py:59
  48.4 2.8 %collective-permute-start.16 = (bf16[1,8,3328]{2,1,0:T(8,128)(2,1)S(1)}, bf16[1,8,3328]{2,1,0:T(8,128)(2,1)S(1)}, u32[]{:S(2)}, u32[]{:S(2)}) collective-permute-start(bf16[1,8,3328]{2,1,0:T(8,128)(2,1)S(1)} %get-tuple-element.23), channel_id=1, source_target_pairs={{0,8},{1,9},{2,10},{3,11},{4,12},{5,13},{6,14},{7,15},{8,0},{9,1},... | collective-permute-start | bytes 159752 | tf_op jit(solution)/shard_map/ppermute | solution.py:59
  52.5 1.7 %collective-permute-done.17 = bf16[1,8,3328]{2,1,0:T(8,128)(2,1)S(1)} collective-permute-done((bf16[1,8,3328]{2,1,0:T(8,128)(2,1)S(1)}, bf16[1,8,3328]{2,1,0:T(8,128)(2,1)S(1)}, u32[]{:S(2)}, u32[]{:S(2)}) %collective-permute-start.17) | collective-permute-done | bytes 53280 | tf_op jit(solution)/shard_map/ppermute | solution.py:59
  56.0 3.7 %collective-permute-start.19 = (bf16[1,32,3328]{2,1,0:T(8,128)(2,1)S(1)}, bf16[1,32,3328]{2,1,0:T(8,128)(2,1)S(1)}, u32[]{:S(2)}, u32[]{:S(2)}) collective-permute-start(bf16[1,32,3328]{2,1,0:T(8,128)(2,1)S(1)} %pad_maximum_fusion.2), channel_id=1, source_target_pairs={{0,2},{1,3},{2,0},{3,1},{4,6},{5,7},{6,4},{7,5},{8,10},{9,11},{10,... | collective-permute-start | bytes 638984 | tf_op jit(solution)/shard_map/ppermute | solution.py:59
  61.2 4.6 %collective-permute-done.18 = bf16[1,32,3328]{2,1,0:T(8,128)(2,1)S(1)} collective-permute-done((bf16[1,32,3328]{2,1,0:T(8,128)(2,1)S(1)}, bf16[1,32,3328]{2,1,0:T(8,128)(2,1)S(1)}, u32[]{:S(2)}, u32[]{:S(2)}) %collective-permute-start.18) | collective-permute-done | bytes 213024 | tf_op jit(solution)/shard_map/ppermute | solution.py:59
  66.8 2.4 %collective-permute-start.23 = (bf16[128,512]{1,0:T(8,128)(2,1)S(1)}, bf16[128,512]{1,0:T(8,128)(2,1)S(1)}, u32[]{:S(2)}, u32[]{:S(2)}) collective-permute-start(bf16[128,512]{1,0:T(8,128)(2,1)S(1)} %get-tuple-element.40), channel_id=1, source_target_pairs={{0,96},{1,97},{2,98},{3,99},{4,100},{5,101},{6,102},{7,103},{8,104... | collective-permute-start | bytes 393224 | tf_op jit(solution)/shard_map/ppermute | solution.py:59
  69.6 3.5 %collective-permute-done.24 = bf16[128,512]{1,0:T(8,128)(2,1)S(1)} collective-permute-done((bf16[128,512]{1,0:T(8,128)(2,1)S(1)}, bf16[128,512]{1,0:T(8,128)(2,1)S(1)}, u32[]{:S(2)}, u32[]{:S(2)}) %collective-permute-start.24) | collective-permute-done | bytes 131104 | tf_op jit(solution)/shard_map/ppermute | solution.py:59
  73.7 1.6 %collective-permute-done.22 = bf16[128,512]{1,0:T(8,128)(2,1)S(1)} collective-permute-done((bf16[128,512]{1,0:T(8,128)(2,1)S(1)}, bf16[128,512]{1,0:T(8,128)(2,1)S(1)}, u32[]{:S(2)}, u32[]{:S(2)}) %collective-permute-start.22) | collective-permute-done | bytes 131104 | tf_op jit(solution)/shard_map/ppermute | solution.py:59
  75.5 2.5 %collective-permute-start.32 = (bf16[2,16,3328]{2,1,0:T(8,128)(2,1)S(1)}, bf16[2,16,3328]{2,1,0:T(8,128)(2,1)S(1)}, u32[]{:S(2)}, u32[]{:S(2)}) collective-permute-start(bf16[2,16,3328]{2,1,0:T(8,128)(2,1)S(1)} %pad_maximum_fusion.3), channel_id=1, source_target_pairs={{0,12},{1,13},{2,14},{3,15},{4,8},{5,9},{6,10},{7,11},{8,4},{9,5},... | collective-permute-start | bytes 638984 | tf_op jit(solution)/shard_map/ppermute | solution.py:59
  80.8 2.1 %collective-permute-start.28 = (bf16[1,32,3328]{2,1,0:T(8,128)(2,1)S(1)}, bf16[1,32,3328]{2,1,0:T(8,128)(2,1)S(1)}, u32[]{:S(2)}, u32[]{:S(2)}) collective-permute-start(bf16[1,32,3328]{2,1,0:T(8,128)(2,1)S(1)} %get-tuple-element.25), channel_id=1, source_target_pairs={{0,3},{1,0},{2,1},{3,2},{4,7},{5,4},{6,5},{7,6},{8,11},{9,8},{10,9... | collective-permute-start | bytes 638984 | tf_op jit(solution)/shard_map/ppermute | solution.py:59
  83.1 3.8 %collective-permute-done.26 = bf16[1,32,3328]{2,1,0:T(8,128)(2,1)S(1)} collective-permute-done((bf16[1,32,3328]{2,1,0:T(8,128)(2,1)S(1)}, bf16[1,32,3328]{2,1,0:T(8,128)(2,1)S(1)}, u32[]{:S(2)}, u32[]{:S(2)}) %collective-permute-start.26) | collective-permute-done | bytes 213024 | tf_op jit(solution)/shard_map/ppermute | solution.py:59
  86.9 2.3 %collective-permute-done.28 = bf16[1,32,3328]{2,1,0:T(8,128)(2,1)S(1)} collective-permute-done((bf16[1,32,3328]{2,1,0:T(8,128)(2,1)S(1)}, bf16[1,32,3328]{2,1,0:T(8,128)(2,1)S(1)}, u32[]{:S(2)}, u32[]{:S(2)}) %collective-permute-start.28) | collective-permute-done | bytes 213024 | tf_op jit(solution)/shard_map/ppermute | solution.py:59
  93.5 2.4 %collective-permute-done.31 = bf16[32,3328]{1,0:T(8,128)(2,1)S(1)} collective-permute-done((bf16[32,3328]{1,0:T(8,128)(2,1)S(1)}, bf16[32,3328]{1,0:T(8,128)(2,1)S(1)}, u32[]{:S(2)}, u32[]{:S(2)}) %collective-permute-start.31) | collective-permute-done | bytes 213024 | tf_op jit(solution)/shard_map/ppermute | solution.py:59
  95.9 4.8 %collective-permute-done.30 = bf16[32,3328]{1,0:T(8,128)(2,1)S(1)} collective-permute-done((bf16[32,3328]{1,0:T(8,128)(2,1)S(1)}, bf16[32,3328]{1,0:T(8,128)(2,1)S(1)}, u32[]{:S(2)}, u32[]{:S(2)}) %collective-permute-start.30) | collective-permute-done | bytes 213024 | tf_op jit(solution)/shard_map/ppermute | solution.py:59
  101.1 3.4 %collective-permute-start.37 = (bf16[1,32,3328]{2,1,0:T(8,128)(2,1)S(1)}, bf16[1,32,3328]{2,1,0:T(8,128)(2,1)S(1)}, u32[]{:S(2)}, u32[]{:S(2)}) collective-permute-start(bf16[1,32,3328]{2,1,0:T(8,128)(2,1)S(1)} %get-tuple-element.20), channel_id=1, source_target_pairs={{0,2},{1,3},{2,0},{3,1},{4,6},{5,7},{6,4},{7,5},{8,10},{9,11},{10,... | collective-permute-start | bytes 638984 | tf_op jit(solution)/shard_map/ppermute | solution.py:59
  104.8 1.8 %collective-permute-start.35 = (bf16[1,32,3328]{2,1,0:T(8,128)(2,1)S(1)}, bf16[1,32,3328]{2,1,0:T(8,128)(2,1)S(1)}, u32[]{:S(2)}, u32[]{:S(2)}) collective-permute-start(bf16[1,32,3328]{2,1,0:T(8,128)(2,1)S(1)} %multiply_convert_fusion.1), channel_id=1, source_target_pairs={{0,1},{1,2},{2,3},{3,0},{4,5},{5,6},{6,7},{7,4},{8,9},{9,10},{10,1... | collective-permute-start | bytes 638984 | tf_op jit(solution)/shard_map/ppermute | solution.py:59
  108.1 1.9 %collective-permute-start.33 = (bf16[1,32,3328]{2,1,0:T(8,128)(2,1)S(1)}, bf16[1,32,3328]{2,1,0:T(8,128)(2,1)S(1)}, u32[]{:S(2)}, u32[]{:S(2)}) collective-permute-start(bf16[1,32,3328]{2,1,0:T(8,128)(2,1)S(1)} %multiply_convert_fusion.1), channel_id=1, source_target_pairs={{0,3},{1,0},{2,1},{3,2},{4,7},{5,4},{6,5},{7,6},{8,11},{9,8},{10,9... | collective-permute-start | bytes 638984 | tf_op jit(solution)/shard_map/ppermute | solution.py:59
  111.4 2.2 %product.3 = bf16[512,3328]{1,0:T(8,128)(2,1)} custom-call(bf16[128,512]{1,0:T(8,128)(2,1)S(1)} %fusion.local_ref, bf16[128,3328]{1,0:T(8,128)(2,1)S(1)} %maximum_bitcast_fusion.1.cot_ref), custom_call_target="tpu_custom_call" | custom-call | tf_op jit(solution)/shard_map/product/pallas_call | solution.py:135
  113.6 1.6 %collective-permute-done.34 = bf16[1,32,3328]{2,1,0:T(8,128)(2,1)S(1)} collective-permute-done((bf16[1,32,3328]{2,1,0:T(8,128)(2,1)S(1)}, bf16[1,32,3328]{2,1,0:T(8,128)(2,1)S(1)}, u32[]{:S(2)}, u32[]{:S(2)}) %collective-permute-start.34) | collective-permute-done | bytes 213024 | tf_op jit(solution)/shard_map/ppermute | solution.py:59
  116.0 2.1 %product.2 = bf16[512,3328]{1,0:T(8,128)(2,1)} custom-call(bf16[128,512]{1,0:T(8,128)(2,1)S(1)} %fusion.local_ref, bf16[128,3328]{1,0:T(8,128)(2,1)S(1)} %maximum_bitcast_fusion.cot_ref), custom_call_target="tpu_custom_call" | custom-call | tf_op jit(solution)/shard_map/product/pallas_call | solution.py:135
  (141 shorter events, 35.5 us)
Async XLA Ops:
  0.6 10.5 %collective-permute-start.1 = (bf16[16,512]{1,0:T(8,128)(2,1)}, bf16[16,512]{1,0:T(8,128)(2,1)S(1)}, u32[]{:S(2)}, u32[]{:S(2)}) collective-permute-start(bf16[16,512]{1,0:T(8,128)(2,1)} %param.6), channel_id=1, source_target_pairs={{0,64},{1,65},{2,66},{3,67},{4,68},{5,69},{6,70},{7,71},{8,72},{9,... | collective-permute-start | bytes 49160 | tf_op jit(solution)/shard_map/ppermute | solution.py:59
  4.7 6.5 %collective-permute-start = (bf16[16,512]{1,0:T(8,128)(2,1)}, bf16[16,512]{1,0:T(8,128)(2,1)S(1)}, u32[]{:S(2)}, u32[]{:S(2)}) collective-permute-start(bf16[16,512]{1,0:T(8,128)(2,1)} %param.6), channel_id=1, source_target_pairs={{0,32},{1,33},{2,34},{3,35},{4,36},{5,37},{6,38},{7,39},{8,40},{9,... | collective-permute-start | bytes 49160 | tf_op jit(solution)/shard_map/ppermute | solution.py:59
  13.5 8.7 %collective-permute-start.4 = (bf16[64,3328]{1,0:T(8,128)(2,1)S(1)}, bf16[64,3328]{1,0:T(8,128)(2,1)S(1)}, u32[]{:S(2)}, u32[]{:S(2)}) collective-permute-start(bf16[64,3328]{1,0:T(8,128)(2,1)S(1)} %slice.409), channel_id=1, source_target_pairs={{0,1},{1,0},{2,3},{3,2},{4,5},{5,4},{6,7},{7,6},{8,9},{9,8},{10,11... | collective-permute-start | bytes 1277960 | tf_op jit(solution)/shard_map/ppermute | solution.py:59
  16.0 9.4 %collective-permute-start.6 = (bf16[64,3328]{1,0:T(8,128)(2,1)S(1)}, bf16[64,3328]{1,0:T(8,128)(2,1)S(1)}, u32[]{:S(2)}, u32[]{:S(2)}) collective-permute-start(bf16[64,3328]{1,0:T(8,128)(2,1)S(1)} %slice.408), channel_id=1, source_target_pairs={{0,3},{1,2},{2,1},{3,0},{4,7},{5,6},{6,5},{7,4},{8,11},{9,10},{10,... | collective-permute-start | bytes 1277960 | tf_op jit(solution)/shard_map/ppermute | solution.py:59
  19.0 8.2 %collective-permute-start.8 = (bf16[64,3328]{1,0:T(8,128)(2,1)S(1)}, bf16[64,3328]{1,0:T(8,128)(2,1)S(1)}, u32[]{:S(2)}, u32[]{:S(2)}) collective-permute-start(bf16[64,3328]{1,0:T(8,128)(2,1)S(1)} %slice.407), channel_id=1, source_target_pairs={{0,1},{1,0},{2,3},{3,2},{4,5},{5,4},{6,7},{7,6},{8,9},{9,8},{10,11... | collective-permute-start | bytes 1277960 | tf_op jit(solution)/shard_map/ppermute | solution.py:59
  20.9 9.4 %collective-permute-start.10 = (bf16[64,3328]{1,0:T(8,128)(2,1)S(1)}, bf16[64,3328]{1,0:T(8,128)(2,1)S(1)}, u32[]{:S(2)}, u32[]{:S(2)}) collective-permute-start(bf16[64,3328]{1,0:T(8,128)(2,1)S(1)} %slice.406), channel_id=1, source_target_pairs={{0,3},{1,2},{2,1},{3,0},{4,7},{5,6},{6,5},{7,4},{8,11},{9,10},{10,... | collective-permute-start | bytes 1277960 | tf_op jit(solution)/shard_map/ppermute | solution.py:59
  22.3 10.3 %collective-permute-start.5 = (bf16[32,3328]{1,0:T(8,128)(2,1)S(1)}, bf16[32,3328]{1,0:T(8,128)(2,1)S(1)}, u32[]{:S(2)}, u32[]{:S(2)}) collective-permute-start(bf16[32,3328]{1,0:T(8,128)(2,1)S(1)} %slice.413), channel_id=1, source_target_pairs={{0,3},{1,2},{2,1},{3,0},{4,7},{5,6},{6,5},{7,4},{8,11},{9,10},{10,... | collective-permute-start | bytes 638984 | tf_op jit(solution)/shard_map/ppermute | solution.py:59
  25.5 7.1 %collective-permute-start.7 = (bf16[32,3328]{1,0:T(8,128)(2,1)S(1)}, bf16[32,3328]{1,0:T(8,128)(2,1)S(1)}, u32[]{:S(2)}, u32[]{:S(2)}) collective-permute-start(bf16[32,3328]{1,0:T(8,128)(2,1)S(1)} %slice.412), channel_id=1, source_target_pairs={{0,1},{1,0},{2,3},{3,2},{4,5},{5,4},{6,7},{7,6},{8,9},{9,8},{10,11... | collective-permute-start | bytes 638984 | tf_op jit(solution)/shard_map/ppermute | solution.py:59
  27.3 7.6 %collective-permute-start.9 = (bf16[32,3328]{1,0:T(8,128)(2,1)S(1)}, bf16[32,3328]{1,0:T(8,128)(2,1)S(1)}, u32[]{:S(2)}, u32[]{:S(2)}) collective-permute-start(bf16[32,3328]{1,0:T(8,128)(2,1)S(1)} %slice.411), channel_id=1, source_target_pairs={{0,3},{1,2},{2,1},{3,0},{4,7},{5,6},{6,5},{7,4},{8,11},{9,10},{10,... | collective-permute-start | bytes 638984 | tf_op jit(solution)/shard_map/ppermute | solution.py:59
  36.7 7.4 %collective-permute-start.12 = (bf16[4,8,3328]{2,1,0:T(8,128)(2,1)S(1)}, bf16[4,8,3328]{2,1,0:T(8,128)(2,1)S(1)}, u32[]{:S(2)}, u32[]{:S(2)}) collective-permute-start(bf16[4,8,3328]{2,1,0:T(8,128)(2,1)S(1)} %get-tuple-element.27), channel_id=1, source_target_pairs={{0,8},{1,9},{2,10},{3,11},{4,12},{5,13},{6,14},{7,15},{8,0},{9,1},... | collective-permute-start | bytes 638984 | tf_op jit(solution)/shard_map/ppermute | solution.py:59
  40.0 6.8 %collective-permute-start.14 = (bf16[4,8,3328]{2,1,0:T(8,128)(2,1)S(1)}, bf16[4,8,3328]{2,1,0:T(8,128)(2,1)S(1)}, u32[]{:S(2)}, u32[]{:S(2)}) collective-permute-start(bf16[4,8,3328]{2,1,0:T(8,128)(2,1)S(1)} %get-tuple-element.28), channel_id=1, source_target_pairs={{0,12},{1,13},{2,14},{3,15},{4,0},{5,1},{6,2},{7,3},{8,4},{9,5},{1... | collective-permute-start | bytes 638984 | tf_op jit(solution)/shard_map/ppermute | solution.py:59
  41.0 7.1 %collective-permute-start.13 = (bf16[4,8,3328]{2,1,0:T(8,128)(2,1)S(1)}, bf16[4,8,3328]{2,1,0:T(8,128)(2,1)S(1)}, u32[]{:S(2)}, u32[]{:S(2)}) collective-permute-start(bf16[4,8,3328]{2,1,0:T(8,128)(2,1)S(1)} %get-tuple-element.29), channel_id=1, source_target_pairs={{0,4},{1,5},{2,6},{3,7},{4,8},{5,9},{6,10},{7,11},{8,12},{9,13},{1... | collective-permute-start | bytes 638984 | tf_op jit(solution)/shard_map/ppermute | solution.py:59
  48.3 6.0 %collective-permute-start.17 = (bf16[1,8,3328]{2,1,0:T(8,128)(2,1)S(1)}, bf16[1,8,3328]{2,1,0:T(8,128)(2,1)S(1)}, u32[]{:S(2)}, u32[]{:S(2)}) collective-permute-start(bf16[1,8,3328]{2,1,0:T(8,128)(2,1)S(1)} %get-tuple-element.23), channel_id=1, source_target_pairs={{0,4},{1,5},{2,6},{3,7},{4,8},{5,9},{6,10},{7,11},{8,12},{9,13},{1... | collective-permute-start | bytes 159752 | tf_op jit(solution)/shard_map/ppermute | solution.py:59
  55.6 10.4 %collective-permute-start.20 = (bf16[1,32,3328]{2,1,0:T(8,128)(2,1)S(1)}, bf16[1,32,3328]{2,1,0:T(8,128)(2,1)S(1)}, u32[]{:S(2)}, u32[]{:S(2)}) collective-permute-start(bf16[1,32,3328]{2,1,0:T(8,128)(2,1)S(1)} %pad_maximum_fusion.2), channel_id=1, source_target_pairs={{0,1},{1,2},{2,3},{3,0},{4,5},{5,6},{6,7},{7,4},{8,9},{9,10},{10,1... | collective-permute-start | bytes 638984 | tf_op jit(solution)/shard_map/ppermute | solution.py:59
  56.0 9.9 %collective-permute-start.19 = (bf16[1,32,3328]{2,1,0:T(8,128)(2,1)S(1)}, bf16[1,32,3328]{2,1,0:T(8,128)(2,1)S(1)}, u32[]{:S(2)}, u32[]{:S(2)}) collective-permute-start(bf16[1,32,3328]{2,1,0:T(8,128)(2,1)S(1)} %pad_maximum_fusion.2), channel_id=1, source_target_pairs={{0,2},{1,3},{2,0},{3,1},{4,6},{5,7},{6,4},{7,5},{8,10},{9,11},{10,... | collective-permute-start | bytes 638984 | tf_op jit(solution)/shard_map/ppermute | solution.py:59
  59.7 6.2 %collective-permute-start.18 = (bf16[1,32,3328]{2,1,0:T(8,128)(2,1)S(1)}, bf16[1,32,3328]{2,1,0:T(8,128)(2,1)S(1)}, u32[]{:S(2)}, u32[]{:S(2)}) collective-permute-start(bf16[1,32,3328]{2,1,0:T(8,128)(2,1)S(1)} %pad_maximum_fusion.2), channel_id=1, source_target_pairs={{0,3},{1,0},{2,1},{3,2},{4,7},{5,4},{6,5},{7,6},{8,11},{9,8},{10,9... | collective-permute-start | bytes 638984 | tf_op jit(solution)/shard_map/ppermute | solution.py:59
  59.7 6.3 %collective-permute-start.21 = (bf16[2,8,3328]{2,1,0:T(8,128)(2,1)S(1)}, bf16[2,8,3328]{2,1,0:T(8,128)(2,1)S(1)}, u32[]{:S(2)}, u32[]{:S(2)}) collective-permute-start(bf16[2,8,3328]{2,1,0:T(8,128)(2,1)S(1)} %pad_maximum_fusion.4), channel_id=1, source_target_pairs={{0,4},{1,5},{2,6},{3,7},{4,0},{5,1},{6,2},{7,3},{8,12},{9,13},{10,... | collective-permute-start | bytes 319496 | tf_op jit(solution)/shard_map/ppermute | solution.py:59
  66.6 6.6 %collective-permute-start.24 = (bf16[128,512]{1,0:T(8,128)(2,1)S(1)}, bf16[128,512]{1,0:T(8,128)(2,1)S(1)}, u32[]{:S(2)}, u32[]{:S(2)}) collective-permute-start(bf16[128,512]{1,0:T(8,128)(2,1)S(1)} %get-tuple-element.40), channel_id=1, source_target_pairs={{0,64},{1,65},{2,66},{3,67},{4,68},{5,69},{6,70},{7,71},{8,72},{9,... | collective-permute-start | bytes 393224 | tf_op jit(solution)/shard_map/ppermute | solution.py:59
  66.8 6.9 %collective-permute-start.23 = (bf16[128,512]{1,0:T(8,128)(2,1)S(1)}, bf16[128,512]{1,0:T(8,128)(2,1)S(1)}, u32[]{:S(2)}, u32[]{:S(2)}) collective-permute-start(bf16[128,512]{1,0:T(8,128)(2,1)S(1)} %get-tuple-element.40), channel_id=1, source_target_pairs={{0,96},{1,97},{2,98},{3,99},{4,100},{5,101},{6,102},{7,103},{8,104... | collective-permute-start | bytes 393224 | tf_op jit(solution)/shard_map/ppermute | solution.py:59
  69.1 6.2 %collective-permute-start.22 = (bf16[128,512]{1,0:T(8,128)(2,1)S(1)}, bf16[128,512]{1,0:T(8,128)(2,1)S(1)}, u32[]{:S(2)}, u32[]{:S(2)}) collective-permute-start(bf16[128,512]{1,0:T(8,128)(2,1)S(1)} %get-tuple-element.40), channel_id=1, source_target_pairs={{0,32},{1,33},{2,34},{3,35},{4,36},{5,37},{6,38},{7,39},{8,40},{9,... | collective-permute-start | bytes 393224 | tf_op jit(solution)/shard_map/ppermute | solution.py:59
  75.5 7.5 %collective-permute-start.32 = (bf16[2,16,3328]{2,1,0:T(8,128)(2,1)S(1)}, bf16[2,16,3328]{2,1,0:T(8,128)(2,1)S(1)}, u32[]{:S(2)}, u32[]{:S(2)}) collective-permute-start(bf16[2,16,3328]{2,1,0:T(8,128)(2,1)S(1)} %pad_maximum_fusion.3), channel_id=1, source_target_pairs={{0,12},{1,13},{2,14},{3,15},{4,8},{5,9},{6,10},{7,11},{8,4},{9,5},... | collective-permute-start | bytes 638984 | tf_op jit(solution)/shard_map/ppermute | solution.py:59
  79.5 7.4 %collective-permute-start.26 = (bf16[1,32,3328]{2,1,0:T(8,128)(2,1)S(1)}, bf16[1,32,3328]{2,1,0:T(8,128)(2,1)S(1)}, u32[]{:S(2)}, u32[]{:S(2)}) collective-permute-start(bf16[1,32,3328]{2,1,0:T(8,128)(2,1)S(1)} %get-tuple-element.24), channel_id=1, source_target_pairs={{0,2},{1,3},{2,0},{3,1},{4,6},{5,7},{6,4},{7,5},{8,10},{9,11},{10,... | collective-permute-start | bytes 638984 | tf_op jit(solution)/shard_map/ppermute | solution.py:59
  80.8 8.4 %collective-permute-start.28 = (bf16[1,32,3328]{2,1,0:T(8,128)(2,1)S(1)}, bf16[1,32,3328]{2,1,0:T(8,128)(2,1)S(1)}, u32[]{:S(2)}, u32[]{:S(2)}) collective-permute-start(bf16[1,32,3328]{2,1,0:T(8,128)(2,1)S(1)} %get-tuple-element.25), channel_id=1, source_target_pairs={{0,3},{1,0},{2,1},{3,2},{4,7},{5,4},{6,5},{7,6},{8,11},{9,8},{10,9... | collective-permute-start | bytes 638984 | tf_op jit(solution)/shard_map/ppermute | solution.py:59
  82.8 7.1 %collective-permute-start.27 = (bf16[1,32,3328]{2,1,0:T(8,128)(2,1)S(1)}, bf16[1,32,3328]{2,1,0:T(8,128)(2,1)S(1)}, u32[]{:S(2)}, u32[]{:S(2)}) collective-permute-start(bf16[1,32,3328]{2,1,0:T(8,128)(2,1)S(1)} %get-tuple-element.26), channel_id=1, source_target_pairs={{0,1},{1,2},{2,3},{3,0},{4,5},{5,6},{6,7},{7,4},{8,9},{9,10},{10,1... | collective-permute-start | bytes 638984 | tf_op jit(solution)/shard_map/ppermute | solution.py:59
  91.3 9.4 %collective-permute-start.30 = (bf16[32,3328]{1,0:T(8,128)(2,1)S(1)}, bf16[32,3328]{1,0:T(8,128)(2,1)S(1)}, u32[]{:S(2)}, u32[]{:S(2)}) collective-permute-start(bf16[32,3328]{1,0:T(8,128)(2,1)S(1)} %convert_bitcast_fusion), channel_id=1, source_target_pairs={{0,4},{1,5},{2,6},{3,7},{4,8},{5,9},{6,10},{7,11},{8,12},{9,13},{1... | collective-permute-start | bytes 638984 | tf_op jit(solution)/shard_map/ppermute | solution.py:59
  92.2 8.6 %collective-permute-start.29 = (bf16[32,3328]{1,0:T(8,128)(2,1)S(1)}, bf16[32,3328]{1,0:T(8,128)(2,1)S(1)}, u32[]{:S(2)}, u32[]{:S(2)}) collective-permute-start(bf16[32,3328]{1,0:T(8,128)(2,1)S(1)} %convert_bitcast_fusion), channel_id=1, source_target_pairs={{0,8},{1,9},{2,10},{3,11},{4,12},{5,13},{6,14},{7,15},{8,0},{9,1},... | collective-permute-start | bytes 638984 | tf_op jit(solution)/shard_map/ppermute | solution.py:59
  101.0 7.1 %collective-permute-start.38 = (bf16[1,32,3328]{2,1,0:T(8,128)(2,1)S(1)}, bf16[1,32,3328]{2,1,0:T(8,128)(2,1)S(1)}, u32[]{:S(2)}, u32[]{:S(2)}) collective-permute-start(bf16[1,32,3328]{2,1,0:T(8,128)(2,1)S(1)} %get-tuple-element.20), channel_id=1, source_target_pairs={{0,1},{1,2},{2,3},{3,0},{4,5},{5,6},{6,7},{7,4},{8,9},{9,10},{10,1... | collective-permute-start | bytes 638984 | tf_op jit(solution)/shard_map/ppermute | solution.py:59
  101.1 9.6 %collective-permute-start.37 = (bf16[1,32,3328]{2,1,0:T(8,128)(2,1)S(1)}, bf16[1,32,3328]{2,1,0:T(8,128)(2,1)S(1)}, u32[]{:S(2)}, u32[]{:S(2)}) collective-permute-start(bf16[1,32,3328]{2,1,0:T(8,128)(2,1)S(1)} %get-tuple-element.20), channel_id=1, source_target_pairs={{0,2},{1,3},{2,0},{3,1},{4,6},{5,7},{6,4},{7,5},{8,10},{9,11},{10,... | collective-permute-start | bytes 638984 | tf_op jit(solution)/shard_map/ppermute | solution.py:59
  104.5 6.8 %collective-permute-start.36 = (bf16[1,32,3328]{2,1,0:T(8,128)(2,1)S(1)}, bf16[1,32,3328]{2,1,0:T(8,128)(2,1)S(1)}, u32[]{:S(2)}, u32[]{:S(2)}) collective-permute-start(bf16[1,32,3328]{2,1,0:T(8,128)(2,1)S(1)} %get-tuple-element.20), channel_id=1, source_target_pairs={{0,3},{1,0},{2,1},{3,2},{4,7},{5,4},{6,5},{7,6},{8,11},{9,8},{10,9... | collective-permute-start | bytes 638984 | tf_op jit(solution)/shard_map/ppermute | solution.py:59
  104.8 8.7 %collective-permute-start.35 = (bf16[1,32,3328]{2,1,0:T(8,128)(2,1)S(1)}, bf16[1,32,3328]{2,1,0:T(8,128)(2,1)S(1)}, u32[]{:S(2)}, u32[]{:S(2)}) collective-permute-start(bf16[1,32,3328]{2,1,0:T(8,128)(2,1)S(1)} %multiply_convert_fusion.1), channel_id=1, source_target_pairs={{0,1},{1,2},{2,3},{3,0},{4,5},{5,6},{6,7},{7,4},{8,9},{9,10},{10,1... | collective-permute-start | bytes 638984 | tf_op jit(solution)/shard_map/ppermute | solution.py:59
  106.6 8.5 %collective-permute-start.34 = (bf16[1,32,3328]{2,1,0:T(8,128)(2,1)S(1)}, bf16[1,32,3328]{2,1,0:T(8,128)(2,1)S(1)}, u32[]{:S(2)}, u32[]{:S(2)}) collective-permute-start(bf16[1,32,3328]{2,1,0:T(8,128)(2,1)S(1)} %multiply_convert_fusion.1), channel_id=1, source_target_pairs={{0,2},{1,3},{2,0},{3,1},{4,6},{5,7},{6,4},{7,5},{8,10},{9,11},{10,... | collective-permute-start | bytes 638984 | tf_op jit(solution)/shard_map/ppermute | solution.py:59
  108.1 7.8 %collective-permute-start.33 = (bf16[1,32,3328]{2,1,0:T(8,128)(2,1)S(1)}, bf16[1,32,3328]{2,1,0:T(8,128)(2,1)S(1)}, u32[]{:S(2)}, u32[]{:S(2)}) collective-permute-start(bf16[1,32,3328]{2,1,0:T(8,128)(2,1)S(1)} %multiply_convert_fusion.1), channel_id=1, source_target_pairs={{0,3},{1,0},{2,1},{3,2},{4,7},{5,4},{6,5},{7,6},{8,11},{9,8},{10,9... | collective-permute-start | bytes 638984 | tf_op jit(solution)/shard_map/ppermute | solution.py:59
  (13 other events, 63.2 us)
